TPU v7x, 512 devices: a whole 4x4x16 slice. The times are simulated.
512 devices in a mesh: row: 32 (over x, z_lo), col: 16 (over y, z_hi, core).
Axes of the slice: x: 4, y: 4, z: 16 (z_hi: 2, z_lo: 8; z = z_hi * 8 + z_lo), core: 2. Of those that a mesh axis runs over, the one named last changes fastest.
Arguments:
- z_iter: float32 [8192, 8192], P('col', 'row'), may hold values from -6 to 6
- y_iter: float32 [8192, 8192], P('col', 'row'), may hold values from -6 to 6
Outputs:
- z_next: float32 [8192, 8192], P('col', 'row')
All inputs are finite; a program needn't handle non-finite values.
Results may differ from a plain program's by a relative error of at most 0.0041.
Values may be sent and summed in bfloat16 or wider, within the bound.
No kernel may reach another device: no remote copies, remote signals or barrier semaphores. Data moves between devices by JAX's collectives and lax.ppermute only.
A program may use at most 64 MiB of HBM per device.

v0:
```python
import jax
import jax.numpy as jnp
from jax import lax
from jax.sharding import PartitionSpec as P


def make_poly(product, order):
    rows_here = product.shape[0]
    cols_here = product.shape[1]
    row_ids = lax.axis_index("col") * rows_here + lax.broadcasted_iota(
        jnp.int32, (rows_here, cols_here), 0
    )
    col_ids = lax.axis_index("row") * cols_here + lax.broadcasted_iota(
        jnp.int32, (rows_here, cols_here), 1
    )
    ident = jnp.where(row_ids == col_ids, 1.0, 0.0).astype(jnp.float32)
    return (1.5 * ident - 0.5 / order * product).astype(jnp.bfloat16)


def shards(z_iter, y_iter):
    order = z_iter.shape[1] * lax.axis_size("row")
    z_half = z_iter.astype(jnp.bfloat16)
    y_half = y_iter.astype(jnp.bfloat16)
    z_rows = lax.all_gather(z_half, "row", axis=1, tiled=True)

    def add_right(piece):
        return jnp.dot(z_rows, piece, preferred_element_type=jnp.float32)

    product = add_right(lax.all_gather(y_half, "col", axis=0, tiled=True))
    poly = make_poly(product, order)
    z_next = add_right(lax.all_gather(poly, "col", axis=0, tiled=True))
    return z_next


def solution(mesh):
    return jax.shard_map(
        shards,
        mesh=mesh,
        in_specs=(P("col", "row"), P("col", "row")),
        out_specs=P("col", "row"),
        check_vma=False,
    )
```

profile of v0, /device:TPU:1, one launch (start us, length us, event | category | flops | bytes accessed | tf_op | source)
XLA Modules:
  0.0 537.1 jit_solution(16725814527837919365)
XLA Ops:
  6.5 0.0 all-gather.6.cloned.1.call-start
  6.5 1.8 convert_element_type.10
  8.3 0.0 all-gather.6.cloned.1.call-update
  8.3 0.0 all-gather.4.cloned.1.call-start
  8.4 1.8 convert_element_type.9
  10.2 0.0 all-gather.4.cloned.1.call-update
  10.2 0.0 all-gather.8.cloned.1.call-start
  10.3 125.4 %all-gather.6.cloned.1.call-done = bf16[8192,256]{1,0:T(8,128)(2,1)} async-done(((bf16[512,256]{1,0:T(8,128)(2,1)}), bf16[8192,256]{1,0:T(8,128)(2,1)}) %all-gather.6.cloned.1.call-update) | async-done | bytes 4194320 | tf_op jit(solution)/shard_map/all_gather | solution.py:29
  135.7 240.5 %all-gather.4.cloned.1.call-done = bf16[512,8192]{1,0:T(8,128)(2,1)} async-done(((bf16[512,256]{1,0:T(8,128)(2,1)}), bf16[512,8192]{1,0:T(8,128)(2,1)}) %all-gather.4.cloned.1.call-update) | async-done | bytes 8388624 | tf_op jit(solution)/shard_map/all_gather | solution.py:24
  376.2 7.6 %fusion.1 = bf16[512,256]{1,0:T(8,128)(2,1)} fusion(bf16[512,8192]{1,0:T(8,128)(2,1)} %all-gather.4.cloned.1.call-done, bf16[8192,256]{1,0:T(8,128)(2,1)} %all-gather.6.cloned.1.call-done, s32[256]{0:T(256)S(1)} %iota_add_fusion.1, s32[512]{0:T(512)S(1)} %iota_add_fusion), kind=kOutput, calls=%fused_computation.3 | convolution fusion | flops 2148270080 | bytes 12848128 | tf_op jit(solution)/shard_map/dot_general | solution.py:27
  383.8 0.0 all-gather.8.cloned.1.call-update
  383.8 138.7 %all-gather.8.cloned.1.call-done = bf16[8192,256]{1,0:T(8,128)(2,1)} async-done(((bf16[512,256]{1,0:T(8,128)(2,1)}), bf16[8192,256]{1,0:T(8,128)(2,1)}) %all-gather.8.cloned.1.call-update) | async-done | bytes 4194320 | tf_op jit(solution)/shard_map/all_gather | solution.py:31
  522.6 7.0 %convolution_bitcast_fusion = f32[512,256]{0,1:T(8,128)S(1)} fusion(bf16[8192,256]{1,0:T(8,128)(2,1)} %all-gather.8.cloned.1.call-done, bf16[512,8192]{1,0:T(8,128)(2,1)} %all-gather.4.cloned.1.call-done), kind=kOutput, calls=%fused_computation | convolution fusion | flops 2147483648 | bytes 13107200 | tf_op jit(solution)/shard_map/dot_general | solution.py:27
  529.6 1.0 copy.3
  (2 shorter events, 0.0 us)
Async XLA Ops:
  6.5 129.2 %all-gather.6.cloned.1.call-start = ((), (), s32[]{:S(2)}) async-start(), calls=%async_computation.1 | async-start | bytes 4456448 | tf_op jit(solution)/shard_map/all_gather | solution.py:29
  8.3 367.9 %all-gather.4.cloned.1.call-start = ((), (), s32[]{:S(2)}) async-start(), calls=%async_computation | async-start | bytes 8650752 | tf_op jit(solution)/shard_map/all_gather | solution.py:24
  10.2 512.4 %all-gather.8.cloned.1.call-start = ((), (), s32[]{:S(2)}) async-start(), calls=%async_computation.2 | async-start | bytes 4456448 | tf_op jit(solution)/shard_map/all_gather | solution.py:31
Sparse Core Ops, SparseCore 0:
  10.6 125.0 all-gather.5
  137.7 238.4 all-gather.3
  384.0 138.5 all-gather.7
where the time goes:
time: 537 us
  waiting for transfers between devices  505 us (94%)
  matrix products  14.6 us (3%)
  between operations  13.1 us (2%)
    all_gather x1, waiting for transfers between devices, shards(): z_rows = lax.all_gather(z_half, 'row', axis=1, tiled=True)  240 us
    all_gather x1, waiting for transfers between devices, shards(): z_next = add_right(lax.all_gather(poly, 'col', axis=0, tiled=True))  139 us
    all_gather x1, waiting for transfers between devices, shards(): product = add_right(lax.all_gather(y_half, 'col', axis=0, tiled=True))  125 us
    dot_general x2, matrix products, add_right(): return jnp.dot(z_rows, piece, preferred_element_type=jnp.float32)  14.6 us
  transfers between devices with their start and end apart: 3, of which 3 were waited for; matrix products, arithmetic and copies ran while one was open for 0% of the time, Pallas kernels for 0%

commit v1 on v0

v1 whole, which is shorter than its diff:
```python
import jax
import jax.numpy as jnp
from jax import lax
from jax.experimental import pallas as pl
from jax.experimental.pallas import tpu as pltpu
from jax.sharding import Mesh
from jax.sharding import PartitionSpec as P

AXES = ("x", "zl", "y", "zh", "c")
SIZES = (4, 8, 4, 2, 2)
PLANE = ("x", "y")
SWAP = [(0, 1), (1, 0)]


def dot_kernel(z_ref, *refs):
    parts, out_ref = refs[:-1], refs[-1]
    zh = lax.axis_index("zh")
    c = lax.axis_index("c")
    depth = z_ref.shape[2]
    total = None
    for n, part in enumerate(parts):
        first = (zh ^ (n // 2)) * 4 + (c ^ (n % 2)) * 2
        for h in range(2):
            term = jnp.dot(
                z_ref[first + h],
                part[0, h * depth : (h + 1) * depth, :],
                preferred_element_type=jnp.float32,
            )
            total = term if total is None else total + term
    out_ref[0] = total.astype(out_ref.dtype)


def dot_parts(z_rows, parts):
    blocks, rows, cols = z_rows.shape[0], z_rows.shape[1], parts[0].shape[2]
    groups = parts[0].shape[0]
    return pl.pallas_call(
        dot_kernel,
        grid=(groups,),
        in_specs=[pl.BlockSpec(z_rows.shape, lambda j: (0, 0, 0))]
        + [pl.BlockSpec((1,) + p.shape[1:], lambda j: (j, 0, 0)) for p in parts],
        out_specs=pl.BlockSpec((1, rows, cols), lambda j: (j, 0, 0)),
        out_shape=jax.ShapeDtypeStruct((groups, rows, cols), jnp.bfloat16),
        compiler_params=pltpu.CompilerParams(vmem_limit_bytes=32 * 2**20),
        cost_estimate=pl.CostEstimate(
            flops=2 * groups * rows * cols * blocks * z_rows.shape[2],
            bytes_accessed=2 * (z_rows.size + 4 * parts[0].size + groups * rows * cols),
            transcendentals=0,
        ),
    )(z_rows, *parts)


def other_core(block):
    return lax.ppermute(block, "c", SWAP)


def make_shift(product, order):
    groups, rows, cols = product.shape
    at = lambda name: lax.axis_index(name)
    group = lax.broadcasted_iota(jnp.int32, product.shape, 0)
    row_ids = (
        group * 2048
        + at("zh") * 1024
        + at("c") * 512
        + at("y") * rows
        + lax.broadcasted_iota(jnp.int32, product.shape, 1)
    )
    col_ids = at("x") * 2048 + at("zl") * cols + lax.broadcasted_iota(jnp.int32, product.shape, 2)
    ident = jnp.where(row_ids == col_ids, 1.5, 0.0).astype(jnp.float32)
    poly = (ident - 0.5 / order * product).astype(jnp.bfloat16)
    return (poly.astype(jnp.float32) - ident).astype(jnp.bfloat16)


def shards(z_iter, y_iter):
    order = z_iter.shape[1] * lax.axis_size("x") * lax.axis_size("zl")
    z_half = z_iter.astype(jnp.bfloat16)
    y_half = y_iter.astype(jnp.bfloat16)
    z_rows = lax.all_gather(z_half, "zl")

    def y_parts(block):
        every = lax.all_to_all(jnp.stack([block] * 4), "y", 0, 0, tiled=True)
        return [every, other_core(every)]

    turn = [(i * 4 + j, j * 4 + i) for i in range(4) for j in range(4)]
    turned = lax.ppermute(y_half, PLANE, turn)
    swapped = lax.ppermute(turned, "zh", SWAP)
    y_all = y_parts(turned) + y_parts(swapped)

    part = dot_parts(z_rows, y_all)
    part = lax.all_to_all(part.reshape(16, 128, 256), PLANE, 0, 0, tiled=True)
    product = part.reshape(4, 4, 128, 256).astype(jnp.float32).sum(0)
    shift = make_shift(product, order)

    def shift_parts(block):
        spread = jnp.broadcast_to(block[:, None], (4, 4, 128, 256)).reshape(16, 128, 256)
        every = lax.all_to_all(spread, PLANE, 0, 0, tiled=True).reshape(4, 512, 256)
        return [every, other_core(every)]

    shift_all = shift_parts(shift) + shift_parts(lax.ppermute(shift, "zh", SWAP))
    part = dot_parts(z_rows, shift_all)
    part = lax.all_to_all(part, "x", 0, 0, tiled=True)
    return 1.5 * z_half.astype(jnp.float32) + part.astype(jnp.float32).sum(0)


def solution(mesh):
    fine = Mesh(mesh.devices.reshape(SIZES), AXES)
    spec = P(("y", "zh", "c"), ("x", "zl"))
    return jax.shard_map(
        shards,
        mesh=fine,
        in_specs=(spec, spec),
        out_specs=spec,
        check_vma=False,
    )
```

time: 537 us -> 236 us (0.44)
  the two profiles are of different devices: /device:TPU:1 before, /device:TPU:32 now
where the time goes in v1:
time: 236 us; the launch traced here: 235 us
  waiting for transfers between devices  109 us (46%)
  starting transfers between devices  74.9 us (32%)
  blocking collectives  18.2 us (8%)
  between operations  13.6 us (6%)
  local copies, waits for them, and re-layouts  9.6 us (4%)
  Pallas kernels  6.45 us (3%)
  other arithmetic  4.2 us (2%)
    ppermute x1, waiting for transfers between devices, shards(): swapped = lax.ppermute(turned, 'zh', SWAP)  37.1 us
    all_to_all x2, starting transfers between devices, y_parts(): every = lax.all_to_all(jnp.stack([block] * 4), 'y', 0, 0, tiled=True)  27.3 us
    ppermute x1, waiting for transfers between devices, shards(): lax.ppermute(shift, 'zh', SWAP)  20.4 us
    all_to_all x1, waiting for transfers between devices, shards(): part = lax.all_to_all(part.reshape(16, 128, 256), PLANE, 0, 0, tiled=True)  18.3 us
    all_to_all x1, blocking collectives, shards(): part = lax.all_to_all(part, 'x', 0, 0, tiled=True)  18.2 us
    all_to_all x2, waiting for transfers between devices, shift_parts(): every = lax.all_to_all(spread, PLANE, 0, 0, tiled=True).reshape(4, 512, 256)  16.1 us
    ppermute x1, starting transfers between devices, shards(): swapped = lax.ppermute(turned, 'zh', SWAP)  14.8 us
    all_to_all x2, waiting for transfers between devices, y_parts(): every = lax.all_to_all(jnp.stack([block] * 4), 'y', 0, 0, tiled=True)  11.4 us
  transfers between devices with their start and end apart: 13, of which 7 were waited for; matrix products, arithmetic and copies ran while one was open for 1% of the time, Pallas kernels for 0%

profile of v1, /device:TPU:32, one launch (start us, length us, event | category | flops | bytes accessed | tf_op | source)
XLA Modules:
  0.0 235.5 jit_solution(4041072710282933890)
XLA Ops:
  6.5 0.0 all-gather.3.cloned.1.call-start
  6.5 1.8 convert_element_type.39
  8.3 0.0 all-gather.3.cloned.1.call-update
  8.3 1.1 convert_element_type.41
  9.4 0.7 collective-permute-start
  10.1 0.0 collective-permute-done
  10.1 1.0 stack.4
  11.1 22.5 %all-to-all-start = ((bf16[4,512,256]{2,1,0:T(8,128)(2,1)}), bf16[4,512,256]{2,1,0:T(8,128)(2,1)S(1)}, u32[]{:S(2)}, u32[]{:S(2)}) async-start(bf16[4,512,256]{2,1,0:T(8,128)(2,1)} %stack.4), calls=%async_computation | async-start | bytes 2097152 | tf_op jit(solution)/shard_map/all_to_all | solution.py:80
  33.6 14.8 %collective-permute-start.2 = (bf16[512,256]{1,0:T(8,128)(2,1)S(1)}, bf16[512,256]{1,0:T(8,128)(2,1)S(1)}, u32[]{:S(2)}, u32[]{:S(2)}) collective-permute-start(bf16[512,256]{1,0:T(8,128)(2,1)S(1)} %collective-permute-done), channel_id=1, source_target_pairs={{0,2},{2,0},{1,3},{3,1},{4,6},{6,4},{5,7},{7,5},{8,10},{10,8},{9,1... | collective-permute-start | bytes 786440 | tf_op jit(solution)/shard_map/ppermute | solution.py:85
  48.4 37.1 %collective-permute-done.2 = bf16[512,256]{1,0:T(8,128)(2,1)S(1)} collective-permute-done((bf16[512,256]{1,0:T(8,128)(2,1)S(1)}, bf16[512,256]{1,0:T(8,128)(2,1)S(1)}, u32[]{:S(2)}, u32[]{:S(2)}) %collective-permute-start.2) | collective-permute-done | bytes 262176 | tf_op jit(solution)/shard_map/ppermute | solution.py:85
  85.5 0.0 all-to-all-done.refs_0_
  85.5 1.0 stack.5
  86.5 4.9 %all-to-all-start.1 = ((bf16[4,512,256]{2,1,0:T(8,128)(2,1)}), bf16[4,512,256]{2,1,0:T(8,128)(2,1)S(1)}, u32[]{:S(2)}, u32[]{:S(2)}) async-start(bf16[4,512,256]{2,1,0:T(8,128)(2,1)} %stack.5), calls=%async_computation.1 | async-start | bytes 2097152 | tf_op jit(solution)/shard_map/all_to_all | solution.py:80
  91.4 1.9 collective-permute-start.1
  93.3 11.4 %all-to-all-done.1.refs_2_ = bf16[4,512,256]{2,1,0:T(8,128)(2,1)S(1)} async-done(((bf16[4,512,256]{2,1,0:T(8,128)(2,1)}), bf16[4,512,256]{2,1,0:T(8,128)(2,1)S(1)}, u32[]{:S(2)}, u32[]{:S(2)}) %all-to-all-start.1) | async-done | bytes 1048608 | tf_op jit(solution)/shard_map/all_to_all | solution.py:80
  104.7 1.9 collective-permute-start.3
  106.7 0.0 collective-permute-done.1.refs_1_
  106.7 2.6 %collective-permute-done.3.refs_3_ = bf16[4,512,256]{2,1,0:T(8,128)(2,1)S(1)} collective-permute-done((bf16[4,512,256]{2,1,0:T(8,128)(2,1)S(1)}, bf16[4,512,256]{2,1,0:T(8,128)(2,1)S(1)}, u32[]{:S(2)}, u32[]{:S(2)}) %collective-permute-start.3) | collective-permute-done | bytes 1048608 | tf_op jit(solution)/shard_map/ppermute | solution.py:53
  109.3 0.0 copy-start.2
  109.3 1.0 copy-done.2
  110.3 0.0 all-gather.3.cloned.1.call-done
  110.3 0.0 copy-start
  110.3 1.6 copy-done
  111.8 1.2 copy-done.3
  113.1 3.6 %shard_map.28 = bf16[4,512,256]{2,1,0:T(8,128)(2,1)} custom-call(bf16[8,512,256]{2,1,0:T(8,128)(2,1)S(1)} %bitcast.12, bf16[4,512,256]{2,1,0:T(8,128)(2,1)S(1)} %all-to-all-done.refs_0_, bf16[4,512,256]{2,1,0:T(8,128)(2,1)S(1)} %collective-permute-done.1.refs_1_, bf16[4,512,256]{2,1,0:T(8,128)(2,1)S(1)} %all-to-all-done.1.refs_2_, ...), custom_call_target="tpu_custom_call" | custom-call | flops 2147483648 | bytes 7340032 | tf_op jit(solution)/shard_map/pallas_call | solution.py:36
  116.6 3.7 %all-to-all-start.2 = ((bf16[16,128,256]{2,1,0:T(8,128)(2,1)}), bf16[16,128,256]{2,1,0:T(8,128)(2,1)S(1)}, u32[]{:S(2)}, u32[]{:S(2)}) async-start(bf16[16,128,256]{2,1,0:T(8,128)(2,1)} %bitcast.1), calls=%async_computation.2 | async-start | bytes 2097152 | tf_op jit(solution)/shard_map/all_to_all | solution.py:89
  120.3 18.3 %all-to-all-done.2 = bf16[16,128,256]{2,1,0:T(8,128)(2,1)S(1)} async-done(((bf16[16,128,256]{2,1,0:T(8,128)(2,1)}), bf16[16,128,256]{2,1,0:T(8,128)(2,1)S(1)}, u32[]{:S(2)}, u32[]{:S(2)}) %all-to-all-start.2) | async-done | bytes 1048608 | tf_op jit(solution)/shard_map/all_to_all | solution.py:89
  138.6 0.2 convert_reduce_fusion
  138.8 0.2 fusion.1
  139.0 1.1 broadcast_in_dim.22
  140.1 3.7 %all-to-all-start.3 = ((bf16[16,128,256]{2,1,0:T(8,128)(2,1)}), bf16[16,128,256]{2,1,0:T(8,128)(2,1)S(1)}, u32[]{:S(2)}, u32[]{:S(2)}) async-start(bf16[16,128,256]{2,1,0:T(8,128)(2,1)} %bitcast.3), calls=%async_computation.3 | async-start | bytes 2097152 | tf_op jit(solution)/shard_map/all_to_all | solution.py:95
  143.7 10.2 %collective-permute-start.5 = (bf16[4,128,256]{2,1,0:T(8,128)(2,1)S(1)}, bf16[4,128,256]{2,1,0:T(8,128)(2,1)S(1)}, u32[]{:S(2)}, u32[]{:S(2)}) collective-permute-start(bf16[4,128,256]{2,1,0:T(8,128)(2,1)S(1)} %fusion.1), channel_id=1, source_target_pairs={{0,2},{2,0},{1,3},{3,1},{4,6},{6,4},{5,7},{7,5},{8,10},{10,8},{9,1... | collective-permute-start | bytes 786440 | tf_op jit(solution)/shard_map/ppermute | solution.py:98
  153.9 20.4 %collective-permute-done.5 = bf16[4,128,256]{2,1,0:T(8,128)(2,1)S(1)} collective-permute-done((bf16[4,128,256]{2,1,0:T(8,128)(2,1)S(1)}, bf16[4,128,256]{2,1,0:T(8,128)(2,1)S(1)}, u32[]{:S(2)}, u32[]{:S(2)}) %collective-permute-start.5) | collective-permute-done | bytes 262176 | tf_op jit(solution)/shard_map/ppermute | solution.py:98
  174.3 0.0 all-to-all-done.3
  174.4 1.1 broadcast_in_dim.23
  175.4 6.9 %all-to-all-start.4 = ((bf16[16,128,256]{2,1,0:T(8,128)(2,1)}), bf16[16,128,256]{2,1,0:T(8,128)(2,1)S(1)}, u32[]{:S(2)}, u32[]{:S(2)}) async-start(bf16[16,128,256]{2,1,0:T(8,128)(2,1)} %bitcast.5), calls=%async_computation.4 | async-start | bytes 2097152 | tf_op jit(solution)/shard_map/all_to_all | solution.py:95
  182.4 1.9 collective-permute-start.4
  184.3 16.1 %all-to-all-done.4 = bf16[16,128,256]{2,1,0:T(8,128)(2,1)S(1)} async-done(((bf16[16,128,256]{2,1,0:T(8,128)(2,1)}), bf16[16,128,256]{2,1,0:T(8,128)(2,1)S(1)}, u32[]{:S(2)}, u32[]{:S(2)}) %all-to-all-start.4) | async-done | bytes 1048608 | tf_op jit(solution)/shard_map/all_to_all | solution.py:95
  200.3 1.9 collective-permute-start.6
  202.3 0.0 collective-permute-done.4.refs_1_
  202.3 2.6 %collective-permute-done.6.refs_3_ = bf16[4,512,256]{2,1,0:T(8,128)(2,1)S(1)} collective-permute-done((bf16[4,512,256]{2,1,0:T(8,128)(2,1)S(1)}, bf16[4,512,256]{2,1,0:T(8,128)(2,1)S(1)}, u32[]{:S(2)}, u32[]{:S(2)}) %collective-permute-start.6) | collective-permute-done | bytes 1048608 | tf_op jit(solution)/shard_map/ppermute | solution.py:53
  204.9 1.6 copy-done.1
  206.5 2.9 %shard_map.29 = bf16[4,512,256]{2,1,0:T(8,128)(2,1)S(1)} custom-call(bf16[8,512,256]{2,1,0:T(8,128)(2,1)S(1)} %bitcast.13, bf16[4,512,256]{2,1,0:T(8,128)(2,1)S(1)} %bitcast.9, bf16[4,512,256]{2,1,0:T(8,128)(2,1)S(1)} %collective-permute-done.4.refs_1_, bf16[4,512,256]{2,1,0:T(8,128)(2,1)S(1)} %bitcast.11, ...), custom_call_target="tpu_custom_call" | custom-call | flops 2147483648 | bytes 7340032 | tf_op jit(solution)/shard_map/pallas_call | solution.py:36
  209.4 0.0 copy-start.4
  209.4 18.2 %all_to_all.30 = bf16[4,512,256]{2,1,0:T(8,128)(2,1)S(1)} all-to-all(bf16[4,512,256]{2,1,0:T(8,128)(2,1)S(1)} %shard_map.29), channel_id=1, replica_groups=mesh['x'=4,'zl'=8,'y'=4,'zh'=2,'c'=2] {'x'}, dimensions={0} | all-to-all | bytes 2097152 | tf_op jit(solution)/shard_map/all_to_all | solution.py:100
  227.6 0.1 convert_reduce_fusion.1
  227.8 0.0 copy-done.4
  227.8 0.9 multiply_add_fusion
  (4 shorter events, 0.0 us)
Async XLA Ops:
  6.5 103.7 %all-gather.3.cloned.1.call-start = ((), (), s32[]{:S(2)}) async-start(), calls=%async_computation.6 | async-start | bytes 2359296 | tf_op jit(solution)/shard_map/all_gather | solution.py:77
  9.4 0.7 collective-permute-start
  11.1 74.3 %all-to-all-start = ((bf16[4,512,256]{2,1,0:T(8,128)(2,1)}), bf16[4,512,256]{2,1,0:T(8,128)(2,1)S(1)}, u32[]{:S(2)}, u32[]{:S(2)}) async-start(bf16[4,512,256]{2,1,0:T(8,128)(2,1)} %stack.4), calls=%async_computation | async-start | bytes 2097152 | tf_op jit(solution)/shard_map/all_to_all | solution.py:80
  33.6 51.9 %collective-permute-start.2 = (bf16[512,256]{1,0:T(8,128)(2,1)S(1)}, bf16[512,256]{1,0:T(8,128)(2,1)S(1)}, u32[]{:S(2)}, u32[]{:S(2)}) collective-permute-start(bf16[512,256]{1,0:T(8,128)(2,1)S(1)} %collective-permute-done), channel_id=1, source_target_pairs={{0,2},{2,0},{1,3},{3,1},{4,6},{6,4},{5,7},{7,5},{8,10},{10,8},{9,1... | collective-permute-start | bytes 786440 | tf_op jit(solution)/shard_map/ppermute | solution.py:85
  86.5 18.2 %all-to-all-start.1 = ((bf16[4,512,256]{2,1,0:T(8,128)(2,1)}), bf16[4,512,256]{2,1,0:T(8,128)(2,1)S(1)}, u32[]{:S(2)}, u32[]{:S(2)}) async-start(bf16[4,512,256]{2,1,0:T(8,128)(2,1)} %stack.5), calls=%async_computation.1 | async-start | bytes 2097152 | tf_op jit(solution)/shard_map/all_to_all | solution.py:80
  91.4 15.3 %collective-permute-start.1 = (bf16[4,512,256]{2,1,0:T(8,128)(2,1)S(1)}, bf16[4,512,256]{2,1,0:T(8,128)(2,1)S(1)}, u32[]{:S(2)}, u32[]{:S(2)}) collective-permute-start(bf16[4,512,256]{2,1,0:T(8,128)(2,1)S(1)} %all-to-all-done.refs_0_), channel_id=1, source_target_pairs={{0,1},{1,0},{2,3},{3,2},{4,5},{5,4},{6,7},{7,6},{8,9},{9,8},{10,11... | collective-permute-start | bytes 3145736 | tf_op jit(solution)/shard_map/ppermute | solution.py:53
  104.7 4.5 %collective-permute-start.3 = (bf16[4,512,256]{2,1,0:T(8,128)(2,1)S(1)}, bf16[4,512,256]{2,1,0:T(8,128)(2,1)S(1)}, u32[]{:S(2)}, u32[]{:S(2)}) collective-permute-start(bf16[4,512,256]{2,1,0:T(8,128)(2,1)S(1)} %all-to-all-done.1.refs_2_), channel_id=1, source_target_pairs={{0,1},{1,0},{2,3},{3,2},{4,5},{5,4},{6,7},{7,6},{8,9},{9,8},{10,11... | collective-permute-start | bytes 3145736 | tf_op jit(solution)/shard_map/ppermute | solution.py:53
  109.3 1.0 copy-start.2
  110.3 1.6 copy-start
  111.8 1.2 copy-start.3
  116.6 22.0 %all-to-all-start.2 = ((bf16[16,128,256]{2,1,0:T(8,128)(2,1)}), bf16[16,128,256]{2,1,0:T(8,128)(2,1)S(1)}, u32[]{:S(2)}, u32[]{:S(2)}) async-start(bf16[16,128,256]{2,1,0:T(8,128)(2,1)} %bitcast.1), calls=%async_computation.2 | async-start | bytes 2097152 | tf_op jit(solution)/shard_map/all_to_all | solution.py:89
  140.1 34.3 %all-to-all-start.3 = ((bf16[16,128,256]{2,1,0:T(8,128)(2,1)}), bf16[16,128,256]{2,1,0:T(8,128)(2,1)S(1)}, u32[]{:S(2)}, u32[]{:S(2)}) async-start(bf16[16,128,256]{2,1,0:T(8,128)(2,1)} %bitcast.3), calls=%async_computation.3 | async-start | bytes 2097152 | tf_op jit(solution)/shard_map/all_to_all | solution.py:95
  143.7 30.6 %collective-permute-start.5 = (bf16[4,128,256]{2,1,0:T(8,128)(2,1)S(1)}, bf16[4,128,256]{2,1,0:T(8,128)(2,1)S(1)}, u32[]{:S(2)}, u32[]{:S(2)}) collective-permute-start(bf16[4,128,256]{2,1,0:T(8,128)(2,1)S(1)} %fusion.1), channel_id=1, source_target_pairs={{0,2},{2,0},{1,3},{3,1},{4,6},{6,4},{5,7},{7,5},{8,10},{10,8},{9,1... | collective-permute-start | bytes 786440 | tf_op jit(solution)/shard_map/ppermute | solution.py:98
  175.4 24.9 %all-to-all-start.4 = ((bf16[16,128,256]{2,1,0:T(8,128)(2,1)}), bf16[16,128,256]{2,1,0:T(8,128)(2,1)S(1)}, u32[]{:S(2)}, u32[]{:S(2)}) async-start(bf16[16,128,256]{2,1,0:T(8,128)(2,1)} %bitcast.5), calls=%async_computation.4 | async-start | bytes 2097152 | tf_op jit(solution)/shard_map/all_to_all | solution.py:95
  182.4 19.9 %collective-permute-start.4 = (bf16[4,512,256]{2,1,0:T(8,128)(2,1)S(1)}, bf16[4,512,256]{2,1,0:T(8,128)(2,1)S(1)}, u32[]{:S(2)}, u32[]{:S(2)}) collective-permute-start(bf16[4,512,256]{2,1,0:T(8,128)(2,1)S(1)} %bitcast.8), channel_id=1, source_target_pairs={{0,1},{1,0},{2,3},{3,2},{4,5},{5,4},{6,7},{7,6},{8,9},{9,8},{10,11... | collective-permute-start | bytes 3145736 | tf_op jit(solution)/shard_map/ppermute | solution.py:53
  200.3 4.5 %collective-permute-start.6 = (bf16[4,512,256]{2,1,0:T(8,128)(2,1)S(1)}, bf16[4,512,256]{2,1,0:T(8,128)(2,1)S(1)}, u32[]{:S(2)}, u32[]{:S(2)}) collective-permute-start(bf16[4,512,256]{2,1,0:T(8,128)(2,1)S(1)} %bitcast.10), channel_id=1, source_target_pairs={{0,1},{1,0},{2,3},{3,2},{4,5},{5,4},{6,7},{7,6},{8,9},{9,8},{10,11... | collective-permute-start | bytes 3145736 | tf_op jit(solution)/shard_map/ppermute | solution.py:53
  204.9 1.6 copy-start.1
  209.4 18.4 %copy-start.4 = (f32[512,256]{1,0:T(8,128)S(1)}, f32[512,256]{1,0:T(8,128)}, u32[]{:S(2)}) copy-start(f32[512,256]{1,0:T(8,128)} %param.2) | copy-start | bytes 1572868
Sparse Core Ops, SparseCore 0:
  9.4 90.5 all-gather.2

commit v2 on v0

v2 whole, which is shorter than its diff:
```python
import jax
import jax.numpy as jnp
from jax import lax
from jax.experimental import pallas as pl
from jax.experimental.pallas import tpu as pltpu
from jax.sharding import Mesh
from jax.sharding import PartitionSpec as P

AXES = ("x", "zl", "y", "zh", "c")
SIZES = (4, 8, 4, 2, 2)
PLANE = ("x", "y")
RING = ("zl", "zh")
SWAP = [(0, 1), (1, 0)]


def flat_id(x, zl, y, zh, c):
    return (((x * 8 + zl) * 4 + y) * 2 + zh) * 2 + c


Z_RINGS = [
    [flat_id(x, z % 8, y, z // 8, c) for z in range(16)]
    for x in range(4)
    for y in range(4)
    for c in range(2)
]


def along_z(block, step):
    place = lambda z: (z % 8) * 2 + z // 8
    return lax.ppermute(block, RING, [(place(z), place((z + step) % 16)) for z in range(16)])


def dot_kernel(z_ref, own_ref, other_ref, out_ref, right):
    groups, _, depth, width = own_ref.shape
    c = lax.axis_index("c")

    @pl.when(pl.program_id(0) == 0)
    def _():
        for ref, core in ((own_ref, c), (other_ref, 1 - c)):
            for s in range(4):
                chunk = (s // 2) * 4 + core * 2 + s % 2
                for j in range(groups):
                    right[chunk, :, j * width : (j + 1) * width] = ref[j, s]

    total = jnp.dot(z_ref[0], right[0], preferred_element_type=jnp.float32)
    for k in range(1, 8):
        total += jnp.dot(z_ref[k], right[k], preferred_element_type=jnp.float32)
    for j in range(groups):
        out_ref[j, 0] = total[:, j * width : (j + 1) * width].astype(out_ref.dtype)


def dot_right(z_rows, own, other):
    groups, steps, depth, width = own.shape
    whole = pl.BlockSpec(own.shape, lambda s: (0, 0, 0, 0))
    return pl.pallas_call(
        dot_kernel,
        grid=(steps,),
        in_specs=[pl.BlockSpec((8, depth, depth), lambda s: (s // 2, s % 2, 0)), whole, whole],
        out_specs=pl.BlockSpec((groups, 1, depth, width), lambda s: (0, s, 0, 0)),
        out_shape=jax.ShapeDtypeStruct(own.shape, jnp.bfloat16),
        scratch_shapes=[pltpu.VMEM((8, depth, groups * width), jnp.bfloat16)],
        compiler_params=pltpu.CompilerParams(vmem_limit_bytes=32 * 2**20),
        cost_estimate=pl.CostEstimate(
            flops=2 * z_rows.size * groups * width,
            bytes_accessed=2 * (z_rows.size + 3 * own.size),
            transcendentals=0,
        ),
    )(z_rows, own, other)


def other_core(block):
    return lax.ppermute(block, "c", SWAP)


def make_shift(product, order, first_col):
    at = lax.axis_index
    rows = product.shape[1]
    row_ids = (
        lax.broadcasted_iota(jnp.int32, product.shape, 0) * 2048
        + at("y") // 2 * 1024
        + at("c") * 512
        + at("y") % 2 * rows
        + lax.broadcasted_iota(jnp.int32, product.shape, 1)
    )
    col_ids = first_col + lax.broadcasted_iota(jnp.int32, product.shape, 2)
    ident = jnp.where(row_ids == col_ids, 1.5, 0.0).astype(jnp.float32)
    poly = lax.reduce_precision(ident - 0.5 / order * product, 8, 7)
    return (poly - ident).astype(jnp.bfloat16)


def shards(z_iter, y_iter):
    at = lax.axis_index
    order = z_iter.shape[1] * lax.axis_size("x") * lax.axis_size("zl")
    z_half = z_iter.astype(jnp.bfloat16)
    y_half = y_iter.astype(jnp.bfloat16)
    z_rows = lax.all_gather(z_half, AXES, axis_index_groups=Z_RINGS)

    low = at("zh") == 0
    z = at("zh") * 8 + at("zl")
    middle = (z >= 4) & (z < 12)
    first_col = at("x") * 2048 + (at("zl") ^ 4) * 256 + jnp.where(middle, 0, 128)
    left, right = y_half[:, :128], y_half[:, 128:]
    up = along_z(jnp.where(low, left, right), 4)
    down = along_z(jnp.where(low, right, left), -4)
    y_both = jnp.stack([jnp.where(middle, up, down), jnp.where(middle, down, up)])
    y_both = y_both.reshape(4, 256, 128)

    turn = [(i * 4 + j, j * 4 + i) for i in range(4) for j in range(4)]
    turned = lax.ppermute(y_both, PLANE, turn)
    y_own = lax.all_to_all(jnp.stack([turned] * 4), "y", 0, 0, tiled=True)
    part = dot_right(z_rows, y_own, other_core(y_own))

    part = lax.all_to_all(part.reshape(16, 256, 128), PLANE, 0, 0, tiled=True)
    product = part.reshape(4, 4, 256, 128).astype(jnp.float32).sum(0)
    shift = make_shift(product, order, first_col)

    spread = jnp.broadcast_to(shift[:, None], (4, 4, 256, 128)).reshape(16, 256, 128)
    own = lax.all_to_all(spread, PLANE, 0, 0, tiled=True).reshape(4, 4, 256, 128)
    part = dot_right(z_rows, own, other_core(own))
    part = lax.all_to_all(part, "x", 0, 0, tiled=True)
    part = part.astype(jnp.float32).sum(0).astype(jnp.bfloat16).reshape(2, 512, 128)
    down = along_z(jnp.where(middle, part[0], part[1]), -4)
    up = along_z(jnp.where(middle, part[1], part[0]), 4)
    part = jnp.concatenate([jnp.where(low, down, up), jnp.where(low, up, down)], axis=1)
    return 1.5 * z_half.astype(jnp.float32) + part.astype(jnp.float32)


def solution(mesh):
    fine = Mesh(mesh.devices.reshape(SIZES), AXES)
    spec = P(("y", "zh", "c"), ("x", "zl"))
    return jax.shard_map(
        shards,
        mesh=fine,
        in_specs=(spec, spec),
        out_specs=spec,
        check_vma=False,
    )
```

time: 537 us -> 198 us (0.37)
  waiting for transfers between devices: 505 us -> 51.5 us
  blocking collectives: 0 us -> 67.4 us
  starting transfers between devices: 0.09 us -> 49.7 us
  matrix products: 14.6 us -> 0 us
  Pallas kernels: 0 us -> 7.99 us
    all_gather x3 -> x1, waiting for transfers between devices: 505 us -> 5.07 us  [shards(): z_rows = lax.all_gather(z_half, AXES, axis_index_groups=Z_RINGS)]
    all_to_all x0 -> x3, blocking collectives: none -> 67.4 us  [the longest x1 35.1 us: shards(): y_own = lax.all_to_all(jnp.stack([turned] * 4), 'y', 0, 0, tiled=True)]
    ppermute x0 -> x7, starting transfers between devices: none -> 42.5 us  [the longest x4 24.4 us: along_z(): lax.ppermute(block, RING, [(place(z), place((z + step) % 16)) for z in ra...]
    ppermute x0 -> x7, waiting for transfers between devices: none -> 34.7 us  [the longest x4 30.2 us: along_z(): lax.ppermute(block, RING, [(place(z), place((z + step) % 16)) for z in ra...]
    dot_general x2 -> x0, matrix products: 14.6 us -> none  [add_right(): return jnp.dot(z_rows, piece, preferred_element_type=jnp.float32)]
    all_to_all x0 -> x1, waiting for transfers between devices: none -> 11.7 us  [shards(): part = lax.all_to_all(part.reshape(16, 256, 128), PLANE, 0, 0, tiled=True)]
    pallas_call x0 -> x2, Pallas kernels: none -> 7.99 us  [dot_right(): pl.pallas_call(dot_kernel, grid=(steps,), in_specs=[pl.BlockSpec((8, dept...]
    all_to_all x0 -> x1, starting transfers between devices: none -> 7.21 us  [shards(): part = lax.all_to_all(part.reshape(16, 256, 128), PLANE, 0, 0, tiled=True)]
  transfers between devices with their start and end apart: 3 -> 9, of which waited for: 3 -> 8; matrix products, arithmetic and copies ran while one was open for 0% -> 1% of each run, Pallas kernels for 0% -> 0%
where the time goes in v2:
time: 198 us; the launch traced here: 197 us
  blocking collectives  67.4 us (34%)
  waiting for transfers between devices  51.5 us (26%)
  starting transfers between devices  49.7 us (25%)
  between operations  13.6 us (7%)
  Pallas kernels  7.99 us (4%)
  other arithmetic  4.42 us (2%)
  local copies, waits for them, and re-layouts  2.59 us (1%)
    all_to_all x1, blocking collectives, shards(): y_own = lax.all_to_all(jnp.stack([turned] * 4), 'y', 0, 0, tiled=True)  35.1 us
    ppermute x4, waiting for transfers between devices, along_z(): lax.ppermute(block, RING, [(place(z), place((z + step) % 16)) for z in ra...  30.2 us
    ppermute x4, starting transfers between devices, along_z(): lax.ppermute(block, RING, [(place(z), place((z + step) % 16)) for z in ra...  24.4 us
    ppermute x2, starting transfers between devices, other_core(): return lax.ppermute(block, 'c', SWAP)  17.4 us
    all_to_all x1, blocking collectives, shards(): part = lax.all_to_all(part, 'x', 0, 0, tiled=True)  17.4 us
    all_to_all x1, blocking collectives, shards(): lax.all_to_all(spread, PLANE, 0, 0, tiled=True).reshape(4, 4, 256, 128)  14.9 us
    all_to_all x1, waiting for transfers between devices, shards(): part = lax.all_to_all(part.reshape(16, 256, 128), PLANE, 0, 0, tiled=True)  11.7 us
    pallas_call x2, Pallas kernels, dot_right(): pl.pallas_call(dot_kernel, grid=(steps,), in_specs=[pl.BlockSpec((8, dept...  7.99 us
  transfers between devices with their start and end apart: 9, of which 8 were waited for; matrix products, arithmetic and copies ran while one was open for 1% of the time, Pallas kernels for 0%

profile of v2, /device:TPU:1, one launch (start us, length us, event | category | flops | bytes accessed | tf_op | source)
XLA Modules:
  0.0 197.2 jit_solution(7205782380868630939)
XLA Ops:
  6.5 0.0 all-gather.3.cloned.1.call-start
  6.5 1.8 convert_element_type.27
  8.3 0.0 all-gather.3.cloned.1.call-update
  8.3 1.1 convert_element_type.29
  9.4 9.6 %collective-permute-start = (bf16[512,128]{1,0:T(8,128)(2,1)S(1)}, bf16[512,128]{1,0:T(8,128)(2,1)S(1)}, u32[]{:S(2)}, u32[]{:S(2)}) collective-permute-start(bf16[512,128]{1,0:T(8,128)(2,1)S(1)} %get-tuple-element.11), channel_id=1, source_target_pairs={{0,64},{16,80},{32,96},{48,112},{64,2},{80,18},{96,34},{112,50},{2... | collective-permute-start | bytes 393224 | tf_op jit(solution)/shard_map/ppermute | solution.py:30
  19.1 5.6 %collective-permute-start.1 = (bf16[512,128]{1,0:T(8,128)(2,1)S(1)}, bf16[512,128]{1,0:T(8,128)(2,1)S(1)}, u32[]{:S(2)}, u32[]{:S(2)}) collective-permute-start(bf16[512,128]{1,0:T(8,128)(2,1)S(1)} %get-tuple-element.12), channel_id=1, source_target_pairs={{0,66},{16,82},{32,98},{48,114},{64,0},{80,16},{96,32},{112,48},{2... | collective-permute-start | bytes 393224 | tf_op jit(solution)/shard_map/ppermute | solution.py:30
  24.7 0.9 collective-permute-done
  25.5 14.8 %collective-permute-done.1 = bf16[512,128]{1,0:T(8,128)(2,1)S(1)} collective-permute-done((bf16[512,128]{1,0:T(8,128)(2,1)S(1)}, bf16[512,128]{1,0:T(8,128)(2,1)S(1)}, u32[]{:S(2)}, u32[]{:S(2)}) %collective-permute-start.1) | collective-permute-done | bytes 131104 | tf_op jit(solution)/shard_map/ppermute | solution.py:30
  40.4 0.7 collective-permute-start.2
  41.0 0.0 collective-permute-done.2
  41.1 0.2 stack.19
  41.3 35.1 %all_to_all.20.own_ref = bf16[4,4,256,128]{3,2,1,0:T(8,128)(2,1)S(1)} all-to-all(bf16[4,4,256,128]{3,2,1,0:T(8,128)(2,1)S(1)} %stack.19), channel_id=1, replica_groups=mesh['x'=4,'zl'=8,'y'=4,'zh'=2,'c'=2] {'y'}, dimensions={0} | all-to-all | bytes 2097152 | tf_op jit(solution)/shard_map/all_to_all | solution.py:110
  76.3 4.4 %collective-permute-start.3 = (bf16[4,4,256,128]{3,2,1,0:T(8,128)(2,1)S(1)}, bf16[4,4,256,128]{3,2,1,0:T(8,128)(2,1)S(1)}, u32[]{:S(2)}, u32[]{:S(2)}) collective-permute-start(bf16[4,4,256,128]{3,2,1,0:T(8,128)(2,1)S(1)} %all_to_all.20.own_ref), channel_id=1, source_target_pairs={{0,1},{1,0},{2,3},{3,2},{4,5},{5,4},{6,7},{7,6},{8,9},{9,8},{10,11... | collective-permute-start | bytes 3145736 | tf_op jit(solution)/shard_map/ppermute | solution.py:72
  80.8 2.3 %collective-permute-done.3.other_ref = bf16[4,4,256,128]{3,2,1,0:T(8,128)(2,1)S(1)} collective-permute-done((bf16[4,4,256,128]{3,2,1,0:T(8,128)(2,1)S(1)}, bf16[4,4,256,128]{3,2,1,0:T(8,128)(2,1)S(1)}, u32[]{:S(2)}, u32[]{:S(2)}) %collective-permute-start.3) | collective-permute-done | bytes 1048608 | tf_op jit(solution)/shard_map/ppermute | solution.py:72
  83.0 5.1 %all-gather.3.cloned.1.call-done = bf16[8192,256]{1,0:T(8,128)(2,1)} async-done(((bf16[512,256]{1,0:T(8,128)(2,1)}), bf16[8192,256]{1,0:T(8,128)(2,1)}) %all-gather.3.cloned.1.call-update) | async-done | bytes 4194320 | tf_op jit(solution)/shard_map/all_gather | solution.py:96
  88.1 0.0 copy-start
  88.1 2.2 %copy-done = bf16[8192,256]{1,0:T(8,128)(2,1)S(1)} copy-done((bf16[8192,256]{1,0:T(8,128)(2,1)S(1)}, bf16[8192,256]{1,0:T(8,128)(2,1)}, u32[]{:S(2)}) %copy-start) | copy-done | bytes 4194328
  90.3 4.3 %shard_map.28 = bf16[4,4,256,128]{3,2,1,0:T(8,128)(2,1)} custom-call(bf16[16,512,256]{2,1,0:T(8,128)(2,1)S(1)} %bitcast.15, bf16[4,4,256,128]{3,2,1,0:T(8,128)(2,1)S(1)} %all_to_all.20.own_ref, bf16[4,4,256,128]{3,2,1,0:T(8,128)(2,1)S(1)} %collective-permute-done.3.other_ref), custom_call_target="tpu_custom_call" | custom-call | flops 2147483648 | bytes 7340032 | tf_op jit(solution)/shard_map/pallas_call | solution.py:55
  94.6 7.2 %all-to-all-start.1 = ((bf16[16,256,128]{2,1,0:T(8,128)(2,1)}), bf16[16,256,128]{2,1,0:T(8,128)(2,1)S(1)}, u32[]{:S(2)}, u32[]{:S(2)}) async-start(bf16[16,256,128]{2,1,0:T(8,128)(2,1)} %bitcast.4), calls=%async_computation.1 | async-start | bytes 2097152 | tf_op jit(solution)/shard_map/all_to_all | solution.py:113
  101.9 11.7 %all-to-all-done.1 = bf16[16,256,128]{2,1,0:T(8,128)(2,1)S(1)} async-done(((bf16[16,256,128]{2,1,0:T(8,128)(2,1)}), bf16[16,256,128]{2,1,0:T(8,128)(2,1)S(1)}, u32[]{:S(2)}, u32[]{:S(2)}) %all-to-all-start.1) | async-done | bytes 1048608 | tf_op jit(solution)/shard_map/all_to_all | solution.py:113
  113.6 0.0 copy-start.1
  113.6 0.2 convert_reduce_fusion
  113.8 0.2 fusion.1
  114.0 0.2 broadcast_in_dim.16
  114.2 14.9 %all_to_all.21 = bf16[16,256,128]{2,1,0:T(8,128)(2,1)S(1)} all-to-all(bf16[16,256,128]{2,1,0:T(8,128)(2,1)S(1)} %bitcast.17), channel_id=1, replica_groups=mesh['x'=4,'zl'=8,'y'=4,'zh'=2,'c'=2] {'x','y'}, dimensions={0} | all-to-all | bytes 2097152 | tf_op jit(solution)/shard_map/all_to_all | solution.py:118
  129.1 13.0 %collective-permute-start.4 = (bf16[4,4,256,128]{3,2,1,0:T(8,128)(2,1)S(1)}, bf16[4,4,256,128]{3,2,1,0:T(8,128)(2,1)S(1)}, u32[]{:S(2)}, u32[]{:S(2)}) collective-permute-start(bf16[4,4,256,128]{3,2,1,0:T(8,128)(2,1)S(1)} %bitcast.13), channel_id=1, source_target_pairs={{0,1},{1,0},{2,3},{3,2},{4,5},{5,4},{6,7},{7,6},{8,9},{9,8},{10,11... | collective-permute-start | bytes 3145736 | tf_op jit(solution)/shard_map/ppermute | solution.py:72
  142.1 2.3 %collective-permute-done.4.other_ref = bf16[4,4,256,128]{3,2,1,0:T(8,128)(2,1)S(1)} collective-permute-done((bf16[4,4,256,128]{3,2,1,0:T(8,128)(2,1)S(1)}, bf16[4,4,256,128]{3,2,1,0:T(8,128)(2,1)S(1)}, u32[]{:S(2)}, u32[]{:S(2)}) %collective-permute-start.4) | collective-permute-done | bytes 1048608 | tf_op jit(solution)/shard_map/ppermute | solution.py:72
  144.4 0.0 copy-done.1
  144.4 3.7 %shard_map.29 = bf16[4,4,256,128]{3,2,1,0:T(8,128)(2,1)S(1)} custom-call(bf16[16,512,256]{2,1,0:T(8,128)(2,1)S(1)} %bitcast.16, bf16[4,4,256,128]{3,2,1,0:T(8,128)(2,1)S(1)} %bitcast.14, bf16[4,4,256,128]{3,2,1,0:T(8,128)(2,1)S(1)} %collective-permute-done.4.other_ref), custom_call_target="tpu_custom_call" | custom-call | flops 2147483648 | bytes 7340032 | tf_op jit(solution)/shard_map/pallas_call | solution.py:55
  148.1 0.0 copy-start.2
  148.1 17.4 %all_to_all.22 = bf16[4,4,256,128]{3,2,1,0:T(8,128)(2,1)S(1)} all-to-all(bf16[4,4,256,128]{3,2,1,0:T(8,128)(2,1)S(1)} %shard_map.29), channel_id=1, replica_groups=mesh['x'=4,'zl'=8,'y'=4,'zh'=2,'c'=2] {'x'}, dimensions={0} | all-to-all | bytes 2097152 | tf_op jit(solution)/shard_map/all_to_all | solution.py:120
  165.5 0.2 reduce_sum.22
  165.7 5.1 %collective-permute-start.6 = (bf16[512,128]{1,0:T(8,128)(2,1)S(1)}, bf16[512,128]{1,0:T(8,128)(2,1)S(1)}, u32[]{:S(2)}, u32[]{:S(2)}) collective-permute-start(bf16[512,128]{1,0:T(8,128)(2,1)S(1)} %bitcast.21), channel_id=1, source_target_pairs={{0,64},{16,80},{32,96},{48,112},{64,2},{80,18},{96,34},{112,50},{2... | collective-permute-start | bytes 393224 | tf_op jit(solution)/shard_map/ppermute | solution.py:30
  170.8 4.1 %collective-permute-start.5 = (bf16[512,128]{1,0:T(8,128)(2,1)S(1)}, bf16[512,128]{1,0:T(8,128)(2,1)S(1)}, u32[]{:S(2)}, u32[]{:S(2)}) collective-permute-start(bf16[512,128]{1,0:T(8,128)(2,1)S(1)} %bitcast.20), channel_id=1, source_target_pairs={{0,66},{16,82},{32,98},{48,114},{64,0},{80,16},{96,32},{112,48},{2... | collective-permute-start | bytes 393224 | tf_op jit(solution)/shard_map/ppermute | solution.py:30
  174.9 3.9 %collective-permute-done.6 = bf16[512,128]{1,0:T(8,128)(2,1)S(1)} collective-permute-done((bf16[512,128]{1,0:T(8,128)(2,1)S(1)}, bf16[512,128]{1,0:T(8,128)(2,1)S(1)}, u32[]{:S(2)}, u32[]{:S(2)}) %collective-permute-start.6) | collective-permute-done | bytes 131104 | tf_op jit(solution)/shard_map/ppermute | solution.py:30
  178.8 10.7 %collective-permute-done.5 = bf16[512,128]{1,0:T(8,128)(2,1)S(1)} collective-permute-done((bf16[512,128]{1,0:T(8,128)(2,1)S(1)}, bf16[512,128]{1,0:T(8,128)(2,1)S(1)}, u32[]{:S(2)}, u32[]{:S(2)}) %collective-permute-start.5) | collective-permute-done | bytes 131104 | tf_op jit(solution)/shard_map/ppermute | solution.py:30
  189.5 0.0 copy-done.2
  189.5 0.9 convert_add_fusion
  (7 shorter events, 0.1 us)
Async XLA Ops:
  6.5 81.6 %all-gather.3.cloned.1.call-start = ((), (), s32[]{:S(2)}) async-start(), calls=%async_computation.4 | async-start | bytes 4456448 | tf_op jit(solution)/shard_map/all_gather | solution.py:96
  9.4 16.1 %collective-permute-start = (bf16[512,128]{1,0:T(8,128)(2,1)S(1)}, bf16[512,128]{1,0:T(8,128)(2,1)S(1)}, u32[]{:S(2)}, u32[]{:S(2)}) collective-permute-start(bf16[512,128]{1,0:T(8,128)(2,1)S(1)} %get-tuple-element.11), channel_id=1, source_target_pairs={{0,64},{16,80},{32,96},{48,112},{64,2},{80,18},{96,34},{112,50},{2... | collective-permute-start | bytes 393224 | tf_op jit(solution)/shard_map/ppermute | solution.py:30
  19.1 21.2 %collective-permute-start.1 = (bf16[512,128]{1,0:T(8,128)(2,1)S(1)}, bf16[512,128]{1,0:T(8,128)(2,1)S(1)}, u32[]{:S(2)}, u32[]{:S(2)}) collective-permute-start(bf16[512,128]{1,0:T(8,128)(2,1)S(1)} %get-tuple-element.12), channel_id=1, source_target_pairs={{0,66},{16,82},{32,98},{48,114},{64,0},{80,16},{96,32},{112,48},{2... | collective-permute-start | bytes 393224 | tf_op jit(solution)/shard_map/ppermute | solution.py:30
  40.4 0.7 collective-permute-start.2
  76.3 6.7 %collective-permute-start.3 = (bf16[4,4,256,128]{3,2,1,0:T(8,128)(2,1)S(1)}, bf16[4,4,256,128]{3,2,1,0:T(8,128)(2,1)S(1)}, u32[]{:S(2)}, u32[]{:S(2)}) collective-permute-start(bf16[4,4,256,128]{3,2,1,0:T(8,128)(2,1)S(1)} %all_to_all.20.own_ref), channel_id=1, source_target_pairs={{0,1},{1,0},{2,3},{3,2},{4,5},{5,4},{6,7},{7,6},{8,9},{9,8},{10,11... | collective-permute-start | bytes 3145736 | tf_op jit(solution)/shard_map/ppermute | solution.py:72
  88.1 2.2 %copy-start = (bf16[8192,256]{1,0:T(8,128)(2,1)S(1)}, bf16[8192,256]{1,0:T(8,128)(2,1)}, u32[]{:S(2)}) copy-start(bf16[8192,256]{1,0:T(8,128)(2,1)} %all-gather.3.cloned.1.call-done) | copy-start | bytes 12582916
  94.6 19.0 %all-to-all-start.1 = ((bf16[16,256,128]{2,1,0:T(8,128)(2,1)}), bf16[16,256,128]{2,1,0:T(8,128)(2,1)S(1)}, u32[]{:S(2)}, u32[]{:S(2)}) async-start(bf16[16,256,128]{2,1,0:T(8,128)(2,1)} %bitcast.4), calls=%async_computation.1 | async-start | bytes 2097152 | tf_op jit(solution)/shard_map/all_to_all | solution.py:113
  113.6 30.8 %copy-start.1 = (bf16[8192,256]{1,0:T(8,128)(2,1)S(1)}, bf16[8192,256]{1,0:T(8,128)(2,1)}, u32[]{:S(2)}) copy-start(bf16[8192,256]{1,0:T(8,128)(2,1)} %all-gather.3.cloned.1.call-done) | copy-start | bytes 12582916
  129.1 15.3 %collective-permute-start.4 = (bf16[4,4,256,128]{3,2,1,0:T(8,128)(2,1)S(1)}, bf16[4,4,256,128]{3,2,1,0:T(8,128)(2,1)S(1)}, u32[]{:S(2)}, u32[]{:S(2)}) collective-permute-start(bf16[4,4,256,128]{3,2,1,0:T(8,128)(2,1)S(1)} %bitcast.13), channel_id=1, source_target_pairs={{0,1},{1,0},{2,3},{3,2},{4,5},{5,4},{6,7},{7,6},{8,9},{9,8},{10,11... | collective-permute-start | bytes 3145736 | tf_op jit(solution)/shard_map/ppermute | solution.py:72
  148.1 41.4 %copy-start.2 = (f32[512,256]{1,0:T(8,128)S(1)}, f32[512,256]{1,0:T(8,128)}, u32[]{:S(2)}) copy-start(f32[512,256]{1,0:T(8,128)} %param.2) | copy-start | bytes 1572868
  165.7 13.1 %collective-permute-start.6 = (bf16[512,128]{1,0:T(8,128)(2,1)S(1)}, bf16[512,128]{1,0:T(8,128)(2,1)S(1)}, u32[]{:S(2)}, u32[]{:S(2)}) collective-permute-start(bf16[512,128]{1,0:T(8,128)(2,1)S(1)} %bitcast.21), channel_id=1, source_target_pairs={{0,64},{16,80},{32,96},{48,112},{64,2},{80,18},{96,34},{112,50},{2... | collective-permute-start | bytes 393224 | tf_op jit(solution)/shard_map/ppermute | solution.py:30
  170.8 18.7 %collective-permute-start.5 = (bf16[512,128]{1,0:T(8,128)(2,1)S(1)}, bf16[512,128]{1,0:T(8,128)(2,1)S(1)}, u32[]{:S(2)}, u32[]{:S(2)}) collective-permute-start(bf16[512,128]{1,0:T(8,128)(2,1)S(1)} %bitcast.20), channel_id=1, source_target_pairs={{0,66},{16,82},{32,98},{48,114},{64,0},{80,16},{96,32},{112,48},{2... | collective-permute-start | bytes 393224 | tf_op jit(solution)/shard_map/ppermute | solution.py:30
Sparse Core Ops, SparseCore 0:
  9.4 78.6 all-gather.2

commit v3 on v2

--- a/solution.py
+++ b/solution.py
@@ -13,38 +13,47 @@
 SWAP = [(0, 1), (1, 0)]
 
 
-def flat_id(x, zl, y, zh, c):
-    return (((x * 8 + zl) * 4 + y) * 2 + zh) * 2 + c
-
-
-Z_RINGS = [
-    [flat_id(x, z % 8, y, z // 8, c) for z in range(16)]
-    for x in range(4)
-    for y in range(4)
-    for c in range(2)
-]
-
-
 def along_z(block, step):
     place = lambda z: (z % 8) * 2 + z // 8
     return lax.ppermute(block, RING, [(place(z), place((z + step) % 16)) for z in range(16)])
 
 
-def dot_kernel(z_ref, own_ref, other_ref, out_ref, right):
+def round_z(block):
+    place = lambda z, c: ((z % 8) * 2 + z // 8) * 2 + c
+    pairs = [(place(z, c), place((z + 1 - 2 * c) % 16, c)) for z in range(16) for c in range(2)]
+    return lax.ppermute(block, RING + ("c",), pairs)
+
+
+def dot_kernel(*refs):
+    own_ref, other_ref, out_ref, left, right, sem = refs[11:]
+    chunks = list(refs[:9]) + [ref.at[n] for ref in refs[9:11] for n in range(ref.shape[0])]
     groups, _, depth, width = own_ref.shape
     c = lax.axis_index("c")
+    step = pl.program_id(0)
 
-    @pl.when(pl.program_id(0) == 0)
+    @pl.when(step == 0)
     def _():
+        z = lax.axis_index("zh") * 8 + lax.axis_index("zl")
+        copies = []
+        for n, ref in enumerate(chunks):
+            away = -n if n <= 8 else n - 8
+            at = lax.rem(z + away * (1 - 2 * c) + 16, 16)
+            copies.append(pltpu.make_async_copy(ref, left.at[at], sem.at[n]))
+        for copy in copies:
+            copy.start()
         for ref, core in ((own_ref, c), (other_ref, 1 - c)):
             for s in range(4):
                 chunk = (s // 2) * 4 + core * 2 + s % 2
                 for j in range(groups):
                     right[chunk, :, j * width : (j + 1) * width] = ref[j, s]
+        for copy in copies:
+            copy.wait()
 
-    total = jnp.dot(z_ref[0], right[0], preferred_element_type=jnp.float32)
+    first = (step // 2) * 8
+    rows = pl.ds(pl.multiple_of((step % 2) * depth, depth), depth)
+    total = jnp.dot(left[first, rows, :], right[0], preferred_element_type=jnp.float32)
     for k in range(1, 8):
-        total += jnp.dot(z_ref[k], right[k], preferred_element_type=jnp.float32)
+        total += jnp.dot(left[first + k, rows, :], right[k], preferred_element_type=jnp.float32)
     for j in range(groups):
         out_ref[j, 0] = total[:, j * width : (j + 1) * width].astype(out_ref.dtype)
 
@@ -55,17 +64,21 @@
     return pl.pallas_call(
         dot_kernel,
         grid=(steps,),
-        in_specs=[pl.BlockSpec((8, depth, depth), lambda s: (s // 2, s % 2, 0)), whole, whole],
+        in_specs=[pl.BlockSpec(memory_space=pl.ANY)] * 11 + [whole, whole],
         out_specs=pl.BlockSpec((groups, 1, depth, width), lambda s: (0, s, 0, 0)),
         out_shape=jax.ShapeDtypeStruct(own.shape, jnp.bfloat16),
-        scratch_shapes=[pltpu.VMEM((8, depth, groups * width), jnp.bfloat16)],
+        scratch_shapes=[
+            pltpu.VMEM((16,) + z_rows[0].shape, jnp.bfloat16),
+            pltpu.VMEM((8, depth, groups * width), jnp.bfloat16),
+            pltpu.SemaphoreType.DMA((16,)),
+        ],
         compiler_params=pltpu.CompilerParams(vmem_limit_bytes=32 * 2**20),
         cost_estimate=pl.CostEstimate(
-            flops=2 * z_rows.size * groups * width,
-            bytes_accessed=2 * (z_rows.size + 3 * own.size),
+            flops=32 * z_rows[0].size * groups * width,
+            bytes_accessed=2 * (16 * z_rows[0].size + 3 * own.size),
             transcendentals=0,
         ),
-    )(z_rows, own, other)
+    )(*z_rows, own, other)
 
 
 def other_core(block):
@@ -93,7 +106,15 @@
     order = z_iter.shape[1] * lax.axis_size("x") * lax.axis_size("zl")
     z_half = z_iter.astype(jnp.bfloat16)
     y_half = y_iter.astype(jnp.bfloat16)
-    z_rows = lax.all_gather(z_half, AXES, axis_index_groups=Z_RINGS)
+
+    mine = [round_z(z_half)]
+    theirs = [round_z(other_core(z_half))]
+    for n in range(1, 8):
+        mine.append(round_z(mine[-1]))
+        if n < 7:
+            theirs.append(round_z(theirs[-1]))
+    z_rows = [z_half] + mine
+    z_rows += [other_core(jnp.stack(theirs[:4])), other_core(jnp.stack(theirs[4:]))]
 
     low = at("zh") == 0
     z = at("zh") * 8 + at("zl")

time: 198 us -> 216 us (1.091)
  the two profiles are of different devices: /device:TPU:1 before, /device:TPU:97 now
where the time goes in v3:
time: 216 us; the launch traced here: 215 us
  starting transfers between devices  102 us (47%)
  waiting for transfers between devices  59.5 us (28%)
  blocking collectives  35.9 us (17%)
  Pallas kernels  9.21 us (4%)
  other arithmetic  3.99 us (2%)
  local copies, waits for them, and re-layouts  2.9 us (1%)
    ppermute x15, starting transfers between devices, round_z(): return lax.ppermute(block, RING + ('c',), pairs)  43.7 us
    ppermute x15, waiting for transfers between devices, round_z(): return lax.ppermute(block, RING + ('c',), pairs)  28.7 us
    ppermute x5, starting transfers between devices, other_core(): return lax.ppermute(block, 'c', SWAP)  24.7 us
    ppermute x4, starting transfers between devices, along_z(): lax.ppermute(block, RING, [(place(z), place((z + step) % 16)) for z in ra...  22.9 us
    all_to_all x1, blocking collectives, shards(): lax.all_to_all(spread, PLANE, 0, 0, tiled=True).reshape(4, 4, 256, 128)  18.6 us
    all_to_all x1, blocking collectives, shards(): part = lax.all_to_all(part, 'x', 0, 0, tiled=True)  17.3 us
    all_to_all x1, waiting for transfers between devices, shards(): part = lax.all_to_all(part.reshape(16, 256, 128), PLANE, 0, 0, tiled=True)  15 us
    ppermute x4, waiting for transfers between devices, along_z(): lax.ppermute(block, RING, [(place(z), place((z + step) % 16)) for z in ra...  12.5 us
  transfers between devices with their start and end apart: 27, of which 12 were waited for; matrix products, arithmetic and copies ran while one was open for 1% of the time, Pallas kernels for 0%

profile of v3, /device:TPU:97, one launch (start us, length us, event | category | flops | bytes accessed | tf_op | source)
XLA Modules:
  0.0 214.6 jit_solution(14666804091281031225)
XLA Ops:
  0.0 1.1 convert_element_type.27.refs_0_
  1.1 2.6 %collective-permute-start.8 = (bf16[512,256]{1,0:T(8,128)(2,1)S(1)}, bf16[512,256]{1,0:T(8,128)(2,1)S(1)}, u32[]{:S(2)}, u32[]{:S(2)}) collective-permute-start(bf16[512,256]{1,0:T(8,128)(2,1)S(1)} %convert_element_type.27.refs_0_), channel_id=1, source_target_pairs={{0,1},{1,0},{2,3},{3,2},{4,5},{5,4},{6,7},{7,6},{8,9},{9,8},{10,11... | collective-permute-start | bytes 786440 | tf_op jit(solution)/shard_map/ppermute | solution.py:85
  3.8 1.1 collective-permute-done.8
  4.9 1.9 collective-permute-start.9
  6.8 8.8 %collective-permute-start.18 = (bf16[512,128]{1,0:T(8,128)(2,1)S(1)}, bf16[512,128]{1,0:T(8,128)(2,1)S(1)}, u32[]{:S(2)}, u32[]{:S(2)}) collective-permute-start(bf16[512,128]{1,0:T(8,128)(2,1)S(1)} %get-tuple-element.11), channel_id=1, source_target_pairs={{0,64},{16,80},{32,96},{48,112},{64,2},{80,18},{96,34},{112,50},{2... | collective-permute-start | bytes 393224 | tf_op jit(solution)/shard_map/ppermute | solution.py:18
  15.6 3.6 %collective-permute-start.19 = (bf16[512,128]{1,0:T(8,128)(2,1)S(1)}, bf16[512,128]{1,0:T(8,128)(2,1)S(1)}, u32[]{:S(2)}, u32[]{:S(2)}) collective-permute-start(bf16[512,128]{1,0:T(8,128)(2,1)S(1)} %get-tuple-element.12), channel_id=1, source_target_pairs={{0,66},{16,82},{32,98},{48,114},{64,0},{80,16},{96,32},{112,48},{2... | collective-permute-start | bytes 393224 | tf_op jit(solution)/shard_map/ppermute | solution.py:18
  19.2 2.6 %collective-permute-start = (bf16[512,256]{1,0:T(8,128)(2,1)S(1)}, bf16[512,256]{1,0:T(8,128)(2,1)S(1)}, u32[]{:S(2)}, u32[]{:S(2)}) collective-permute-start(bf16[512,256]{1,0:T(8,128)(2,1)S(1)} %convert_element_type.27.refs_0_), channel_id=1, source_target_pairs={{0,16},{1,115},{16,32},{17,1},{32,48},{33,17},{48,64},{49,33},{64,... | collective-permute-start | bytes 786440 | tf_op jit(solution)/shard_map/ppermute | solution.py:24
  21.9 2.8 %collective-permute-start.10 = (bf16[512,256]{1,0:T(8,128)(2,1)S(1)}, bf16[512,256]{1,0:T(8,128)(2,1)S(1)}, u32[]{:S(2)}, u32[]{:S(2)}) collective-permute-start(bf16[512,256]{1,0:T(8,128)(2,1)S(1)} %collective-permute-done.9), channel_id=1, source_target_pairs={{0,16},{1,115},{16,32},{17,1},{32,48},{33,17},{48,64},{49,33},{64,... | collective-permute-start | bytes 786440 | tf_op jit(solution)/shard_map/ppermute | solution.py:24
  24.7 3.0 %collective-permute-done.18 = bf16[512,128]{1,0:T(8,128)(2,1)S(1)} collective-permute-done((bf16[512,128]{1,0:T(8,128)(2,1)S(1)}, bf16[512,128]{1,0:T(8,128)(2,1)S(1)}, u32[]{:S(2)}, u32[]{:S(2)}) %collective-permute-start.18) | collective-permute-done | bytes 131104 | tf_op jit(solution)/shard_map/ppermute | solution.py:18
  28.5 10.5 %collective-permute-done.10 = bf16[512,256]{1,0:T(8,128)(2,1)S(1)} collective-permute-done((bf16[512,256]{1,0:T(8,128)(2,1)S(1)}, bf16[512,256]{1,0:T(8,128)(2,1)S(1)}, u32[]{:S(2)}, u32[]{:S(2)}) %collective-permute-start.10) | collective-permute-done | bytes 262176 | tf_op jit(solution)/shard_map/ppermute | solution.py:24
  39.0 1.9 collective-permute-start.11
  40.9 2.1 collective-permute-start.1
  43.1 1.2 stack.55
  44.3 4.2 %all-to-all-start = ((bf16[4,4,256,128]{3,2,1,0:T(8,128)(2,1)}), bf16[4,4,256,128]{3,2,1,0:T(8,128)(2,1)S(1)}, u32[]{:S(2)}, u32[]{:S(2)}) async-start(bf16[4,4,256,128]{3,2,1,0:T(8,128)(2,1)} %stack.55), calls=%async_computation | async-start | bytes 2097152 | tf_op jit(solution)/shard_map/all_to_all | solution.py:131
  48.5 3.3 %collective-permute-start.12 = (bf16[512,256]{1,0:T(8,128)(2,1)S(1)}, bf16[512,256]{1,0:T(8,128)(2,1)S(1)}, u32[]{:S(2)}, u32[]{:S(2)}) collective-permute-start(bf16[512,256]{1,0:T(8,128)(2,1)S(1)} %collective-permute-done.11), channel_id=1, source_target_pairs={{0,16},{1,115},{16,32},{17,1},{32,48},{33,17},{48,64},{49,33},{64,... | collective-permute-start | bytes 786440 | tf_op jit(solution)/shard_map/ppermute | solution.py:24
  51.9 8.5 %collective-permute-start.2 = (bf16[512,256]{1,0:T(8,128)(2,1)S(1)}, bf16[512,256]{1,0:T(8,128)(2,1)S(1)}, u32[]{:S(2)}, u32[]{:S(2)}) collective-permute-start(bf16[512,256]{1,0:T(8,128)(2,1)S(1)} %collective-permute-done.1.refs_2_), channel_id=1, source_target_pairs={{0,16},{1,115},{16,32},{17,1},{32,48},{33,17},{48,64},{49,33},{64,... | collective-permute-start | bytes 786440 | tf_op jit(solution)/shard_map/ppermute | solution.py:24
  60.4 0.7 copy-done
  61.1 5.3 %collective-permute-start.14 = (bf16[512,256]{1,0:T(8,128)(2,1)S(1)}, bf16[512,256]{1,0:T(8,128)(2,1)S(1)}, u32[]{:S(2)}, u32[]{:S(2)}) collective-permute-start(bf16[512,256]{1,0:T(8,128)(2,1)S(1)} %collective-permute-done.12), channel_id=1, source_target_pairs={{0,16},{1,115},{16,32},{17,1},{32,48},{33,17},{48,64},{49,33},{64,... | collective-permute-start | bytes 786440 | tf_op jit(solution)/shard_map/ppermute | solution.py:24
  66.4 2.6 %collective-permute-start.3 = (bf16[512,256]{1,0:T(8,128)(2,1)S(1)}, bf16[512,256]{1,0:T(8,128)(2,1)S(1)}, u32[]{:S(2)}, u32[]{:S(2)}) collective-permute-start(bf16[512,256]{1,0:T(8,128)(2,1)S(1)} %collective-permute-done.2.refs_3_), channel_id=1, source_target_pairs={{0,16},{1,115},{16,32},{17,1},{32,48},{33,17},{48,64},{49,33},{64,... | collective-permute-start | bytes 786440 | tf_op jit(solution)/shard_map/ppermute | solution.py:24
  69.0 0.7 copy-done.3
  69.7 1.8 collective-permute-done.14
  71.5 2.3 %collective-permute-start.15 = (bf16[512,256]{1,0:T(8,128)(2,1)S(1)}, bf16[512,256]{1,0:T(8,128)(2,1)S(1)}, u32[]{:S(2)}, u32[]{:S(2)}) collective-permute-start(bf16[512,256]{1,0:T(8,128)(2,1)S(1)} %collective-permute-done.14), channel_id=1, source_target_pairs={{0,16},{1,115},{16,32},{17,1},{32,48},{33,17},{48,64},{49,33},{64,... | collective-permute-start | bytes 786440 | tf_op jit(solution)/shard_map/ppermute | solution.py:24
  73.9 0.9 collective-permute-done.3.refs_4_
  74.8 2.2 %collective-permute-start.4 = (bf16[512,256]{1,0:T(8,128)(2,1)S(1)}, bf16[512,256]{1,0:T(8,128)(2,1)}, u32[]{:S(2)}, u32[]{:S(2)}) collective-permute-start(bf16[512,256]{1,0:T(8,128)(2,1)S(1)} %collective-permute-done.3.refs_4_), channel_id=1, source_target_pairs={{0,16},{1,115},{16,32},{17,1},{32,48},{33,17},{48,64},{49,33},{64,... | collective-permute-start | bytes 786440 | tf_op jit(solution)/shard_map/ppermute | solution.py:24
  77.0 9.6 %collective-permute-start.21 = (bf16[4,4,256,128]{3,2,1,0:T(8,128)(2,1)S(1)}, bf16[4,4,256,128]{3,2,1,0:T(8,128)(2,1)S(1)}, u32[]{:S(2)}, u32[]{:S(2)}) collective-permute-start(bf16[4,4,256,128]{3,2,1,0:T(8,128)(2,1)S(1)} %all-to-all-done.refs_11_), channel_id=1, source_target_pairs={{0,1},{1,0},{2,3},{3,2},{4,5},{5,4},{6,7},{7,6},{8,9},{9,8},{10,11... | collective-permute-start | bytes 3145736 | tf_op jit(solution)/shard_map/ppermute | solution.py:85
  86.7 1.9 collective-permute-start.16
  88.6 1.2 pad_maximum_fusion
  89.8 3.6 %collective-permute-start.13 = (bf16[4,512,256]{2,1,0:T(8,128)(2,1)S(1)}, bf16[4,512,256]{2,1,0:T(8,128)(2,1)S(1)}, u32[]{:S(2)}, u32[]{:S(2)}) collective-permute-start(bf16[4,512,256]{2,1,0:T(8,128)(2,1)S(1)} %pad_maximum_fusion), channel_id=1, source_target_pairs={{0,1},{1,0},{2,3},{3,2},{4,5},{5,4},{6,7},{7,6},{8,9},{9,8},{10,11... | collective-permute-start | bytes 3145736 | tf_op jit(solution)/shard_map/ppermute | solution.py:85
  93.4 2.3 %collective-permute-start.5 = (bf16[512,256]{1,0:T(8,128)(2,1)}, bf16[512,256]{1,0:T(8,128)(2,1)S(1)}, u32[]{:S(2)}, u32[]{:S(2)}) collective-permute-start(bf16[512,256]{1,0:T(8,128)(2,1)} %collective-permute-done.4.refs_5_), channel_id=1, source_target_pairs={{0,16},{1,115},{16,32},{17,1},{32,48},{33,17},{48,64},{49,33},{64,... | collective-permute-start | bytes 786440 | tf_op jit(solution)/shard_map/ppermute | solution.py:24
  95.8 3.6 %collective-permute-start.17 = (bf16[3,512,256]{2,1,0:T(8,128)(2,1)S(1)}, bf16[3,512,256]{2,1,0:T(8,128)(2,1)S(1)}, u32[]{:S(2)}, u32[]{:S(2)}) collective-permute-start(bf16[3,512,256]{2,1,0:T(8,128)(2,1)S(1)} %pad_maximum_fusion.1), channel_id=1, source_target_pairs={{0,1},{1,0},{2,3},{3,2},{4,5},{5,4},{6,7},{7,6},{8,9},{9,8},{10,11... | collective-permute-start | bytes 2359304 | tf_op jit(solution)/shard_map/ppermute | solution.py:85
  99.4 2.7 %collective-permute-done.5.refs_6_ = bf16[512,256]{1,0:T(8,128)(2,1)S(1)} collective-permute-done((bf16[512,256]{1,0:T(8,128)(2,1)}, bf16[512,256]{1,0:T(8,128)(2,1)S(1)}, u32[]{:S(2)}, u32[]{:S(2)}) %collective-permute-start.5) | collective-permute-done | bytes 262176 | tf_op jit(solution)/shard_map/ppermute | solution.py:24
  102.1 1.9 collective-permute-start.6
  104.0 6.4 %collective-permute-done.6.refs_7_ = bf16[512,256]{1,0:T(8,128)(2,1)S(1)} collective-permute-done((bf16[512,256]{1,0:T(8,128)(2,1)S(1)}, bf16[512,256]{1,0:T(8,128)(2,1)S(1)}, u32[]{:S(2)}, u32[]{:S(2)}) %collective-permute-start.6) | collective-permute-done | bytes 262176 | tf_op jit(solution)/shard_map/ppermute | solution.py:24
  110.4 1.9 collective-permute-start.7
  112.3 6.4 %collective-permute-done.7.refs_8_ = bf16[512,256]{1,0:T(8,128)(2,1)S(1)} collective-permute-done((bf16[512,256]{1,0:T(8,128)(2,1)S(1)}, bf16[512,256]{1,0:T(8,128)(2,1)S(1)}, u32[]{:S(2)}, u32[]{:S(2)}) %collective-permute-start.7) | collective-permute-done | bytes 262176 | tf_op jit(solution)/shard_map/ppermute | solution.py:24
  118.7 5.0 %shard_map.28 = bf16[4,4,256,128]{3,2,1,0:T(8,128)(2,1)} custom-call(bf16[512,256]{1,0:T(8,128)(2,1)S(1)} %convert_element_type.27.refs_0_, bf16[512,256]{1,0:T(8,128)(2,1)S(1)} %collective-permute-done.refs_1_, bf16[512,256]{1,0:T(8,128)(2,1)S(1)} %copy-done.1, bf16[512,256]{1,0:T(8,128)(2,1)S(1)} %copy-done.4, bf16[512,256]{1,0:T(8,128)(2,1)S(1)} %copy-done.7, ...), custom_call_target="tpu_custom_call" | custom-call | flops 2147483648 | bytes 7340032 | tf_op jit(solution)/shard_map/pallas_call | solution.py:64
  123.7 6.3 %all-to-all-start.1 = ((bf16[16,256,128]{2,1,0:T(8,128)(2,1)}), bf16[16,256,128]{2,1,0:T(8,128)(2,1)S(1)}, u32[]{:S(2)}, u32[]{:S(2)}) async-start(bf16[16,256,128]{2,1,0:T(8,128)(2,1)} %bitcast.10), calls=%async_computation.1 | async-start | bytes 2097152 | tf_op jit(solution)/shard_map/all_to_all | solution.py:134
  130.1 15.0 %all-to-all-done.1 = bf16[16,256,128]{2,1,0:T(8,128)(2,1)S(1)} async-done(((bf16[16,256,128]{2,1,0:T(8,128)(2,1)}), bf16[16,256,128]{2,1,0:T(8,128)(2,1)S(1)}, u32[]{:S(2)}, u32[]{:S(2)}) %all-to-all-start.1) | async-done | bytes 1048608 | tf_op jit(solution)/shard_map/all_to_all | solution.py:134
  145.7 18.6 %all_to_all.20 = bf16[16,256,128]{2,1,0:T(8,128)(2,1)S(1)} all-to-all(bf16[16,256,128]{2,1,0:T(8,128)(2,1)S(1)} %bitcast.21), channel_id=1, replica_groups=mesh['x'=4,'zl'=8,'y'=4,'zh'=2,'c'=2] {'x','y'}, dimensions={0} | all-to-all | bytes 2097152 | tf_op jit(solution)/shard_map/all_to_all | solution.py:139
  164.4 5.3 %collective-permute-start.22 = (bf16[4,4,256,128]{3,2,1,0:T(8,128)(2,1)S(1)}, bf16[4,4,256,128]{3,2,1,0:T(8,128)(2,1)S(1)}, u32[]{:S(2)}, u32[]{:S(2)}) collective-permute-start(bf16[4,4,256,128]{3,2,1,0:T(8,128)(2,1)S(1)} %bitcast.19), channel_id=1, source_target_pairs={{0,1},{1,0},{2,3},{3,2},{4,5},{5,4},{6,7},{7,6},{8,9},{9,8},{10,11... | collective-permute-start | bytes 3145736 | tf_op jit(solution)/shard_map/ppermute | solution.py:85
  169.7 2.3 %collective-permute-done.22.refs_12_ = bf16[4,4,256,128]{3,2,1,0:T(8,128)(2,1)S(1)} collective-permute-done((bf16[4,4,256,128]{3,2,1,0:T(8,128)(2,1)S(1)}, bf16[4,4,256,128]{3,2,1,0:T(8,128)(2,1)S(1)}, u32[]{:S(2)}, u32[]{:S(2)}) %collective-permute-start.22) | collective-permute-done | bytes 1048608 | tf_op jit(solution)/shard_map/ppermute | solution.py:85
  172.0 4.3 %shard_map.29 = bf16[4,4,256,128]{3,2,1,0:T(8,128)(2,1)S(1)} custom-call(bf16[512,256]{1,0:T(8,128)(2,1)S(1)} %convert_element_type.27.refs_0_, bf16[512,256]{1,0:T(8,128)(2,1)S(1)} %collective-permute-done.refs_1_, bf16[512,256]{1,0:T(8,128)(2,1)S(1)} %copy-done.2, bf16[512,256]{1,0:T(8,128)(2,1)S(1)} %copy-done.5, bf16[512,256]{1,0:T(8,128)(2,1)S(1)} %copy-done.8, ...), custom_call_target="tpu_custom_call" | custom-call | flops 2147483648 | bytes 7340032 | tf_op jit(solution)/shard_map/pallas_call | solution.py:64
  176.2 17.3 %all_to_all.21 = bf16[4,4,256,128]{3,2,1,0:T(8,128)(2,1)S(1)} all-to-all(bf16[4,4,256,128]{3,2,1,0:T(8,128)(2,1)S(1)} %shard_map.29), channel_id=1, replica_groups=mesh['x'=4,'zl'=8,'y'=4,'zh'=2,'c'=2] {'x'}, dimensions={0} | all-to-all | bytes 2097152 | tf_op jit(solution)/shard_map/all_to_all | solution.py:141
  193.7 6.2 %collective-permute-start.23 = (bf16[512,128]{1,0:T(8,128)(2,1)S(1)}, bf16[512,128]{1,0:T(8,128)(2,1)S(1)}, u32[]{:S(2)}, u32[]{:S(2)}) collective-permute-start(bf16[512,128]{1,0:T(8,128)(2,1)S(1)} %bitcast.32), channel_id=1, source_target_pairs={{0,66},{16,82},{32,98},{48,114},{64,0},{80,16},{96,32},{112,48},{2... | collective-permute-start | bytes 393224 | tf_op jit(solution)/shard_map/ppermute | solution.py:18
  199.9 4.3 %collective-permute-start.24 = (bf16[512,128]{1,0:T(8,128)(2,1)S(1)}, bf16[512,128]{1,0:T(8,128)(2,1)S(1)}, u32[]{:S(2)}, u32[]{:S(2)}) collective-permute-start(bf16[512,128]{1,0:T(8,128)(2,1)S(1)} %bitcast.31), channel_id=1, source_target_pairs={{0,64},{16,80},{32,96},{48,112},{64,2},{80,18},{96,34},{112,50},{2... | collective-permute-start | bytes 393224 | tf_op jit(solution)/shard_map/ppermute | solution.py:18
  204.2 3.8 %collective-permute-done.23 = bf16[512,128]{1,0:T(8,128)(2,1)S(1)} collective-permute-done((bf16[512,128]{1,0:T(8,128)(2,1)S(1)}, bf16[512,128]{1,0:T(8,128)(2,1)S(1)}, u32[]{:S(2)}, u32[]{:S(2)}) %collective-permute-start.23) | collective-permute-done | bytes 131104 | tf_op jit(solution)/shard_map/ppermute | solution.py:18
  208.1 5.6 %collective-permute-done.24 = bf16[512,128]{1,0:T(8,128)(2,1)S(1)} collective-permute-done((bf16[512,128]{1,0:T(8,128)(2,1)S(1)}, bf16[512,128]{1,0:T(8,128)(2,1)S(1)}, u32[]{:S(2)}, u32[]{:S(2)}) %collective-permute-start.24) | collective-permute-done | bytes 131104 | tf_op jit(solution)/shard_map/ppermute | solution.py:18
  213.7 0.9 convert_add_fusion
  (65 shorter events, 1.8 us)
Async XLA Ops:
  0.0 3.7 %copy-start.16 = (f32[512,256]{1,0:T(8,128)S(1)}, f32[512,256]{1,0:T(8,128)}, u32[]{:S(2)}) copy-start(f32[512,256]{1,0:T(8,128)} %param.3) | copy-start | bytes 1572868
  1.1 3.7 %collective-permute-start.8 = (bf16[512,256]{1,0:T(8,128)(2,1)S(1)}, bf16[512,256]{1,0:T(8,128)(2,1)S(1)}, u32[]{:S(2)}, u32[]{:S(2)}) collective-permute-start(bf16[512,256]{1,0:T(8,128)(2,1)S(1)} %convert_element_type.27.refs_0_), channel_id=1, source_target_pairs={{0,1},{1,0},{2,3},{3,2},{4,5},{5,4},{6,7},{7,6},{8,9},{9,8},{10,11... | collective-permute-start | bytes 786440 | tf_op jit(solution)/shard_map/ppermute | solution.py:85
  4.9 17.0 %collective-permute-start.9 = (bf16[512,256]{1,0:T(8,128)(2,1)S(1)}, bf16[512,256]{1,0:T(8,128)(2,1)S(1)}, u32[]{:S(2)}, u32[]{:S(2)}) collective-permute-start(bf16[512,256]{1,0:T(8,128)(2,1)S(1)} %collective-permute-done.8), channel_id=1, source_target_pairs={{0,16},{1,115},{16,32},{17,1},{32,48},{33,17},{48,64},{49,33},{64,... | collective-permute-start | bytes 786440 | tf_op jit(solution)/shard_map/ppermute | solution.py:24
  6.8 20.9 %collective-permute-start.18 = (bf16[512,128]{1,0:T(8,128)(2,1)S(1)}, bf16[512,128]{1,0:T(8,128)(2,1)S(1)}, u32[]{:S(2)}, u32[]{:S(2)}) collective-permute-start(bf16[512,128]{1,0:T(8,128)(2,1)S(1)} %get-tuple-element.11), channel_id=1, source_target_pairs={{0,64},{16,80},{32,96},{48,112},{64,2},{80,18},{96,34},{112,50},{2... | collective-permute-start | bytes 393224 | tf_op jit(solution)/shard_map/ppermute | solution.py:18
  15.6 12.1 %collective-permute-start.19 = (bf16[512,128]{1,0:T(8,128)(2,1)S(1)}, bf16[512,128]{1,0:T(8,128)(2,1)S(1)}, u32[]{:S(2)}, u32[]{:S(2)}) collective-permute-start(bf16[512,128]{1,0:T(8,128)(2,1)S(1)} %get-tuple-element.12), channel_id=1, source_target_pairs={{0,66},{16,82},{32,98},{48,114},{64,0},{80,16},{96,32},{112,48},{2... | collective-permute-start | bytes 393224 | tf_op jit(solution)/shard_map/ppermute | solution.py:18
  19.2 21.7 %collective-permute-start = (bf16[512,256]{1,0:T(8,128)(2,1)S(1)}, bf16[512,256]{1,0:T(8,128)(2,1)S(1)}, u32[]{:S(2)}, u32[]{:S(2)}) collective-permute-start(bf16[512,256]{1,0:T(8,128)(2,1)S(1)} %convert_element_type.27.refs_0_), channel_id=1, source_target_pairs={{0,16},{1,115},{16,32},{17,1},{32,48},{33,17},{48,64},{49,33},{64,... | collective-permute-start | bytes 786440 | tf_op jit(solution)/shard_map/ppermute | solution.py:24
  21.9 17.1 %collective-permute-start.10 = (bf16[512,256]{1,0:T(8,128)(2,1)S(1)}, bf16[512,256]{1,0:T(8,128)(2,1)S(1)}, u32[]{:S(2)}, u32[]{:S(2)}) collective-permute-start(bf16[512,256]{1,0:T(8,128)(2,1)S(1)} %collective-permute-done.9), channel_id=1, source_target_pairs={{0,16},{1,115},{16,32},{17,1},{32,48},{33,17},{48,64},{49,33},{64,... | collective-permute-start | bytes 786440 | tf_op jit(solution)/shard_map/ppermute | solution.py:24
  27.8 15.3 %collective-permute-start.20 = (bf16[4,256,128]{2,1,0:T(8,128)(2,1)S(1)}, bf16[4,256,128]{2,1,0:T(8,128)(2,1)S(1)}, u32[]{:S(2)}, u32[]{:S(2)}) collective-permute-start(bf16[4,256,128]{2,1,0:T(8,128)(2,1)S(1)} %bitcast.23), channel_id=1, source_target_pairs={{0,0},{4,128},{8,256},{12,384},{128,4},{132,132},{136,260},{140,38... | collective-permute-start | bytes 786440 | tf_op jit(solution)/shard_map/ppermute | solution.py:130
  39.0 9.5 %collective-permute-start.11 = (bf16[512,256]{1,0:T(8,128)(2,1)S(1)}, bf16[512,256]{1,0:T(8,128)(2,1)S(1)}, u32[]{:S(2)}, u32[]{:S(2)}) collective-permute-start(bf16[512,256]{1,0:T(8,128)(2,1)S(1)} %collective-permute-done.10), channel_id=1, source_target_pairs={{0,16},{1,115},{16,32},{17,1},{32,48},{33,17},{48,64},{49,33},{64,... | collective-permute-start | bytes 786440 | tf_op jit(solution)/shard_map/ppermute | solution.py:24
  40.9 10.9 %collective-permute-start.1 = (bf16[512,256]{1,0:T(8,128)(2,1)S(1)}, bf16[512,256]{1,0:T(8,128)(2,1)S(1)}, u32[]{:S(2)}, u32[]{:S(2)}) collective-permute-start(bf16[512,256]{1,0:T(8,128)(2,1)S(1)} %collective-permute-done.refs_1_), channel_id=1, source_target_pairs={{0,16},{1,115},{16,32},{17,1},{32,48},{33,17},{48,64},{49,33},{64,... | collective-permute-start | bytes 786440 | tf_op jit(solution)/shard_map/ppermute | solution.py:24
  44.3 32.7 %all-to-all-start = ((bf16[4,4,256,128]{3,2,1,0:T(8,128)(2,1)}), bf16[4,4,256,128]{3,2,1,0:T(8,128)(2,1)S(1)}, u32[]{:S(2)}, u32[]{:S(2)}) async-start(bf16[4,4,256,128]{3,2,1,0:T(8,128)(2,1)} %stack.55), calls=%async_computation | async-start | bytes 2097152 | tf_op jit(solution)/shard_map/all_to_all | solution.py:131
  48.5 11.9 %copy-start.17 = (bf16[512,256]{1,0:T(8,128)(2,1)}, bf16[512,256]{1,0:T(8,128)(2,1)S(1)}, u32[]{:S(2)}) copy-start(bf16[512,256]{1,0:T(8,128)(2,1)S(1)} %collective-permute-done.11) | copy-start | bytes 786436
  48.5 12.6 %collective-permute-start.12 = (bf16[512,256]{1,0:T(8,128)(2,1)S(1)}, bf16[512,256]{1,0:T(8,128)(2,1)S(1)}, u32[]{:S(2)}, u32[]{:S(2)}) collective-permute-start(bf16[512,256]{1,0:T(8,128)(2,1)S(1)} %collective-permute-done.11), channel_id=1, source_target_pairs={{0,16},{1,115},{16,32},{17,1},{32,48},{33,17},{48,64},{49,33},{64,... | collective-permute-start | bytes 786440 | tf_op jit(solution)/shard_map/ppermute | solution.py:24
  51.9 14.6 %collective-permute-start.2 = (bf16[512,256]{1,0:T(8,128)(2,1)S(1)}, bf16[512,256]{1,0:T(8,128)(2,1)S(1)}, u32[]{:S(2)}, u32[]{:S(2)}) collective-permute-start(bf16[512,256]{1,0:T(8,128)(2,1)S(1)} %collective-permute-done.1.refs_2_), channel_id=1, source_target_pairs={{0,16},{1,115},{16,32},{17,1},{32,48},{33,17},{48,64},{49,33},{64,... | collective-permute-start | bytes 786440 | tf_op jit(solution)/shard_map/ppermute | solution.py:24
  60.4 0.7 copy-start
  61.1 7.9 %copy-start.18 = (bf16[512,256]{1,0:T(8,128)(2,1)}, bf16[512,256]{1,0:T(8,128)(2,1)S(1)}, u32[]{:S(2)}) copy-start(bf16[512,256]{1,0:T(8,128)(2,1)S(1)} %collective-permute-done.12) | copy-start | bytes 786436
  61.1 10.4 %collective-permute-start.14 = (bf16[512,256]{1,0:T(8,128)(2,1)S(1)}, bf16[512,256]{1,0:T(8,128)(2,1)S(1)}, u32[]{:S(2)}, u32[]{:S(2)}) collective-permute-start(bf16[512,256]{1,0:T(8,128)(2,1)S(1)} %collective-permute-done.12), channel_id=1, source_target_pairs={{0,16},{1,115},{16,32},{17,1},{32,48},{33,17},{48,64},{49,33},{64,... | collective-permute-start | bytes 786440 | tf_op jit(solution)/shard_map/ppermute | solution.py:24
  66.4 8.3 %collective-permute-start.3 = (bf16[512,256]{1,0:T(8,128)(2,1)S(1)}, bf16[512,256]{1,0:T(8,128)(2,1)S(1)}, u32[]{:S(2)}, u32[]{:S(2)}) collective-permute-start(bf16[512,256]{1,0:T(8,128)(2,1)S(1)} %collective-permute-done.2.refs_3_), channel_id=1, source_target_pairs={{0,16},{1,115},{16,32},{17,1},{32,48},{33,17},{48,64},{49,33},{64,... | collective-permute-start | bytes 786440 | tf_op jit(solution)/shard_map/ppermute | solution.py:24
  69.0 0.7 copy-start.3
  71.5 15.2 %collective-permute-start.15 = (bf16[512,256]{1,0:T(8,128)(2,1)S(1)}, bf16[512,256]{1,0:T(8,128)(2,1)S(1)}, u32[]{:S(2)}, u32[]{:S(2)}) collective-permute-start(bf16[512,256]{1,0:T(8,128)(2,1)S(1)} %collective-permute-done.14), channel_id=1, source_target_pairs={{0,16},{1,115},{16,32},{17,1},{32,48},{33,17},{48,64},{49,33},{64,... | collective-permute-start | bytes 786440 | tf_op jit(solution)/shard_map/ppermute | solution.py:24
  74.8 15.0 %copy-start.6 = (bf16[512,256]{1,0:T(8,128)(2,1)}, bf16[512,256]{1,0:T(8,128)(2,1)S(1)}, u32[]{:S(2)}) copy-start(bf16[512,256]{1,0:T(8,128)(2,1)S(1)} %collective-permute-done.3.refs_4_) | copy-start | bytes 786436
  74.8 18.6 %collective-permute-start.4 = (bf16[512,256]{1,0:T(8,128)(2,1)S(1)}, bf16[512,256]{1,0:T(8,128)(2,1)}, u32[]{:S(2)}, u32[]{:S(2)}) collective-permute-start(bf16[512,256]{1,0:T(8,128)(2,1)S(1)} %collective-permute-done.3.refs_4_), channel_id=1, source_target_pairs={{0,16},{1,115},{16,32},{17,1},{32,48},{33,17},{48,64},{49,33},{64,... | collective-permute-start | bytes 786440 | tf_op jit(solution)/shard_map/ppermute | solution.py:24
  77.0 41.7 %collective-permute-start.21 = (bf16[4,4,256,128]{3,2,1,0:T(8,128)(2,1)S(1)}, bf16[4,4,256,128]{3,2,1,0:T(8,128)(2,1)S(1)}, u32[]{:S(2)}, u32[]{:S(2)}) collective-permute-start(bf16[4,4,256,128]{3,2,1,0:T(8,128)(2,1)S(1)} %all-to-all-done.refs_11_), channel_id=1, source_target_pairs={{0,1},{1,0},{2,3},{3,2},{4,5},{5,4},{6,7},{7,6},{8,9},{9,8},{10,11... | collective-permute-start | bytes 3145736 | tf_op jit(solution)/shard_map/ppermute | solution.py:85
  86.7 9.0 %collective-permute-start.16 = (bf16[512,256]{1,0:T(8,128)(2,1)S(1)}, bf16[512,256]{1,0:T(8,128)(2,1)S(1)}, u32[]{:S(2)}, u32[]{:S(2)}) collective-permute-start(bf16[512,256]{1,0:T(8,128)(2,1)S(1)} %collective-permute-done.15), channel_id=1, source_target_pairs={{0,16},{1,115},{16,32},{17,1},{32,48},{33,17},{48,64},{49,33},{64,... | collective-permute-start | bytes 786440 | tf_op jit(solution)/shard_map/ppermute | solution.py:24
  89.8 28.9 %copy-start.1 = (bf16[512,256]{1,0:T(8,128)(2,1)S(1)}, bf16[512,256]{1,0:T(8,128)(2,1)}, u32[]{:S(2)}) copy-start(bf16[512,256]{1,0:T(8,128)(2,1)} %copy-done) | copy-start | bytes 786436
  89.8 28.9 %copy-start.4 = (bf16[512,256]{1,0:T(8,128)(2,1)S(1)}, bf16[512,256]{1,0:T(8,128)(2,1)}, u32[]{:S(2)}) copy-start(bf16[512,256]{1,0:T(8,128)(2,1)} %copy-done.3) | copy-start | bytes 786436
  89.8 28.9 %collective-permute-start.13 = (bf16[4,512,256]{2,1,0:T(8,128)(2,1)S(1)}, bf16[4,512,256]{2,1,0:T(8,128)(2,1)S(1)}, u32[]{:S(2)}, u32[]{:S(2)}) collective-permute-start(bf16[4,512,256]{2,1,0:T(8,128)(2,1)S(1)} %pad_maximum_fusion), channel_id=1, source_target_pairs={{0,1},{1,0},{2,3},{3,2},{4,5},{5,4},{6,7},{7,6},{8,9},{9,8},{10,11... | collective-permute-start | bytes 3145736 | tf_op jit(solution)/shard_map/ppermute | solution.py:85
  93.4 25.4 %copy-start.7 = (bf16[512,256]{1,0:T(8,128)(2,1)S(1)}, bf16[512,256]{1,0:T(8,128)(2,1)}, u32[]{:S(2)}) copy-start(bf16[512,256]{1,0:T(8,128)(2,1)} %copy-done.6) | copy-start | bytes 786436
  93.4 8.7 %collective-permute-start.5 = (bf16[512,256]{1,0:T(8,128)(2,1)}, bf16[512,256]{1,0:T(8,128)(2,1)S(1)}, u32[]{:S(2)}, u32[]{:S(2)}) collective-permute-start(bf16[512,256]{1,0:T(8,128)(2,1)} %collective-permute-done.4.refs_5_), channel_id=1, source_target_pairs={{0,16},{1,115},{16,32},{17,1},{32,48},{33,17},{48,64},{49,33},{64,... | collective-permute-start | bytes 786440 | tf_op jit(solution)/shard_map/ppermute | solution.py:24
  95.8 22.9 %collective-permute-start.17 = (bf16[3,512,256]{2,1,0:T(8,128)(2,1)S(1)}, bf16[3,512,256]{2,1,0:T(8,128)(2,1)S(1)}, u32[]{:S(2)}, u32[]{:S(2)}) collective-permute-start(bf16[3,512,256]{2,1,0:T(8,128)(2,1)S(1)} %pad_maximum_fusion.1), channel_id=1, source_target_pairs={{0,1},{1,0},{2,3},{3,2},{4,5},{5,4},{6,7},{7,6},{8,9},{9,8},{10,11... | collective-permute-start | bytes 2359304 | tf_op jit(solution)/shard_map/ppermute | solution.py:85
  102.1 21.6 %copy-start.9 = (bf16[512,256]{1,0:T(8,128)(2,1)}, bf16[512,256]{1,0:T(8,128)(2,1)S(1)}, u32[]{:S(2)}) copy-start(bf16[512,256]{1,0:T(8,128)(2,1)S(1)} %collective-permute-done.5.refs_6_) | copy-start | bytes 786436
  102.1 8.3 %collective-permute-start.6 = (bf16[512,256]{1,0:T(8,128)(2,1)S(1)}, bf16[512,256]{1,0:T(8,128)(2,1)S(1)}, u32[]{:S(2)}, u32[]{:S(2)}) collective-permute-start(bf16[512,256]{1,0:T(8,128)(2,1)S(1)} %collective-permute-done.5.refs_6_), channel_id=1, source_target_pairs={{0,16},{1,115},{16,32},{17,1},{32,48},{33,17},{48,64},{49,33},{64,... | collective-permute-start | bytes 786440 | tf_op jit(solution)/shard_map/ppermute | solution.py:24
  110.4 13.3 %copy-start.11 = (bf16[512,256]{1,0:T(8,128)(2,1)}, bf16[512,256]{1,0:T(8,128)(2,1)S(1)}, u32[]{:S(2)}) copy-start(bf16[512,256]{1,0:T(8,128)(2,1)S(1)} %collective-permute-done.6.refs_7_) | copy-start | bytes 786436
  110.4 8.3 %collective-permute-start.7 = (bf16[512,256]{1,0:T(8,128)(2,1)S(1)}, bf16[512,256]{1,0:T(8,128)(2,1)S(1)}, u32[]{:S(2)}, u32[]{:S(2)}) collective-permute-start(bf16[512,256]{1,0:T(8,128)(2,1)S(1)} %collective-permute-done.6.refs_7_), channel_id=1, source_target_pairs={{0,16},{1,115},{16,32},{17,1},{32,48},{33,17},{48,64},{49,33},{64,... | collective-permute-start | bytes 786440 | tf_op jit(solution)/shard_map/ppermute | solution.py:24
  118.7 5.0 %copy-start.13 = (bf16[512,256]{1,0:T(8,128)(2,1)}, bf16[512,256]{1,0:T(8,128)(2,1)S(1)}, u32[]{:S(2)}) copy-start(bf16[512,256]{1,0:T(8,128)(2,1)S(1)} %collective-permute-done.7.refs_8_) | copy-start | bytes 786436
  123.7 21.4 %all-to-all-start.1 = ((bf16[16,256,128]{2,1,0:T(8,128)(2,1)}), bf16[16,256,128]{2,1,0:T(8,128)(2,1)S(1)}, u32[]{:S(2)}, u32[]{:S(2)}) async-start(bf16[16,256,128]{2,1,0:T(8,128)(2,1)} %bitcast.10), calls=%async_computation.1 | async-start | bytes 2097152 | tf_op jit(solution)/shard_map/all_to_all | solution.py:134
  145.7 26.3 %copy-start.2 = (bf16[512,256]{1,0:T(8,128)(2,1)S(1)}, bf16[512,256]{1,0:T(8,128)(2,1)}, u32[]{:S(2)}) copy-start(bf16[512,256]{1,0:T(8,128)(2,1)} %copy-done) | copy-start | bytes 786436
  145.7 26.3 %copy-start.5 = (bf16[512,256]{1,0:T(8,128)(2,1)S(1)}, bf16[512,256]{1,0:T(8,128)(2,1)}, u32[]{:S(2)}) copy-start(bf16[512,256]{1,0:T(8,128)(2,1)} %copy-done.3) | copy-start | bytes 786436
  145.7 26.2 %copy-start.8 = (bf16[512,256]{1,0:T(8,128)(2,1)S(1)}, bf16[512,256]{1,0:T(8,128)(2,1)}, u32[]{:S(2)}) copy-start(bf16[512,256]{1,0:T(8,128)(2,1)} %copy-done.6) | copy-start | bytes 786436
  145.7 26.2 %copy-start.10 = (bf16[512,256]{1,0:T(8,128)(2,1)S(1)}, bf16[512,256]{1,0:T(8,128)(2,1)}, u32[]{:S(2)}) copy-start(bf16[512,256]{1,0:T(8,128)(2,1)} %copy-done.9) | copy-start | bytes 786436
  145.7 26.2 %copy-start.12 = (bf16[512,256]{1,0:T(8,128)(2,1)S(1)}, bf16[512,256]{1,0:T(8,128)(2,1)}, u32[]{:S(2)}) copy-start(bf16[512,256]{1,0:T(8,128)(2,1)} %copy-done.11) | copy-start | bytes 786436
  145.7 26.2 %copy-start.14 = (bf16[512,256]{1,0:T(8,128)(2,1)S(1)}, bf16[512,256]{1,0:T(8,128)(2,1)}, u32[]{:S(2)}) copy-start(bf16[512,256]{1,0:T(8,128)(2,1)} %copy-done.13) | copy-start | bytes 786436
  164.4 7.6 %collective-permute-start.22 = (bf16[4,4,256,128]{3,2,1,0:T(8,128)(2,1)S(1)}, bf16[4,4,256,128]{3,2,1,0:T(8,128)(2,1)S(1)}, u32[]{:S(2)}, u32[]{:S(2)}) collective-permute-start(bf16[4,4,256,128]{3,2,1,0:T(8,128)(2,1)S(1)} %bitcast.19), channel_id=1, source_target_pairs={{0,1},{1,0},{2,3},{3,2},{4,5},{5,4},{6,7},{7,6},{8,9},{9,8},{10,11... | collective-permute-start | bytes 3145736 | tf_op jit(solution)/shard_map/ppermute | solution.py:85
  193.5 20.2 %copy-start.15 = (f32[512,256]{1,0:T(8,128)S(1)}, f32[512,256]{1,0:T(8,128)}, u32[]{:S(2)}) copy-start(f32[512,256]{1,0:T(8,128)} %param.2) | copy-start | bytes 1572868
  193.7 14.3 %collective-permute-start.23 = (bf16[512,128]{1,0:T(8,128)(2,1)S(1)}, bf16[512,128]{1,0:T(8,128)(2,1)S(1)}, u32[]{:S(2)}, u32[]{:S(2)}) collective-permute-start(bf16[512,128]{1,0:T(8,128)(2,1)S(1)} %bitcast.32), channel_id=1, source_target_pairs={{0,66},{16,82},{32,98},{48,114},{64,0},{80,16},{96,32},{112,48},{2... | collective-permute-start | bytes 393224 | tf_op jit(solution)/shard_map/ppermute | solution.py:18
  199.9 13.8 %collective-permute-start.24 = (bf16[512,128]{1,0:T(8,128)(2,1)S(1)}, bf16[512,128]{1,0:T(8,128)(2,1)S(1)}, u32[]{:S(2)}, u32[]{:S(2)}) collective-permute-start(bf16[512,128]{1,0:T(8,128)(2,1)S(1)} %bitcast.31), channel_id=1, source_target_pairs={{0,64},{16,80},{32,96},{48,112},{64,2},{80,18},{96,34},{112,50},{2... | collective-permute-start | bytes 393224 | tf_op jit(solution)/shard_map/ppermute | solution.py:18

commit v4 on v3

--- a/solution.py
+++ b/solution.py
@@ -18,15 +18,19 @@
     return lax.ppermute(block, RING, [(place(z), place((z + step) % 16)) for z in range(16)])
 
 
-def round_z(block):
-    place = lambda z, c: ((z % 8) * 2 + z // 8) * 2 + c
-    pairs = [(place(z, c), place((z + 1 - 2 * c) % 16, c)) for z in range(16) for c in range(2)]
-    return lax.ppermute(block, RING + ("c",), pairs)
+def turn_and_along_z(block, step):
+    place = lambda x, z, y: ((x * 8 + z % 8) * 4 + y) * 2 + z // 8
+    pairs = [
+        (place(x, z, y), place(y, (z + step) % 16, x))
+        for x in range(4)
+        for y in range(4)
+        for z in range(16)
+    ]
+    return lax.ppermute(block, ("x", "zl", "y", "zh"), pairs)
 
 
 def dot_kernel(*refs):
-    own_ref, other_ref, out_ref, left, right, sem = refs[11:]
-    chunks = list(refs[:9]) + [ref.at[n] for ref in refs[9:11] for n in range(ref.shape[0])]
+    chunks, (own_ref, other_ref, out_ref, left, right, sem) = refs[:16], refs[16:]
     groups, _, depth, width = own_ref.shape
     c = lax.axis_index("c")
     step = pl.program_id(0)
@@ -37,7 +41,7 @@
         copies = []
         for n, ref in enumerate(chunks):
             away = -n if n <= 8 else n - 8
-            at = lax.rem(z + away * (1 - 2 * c) + 16, 16)
+            at = lax.rem(z + away + 16, 16)
             copies.append(pltpu.make_async_copy(ref, left.at[at], sem.at[n]))
         for copy in copies:
             copy.start()
@@ -64,7 +68,7 @@
     return pl.pallas_call(
         dot_kernel,
         grid=(steps,),
-        in_specs=[pl.BlockSpec(memory_space=pl.ANY)] * 11 + [whole, whole],
+        in_specs=[pl.BlockSpec(memory_space=pl.ANY)] * 16 + [whole, whole],
         out_specs=pl.BlockSpec((groups, 1, depth, width), lambda s: (0, s, 0, 0)),
         out_shape=jax.ShapeDtypeStruct(own.shape, jnp.bfloat16),
         scratch_shapes=[
@@ -107,29 +111,42 @@
     z_half = z_iter.astype(jnp.bfloat16)
     y_half = y_iter.astype(jnp.bfloat16)
 
-    mine = [round_z(z_half)]
-    theirs = [round_z(other_core(z_half))]
-    for n in range(1, 8):
-        mine.append(round_z(mine[-1]))
-        if n < 7:
-            theirs.append(round_z(theirs[-1]))
-    z_rows = [z_half] + mine
-    z_rows += [other_core(jnp.stack(theirs[:4])), other_core(jnp.stack(theirs[4:]))]
-
     low = at("zh") == 0
     z = at("zh") * 8 + at("zl")
     middle = (z >= 4) & (z < 12)
     first_col = at("x") * 2048 + (at("zl") ^ 4) * 256 + jnp.where(middle, 0, 128)
     left, right = y_half[:, :128], y_half[:, 128:]
-    up = along_z(jnp.where(low, left, right), 4)
-    down = along_z(jnp.where(low, right, left), -4)
-    y_both = jnp.stack([jnp.where(middle, up, down), jnp.where(middle, down, up)])
-    y_both = y_both.reshape(4, 256, 128)
+    send_up, send_down = jnp.where(low, left, right), jnp.where(low, right, left)
 
-    turn = [(i * 4 + j, j * 4 + i) for i in range(4) for j in range(4)]
-    turned = lax.ppermute(y_both, PLANE, turn)
-    y_own = lax.all_to_all(jnp.stack([turned] * 4), "y", 0, 0, tiled=True)
-    part = dot_right(z_rows, y_own, other_core(y_own))
+    tie = lax.optimization_barrier
+    ups, downs = [along_z(z_half, 1)], [along_z(z_half, -1)]
+    up = along_z(send_up, 2)
+    for n in range(2, 9):
+        if n == 2:
+            up, ups[-1], downs[-1] = tie((up, ups[-1], downs[-1]))
+        if n == 3:
+            up, send_down, ups[-1], downs[-1] = tie((up, send_down, ups[-1], downs[-1]))
+        if n == 4 or n == 5:
+            down, ups[-1], downs[-1] = tie((down, ups[-1], downs[-1]))
+        if n == 7:
+            y_own, ups[-1], downs[-1] = tie((y_own, ups[-1], downs[-1]))
+        ups.append(along_z(ups[-1], 1))
+        if n < 8:
+            downs.append(along_z(downs[-1], -1))
+        if n == 2:
+            up = turn_and_along_z(up, 2)
+        if n == 3:
+            down = along_z(send_down, -2)
+        if n == 4:
+            down = turn_and_along_z(down, -2)
+        if n == 5:
+            y_both = jnp.stack([jnp.where(middle, up, down), jnp.where(middle, down, up)])
+            y_both = y_both.reshape(4, 256, 128)
+            y_own = lax.all_to_all(jnp.stack([y_both] * 4), "y", 0, 0, tiled=True)
+        if n == 7:
+            y_other = other_core(y_own)
+    z_rows = [z_half] + ups + downs
+    part = dot_right(z_rows, y_own, y_other)
 
     part = lax.all_to_all(part.reshape(16, 256, 128), PLANE, 0, 0, tiled=True)
     product = part.reshape(4, 4, 256, 128).astype(jnp.float32).sum(0)

time: 216 us -> 242 us (1.12)
  the two profiles are of different devices: /device:TPU:97 before, /device:TPU:1 now
where the time goes in v4:
time: 242 us; the launch traced here: 241 us
  starting transfers between devices  112 us (46%)
  waiting for transfers between devices  73.8 us (30%)
  blocking collectives  35.9 us (15%)
  Pallas kernels  9.41 us (4%)
  local copies, waits for them, and re-layouts  6.5 us (3%)
  other arithmetic  2.73 us (1%)
    ppermute x19, starting transfers between devices, along_z(): lax.ppermute(block, RING, [(place(z), place((z + step) % 16)) for z in ra...  70.3 us
    ppermute x19, waiting for transfers between devices, along_z(): lax.ppermute(block, RING, [(place(z), place((z + step) % 16)) for z in ra...  45.8 us
    all_to_all x1, blocking collectives, shards(): lax.all_to_all(spread, PLANE, 0, 0, tiled=True).reshape(4, 4, 256, 128)  18.6 us
    all_to_all x1, blocking collectives, shards(): part = lax.all_to_all(part, 'x', 0, 0, tiled=True)  17.3 us
    all_to_all x1, starting transfers between devices, shards(): y_own = lax.all_to_all(jnp.stack([y_both] * 4), 'y', 0, 0, tiled=True)  15.6 us
    ppermute x2, starting transfers between devices, other_core(): return lax.ppermute(block, 'c', SWAP)  15.5 us
    all_to_all x1, waiting for transfers between devices, shards(): part = lax.all_to_all(part.reshape(16, 256, 128), PLANE, 0, 0, tiled=True)  15 us
    ppermute x2, waiting for transfers between devices, turn_and_along_z(): return lax.ppermute(block, ('x', 'zl', 'y', 'zh'), pairs)  10.7 us
  transfers between devices with their start and end apart: 25, of which 13 were waited for; matrix products, arithmetic and copies ran while one was open for 0% of the time, Pallas kernels for 0%

profile of v4, /device:TPU:1, one launch (start us, length us, event | category | flops | bytes accessed | tf_op | source)
XLA Modules:
  0.0 240.8 jit_solution(4129575288172839005)
XLA Ops:
  0.0 1.1 convert_element_type.27.refs_0_
  1.1 12.0 %collective-permute-start.2 = (bf16[512,256]{1,0:T(8,128)(2,1)S(1)}, bf16[512,256]{1,0:T(8,128)(2,1)S(1)}, u32[]{:S(2)}, u32[]{:S(2)}) collective-permute-start(bf16[512,256]{1,0:T(8,128)(2,1)S(1)} %convert_element_type.27.refs_0_), channel_id=1, source_target_pairs={{0,114},{16,0},{32,16},{48,32},{64,48},{80,64},{96,80},{112,96},{2... | collective-permute-start | bytes 786440 | tf_op jit(solution)/shard_map/ppermute | solution.py:18
  13.1 1.9 collective-permute-start.1
  15.1 1.9 collective-permute-start
  17.0 8.8 %collective-permute-done = bf16[512,128]{1,0:T(8,128)(2,1)S(1)} collective-permute-done((bf16[512,128]{1,0:T(8,128)(2,1)S(1)}, bf16[512,128]{1,0:T(8,128)(2,1)S(1)}, u32[]{:S(2)}, u32[]{:S(2)}) %collective-permute-start) | collective-permute-done | bytes 131104 | tf_op jit(solution)/shard_map/ppermute | solution.py:18
  25.8 5.7 %collective-permute-start.4 = (bf16[512,256]{1,0:T(8,128)(2,1)S(1)}, bf16[512,256]{1,0:T(8,128)(2,1)S(1)}, u32[]{:S(2)}, u32[]{:S(2)}) collective-permute-start(bf16[512,256]{1,0:T(8,128)(2,1)S(1)} %collective-permute-done.1.refs_1_), channel_id=1, source_target_pairs={{0,16},{16,32},{32,48},{48,64},{64,80},{80,96},{96,112},{112,2},{2... | collective-permute-start | bytes 786440 | tf_op jit(solution)/shard_map/ppermute | solution.py:18
  31.5 1.9 collective-permute-start.5
  33.4 3.1 %collective-permute-start.3 = (bf16[512,128]{1,0:T(8,128)(2,1)S(1)}, bf16[512,128]{1,0:T(8,128)(2,1)S(1)}, u32[]{:S(2)}, u32[]{:S(2)}) collective-permute-start(bf16[512,128]{1,0:T(8,128)(2,1)S(1)} %collective-permute-done), channel_id=1, source_target_pairs={{0,32},{16,48},{32,64},{48,80},{64,96},{80,112},{96,2},{112,18},{2... | collective-permute-start | bytes 393224 | tf_op jit(solution)/shard_map/ppermute | solution.py:29
  36.5 6.0 %collective-permute-done.3 = bf16[512,128]{1,0:T(8,128)(2,1)S(1)} collective-permute-done((bf16[512,128]{1,0:T(8,128)(2,1)S(1)}, bf16[512,128]{1,0:T(8,128)(2,1)S(1)}, u32[]{:S(2)}, u32[]{:S(2)}) %collective-permute-start.3) | collective-permute-done | bytes 131104 | tf_op jit(solution)/shard_map/ppermute | solution.py:29
  42.5 3.4 %collective-permute-start.7 = (bf16[512,256]{1,0:T(8,128)(2,1)S(1)}, bf16[512,256]{1,0:T(8,128)(2,1)S(1)}, u32[]{:S(2)}, u32[]{:S(2)}) collective-permute-start(bf16[512,256]{1,0:T(8,128)(2,1)S(1)} %collective-permute-done.4.refs_2_), channel_id=1, source_target_pairs={{0,16},{16,32},{32,48},{48,64},{64,80},{80,96},{96,112},{112,2},{2... | collective-permute-start | bytes 786440 | tf_op jit(solution)/shard_map/ppermute | solution.py:18
  45.9 3.1 %collective-permute-start.8 = (bf16[512,256]{1,0:T(8,128)(2,1)S(1)}, bf16[512,256]{1,0:T(8,128)(2,1)S(1)}, u32[]{:S(2)}, u32[]{:S(2)}) collective-permute-start(bf16[512,256]{1,0:T(8,128)(2,1)S(1)} %collective-permute-done.5.refs_10_), channel_id=1, source_target_pairs={{0,114},{16,0},{32,16},{48,32},{64,48},{80,64},{96,80},{112,96},{2... | collective-permute-start | bytes 786440 | tf_op jit(solution)/shard_map/ppermute | solution.py:18
  49.0 2.6 %collective-permute-start.6 = (bf16[512,128]{1,0:T(8,128)(2,1)S(1)}, bf16[512,128]{1,0:T(8,128)(2,1)S(1)}, u32[]{:S(2)}, u32[]{:S(2)}) collective-permute-start(bf16[512,128]{1,0:T(8,128)(2,1)S(1)} %get-tuple-element.25), channel_id=1, source_target_pairs={{0,98},{16,114},{32,0},{48,16},{64,32},{80,48},{96,64},{112,80},{2... | collective-permute-start | bytes 393224 | tf_op jit(solution)/shard_map/ppermute | solution.py:18
  51.6 6.7 %collective-permute-done.6 = bf16[512,128]{1,0:T(8,128)(2,1)S(1)} collective-permute-done((bf16[512,128]{1,0:T(8,128)(2,1)S(1)}, bf16[512,128]{1,0:T(8,128)(2,1)S(1)}, u32[]{:S(2)}, u32[]{:S(2)}) %collective-permute-start.6) | collective-permute-done | bytes 131104 | tf_op jit(solution)/shard_map/ppermute | solution.py:18
  58.3 1.9 collective-permute-start.10
  60.2 4.6 %collective-permute-start.11 = (bf16[512,256]{1,0:T(8,128)(2,1)S(1)}, bf16[512,256]{1,0:T(8,128)(2,1)S(1)}, u32[]{:S(2)}, u32[]{:S(2)}) collective-permute-start(bf16[512,256]{1,0:T(8,128)(2,1)S(1)} %collective-permute-done.8.refs_11_), channel_id=1, source_target_pairs={{0,114},{16,0},{32,16},{48,32},{64,48},{80,64},{96,80},{112,96},{2... | collective-permute-start | bytes 786440 | tf_op jit(solution)/shard_map/ppermute | solution.py:18
  64.8 2.4 collective-permute-start.9
  67.2 4.7 %collective-permute-done.9 = bf16[512,128]{1,0:T(8,128)(2,1)S(1)} collective-permute-done((bf16[512,128]{1,0:T(8,128)(2,1)S(1)}, bf16[512,128]{1,0:T(8,128)(2,1)S(1)}, u32[]{:S(2)}, u32[]{:S(2)}) %collective-permute-start.9) | collective-permute-done | bytes 131104 | tf_op jit(solution)/shard_map/ppermute | solution.py:29
  72.0 1.2 stack.15
  73.2 15.6 %all-to-all-start = ((bf16[4,4,256,128]{3,2,1,0:T(8,128)(2,1)}), bf16[4,4,256,128]{3,2,1,0:T(8,128)(2,1)S(1)}, u32[]{:S(2)}, u32[]{:S(2)}) async-start(bf16[4,4,256,128]{3,2,1,0:T(8,128)(2,1)} %stack.15), calls=%async_computation | async-start | bytes 2097152 | tf_op jit(solution)/shard_map/all_to_all | solution.py:145
  88.8 1.9 collective-permute-start.12
  90.7 4.6 %collective-permute-start.14 = (bf16[512,256]{1,0:T(8,128)(2,1)S(1)}, bf16[512,256]{1,0:T(8,128)(2,1)S(1)}, u32[]{:S(2)}, u32[]{:S(2)}) collective-permute-start(bf16[512,256]{1,0:T(8,128)(2,1)S(1)} %collective-permute-done.11.refs_12_), channel_id=1, source_target_pairs={{0,114},{16,0},{32,16},{48,32},{64,48},{80,64},{96,80},{112,96},{2... | collective-permute-start | bytes 786440 | tf_op jit(solution)/shard_map/ppermute | solution.py:18
  95.3 1.8 collective-permute-done.12.refs_5_
  97.1 1.9 collective-permute-start.13
  99.7 4.6 %collective-permute-start.15 = (bf16[512,256]{1,0:T(8,128)(2,1)S(1)}, bf16[512,256]{1,0:T(8,128)(2,1)}, u32[]{:S(2)}, u32[]{:S(2)}) collective-permute-start(bf16[512,256]{1,0:T(8,128)(2,1)S(1)} %collective-permute-done.14.refs_13_), channel_id=1, source_target_pairs={{0,114},{16,0},{32,16},{48,32},{64,48},{80,64},{96,80},{112,96},{2... | collective-permute-start | bytes 786440 | tf_op jit(solution)/shard_map/ppermute | solution.py:18
  105.0 1.0 collective-permute-done.13.refs_6_
  106.7 1.0 collective-permute-done.15.refs_14_
  107.7 10.2 %collective-permute-start.19 = (bf16[4,4,256,128]{3,2,1,0:T(8,128)(2,1)S(1)}, bf16[4,4,256,128]{3,2,1,0:T(8,128)(2,1)S(1)}, u32[]{:S(2)}, u32[]{:S(2)}) collective-permute-start(bf16[4,4,256,128]{3,2,1,0:T(8,128)(2,1)S(1)} %all-to-all-done.refs_16_), channel_id=1, source_target_pairs={{0,1},{1,0},{2,3},{3,2},{4,5},{5,4},{6,7},{7,6},{8,9},{9,8},{10,11... | collective-permute-start | bytes 3145736 | tf_op jit(solution)/shard_map/ppermute | solution.py:89
  117.9 3.6 %collective-permute-start.16 = (bf16[512,256]{1,0:T(8,128)(2,1)}, bf16[512,256]{1,0:T(8,128)(2,1)S(1)}, u32[]{:S(2)}, u32[]{:S(2)}) collective-permute-start(bf16[512,256]{1,0:T(8,128)(2,1)} %copy-done.6), channel_id=1, source_target_pairs={{0,16},{16,32},{32,48},{48,64},{64,80},{80,96},{96,112},{112,2},{2... | collective-permute-start | bytes 786440 | tf_op jit(solution)/shard_map/ppermute | solution.py:18
  121.5 3.7 %collective-permute-start.18 = (bf16[512,256]{1,0:T(8,128)(2,1)}, bf16[512,256]{1,0:T(8,128)(2,1)S(1)}, u32[]{:S(2)}, u32[]{:S(2)}) collective-permute-start(bf16[512,256]{1,0:T(8,128)(2,1)} %collective-permute-done.15.refs_14_), channel_id=1, source_target_pairs={{0,114},{16,0},{32,16},{48,32},{64,48},{80,64},{96,80},{112,96},{2... | collective-permute-start | bytes 786440 | tf_op jit(solution)/shard_map/ppermute | solution.py:18
  125.2 4.9 %collective-permute-done.16.refs_7_ = bf16[512,256]{1,0:T(8,128)(2,1)S(1)} collective-permute-done((bf16[512,256]{1,0:T(8,128)(2,1)}, bf16[512,256]{1,0:T(8,128)(2,1)S(1)}, u32[]{:S(2)}, u32[]{:S(2)}) %collective-permute-start.16) | collective-permute-done | bytes 262176 | tf_op jit(solution)/shard_map/ppermute | solution.py:18
  130.1 1.9 collective-permute-start.17
  132.1 8.4 %collective-permute-done.17.refs_8_ = bf16[512,256]{1,0:T(8,128)(2,1)S(1)} collective-permute-done((bf16[512,256]{1,0:T(8,128)(2,1)S(1)}, bf16[512,256]{1,0:T(8,128)(2,1)S(1)}, u32[]{:S(2)}, u32[]{:S(2)}) %collective-permute-start.17) | collective-permute-done | bytes 262176 | tf_op jit(solution)/shard_map/ppermute | solution.py:18
  140.5 1.0 copy-done.1
  141.5 0.9 copy-done.4
  142.5 0.9 copy-done.7
  143.4 5.0 %shard_map.28 = bf16[4,4,256,128]{3,2,1,0:T(8,128)(2,1)} custom-call(bf16[512,256]{1,0:T(8,128)(2,1)S(1)} %convert_element_type.27.refs_0_, bf16[512,256]{1,0:T(8,128)(2,1)S(1)} %collective-permute-done.1.refs_1_, bf16[512,256]{1,0:T(8,128)(2,1)S(1)} %collective-permute-done.4.refs_2_, bf16[512,256]{1,0:T(8,128)(2,1)S(1)} %collective-permute-done.7.refs_3_, ...), custom_call_target="tpu_custom_call" | custom-call | flops 2147483648 | bytes 7340032 | tf_op jit(solution)/shard_map/pallas_call | solution.py:68
  148.5 5.2 %all-to-all-start.1 = ((bf16[16,256,128]{2,1,0:T(8,128)(2,1)}), bf16[16,256,128]{2,1,0:T(8,128)(2,1)S(1)}, u32[]{:S(2)}, u32[]{:S(2)}) async-start(bf16[16,256,128]{2,1,0:T(8,128)(2,1)} %bitcast.3), calls=%async_computation.1 | async-start | bytes 2097152 | tf_op jit(solution)/shard_map/all_to_all | solution.py:151
  153.7 15.0 %all-to-all-done.1 = bf16[16,256,128]{2,1,0:T(8,128)(2,1)S(1)} async-done(((bf16[16,256,128]{2,1,0:T(8,128)(2,1)}), bf16[16,256,128]{2,1,0:T(8,128)(2,1)S(1)}, u32[]{:S(2)}, u32[]{:S(2)}) %all-to-all-start.1) | async-done | bytes 1048608 | tf_op jit(solution)/shard_map/all_to_all | solution.py:151
  169.4 18.6 %all_to_all.20 = bf16[16,256,128]{2,1,0:T(8,128)(2,1)S(1)} all-to-all(bf16[16,256,128]{2,1,0:T(8,128)(2,1)S(1)} %bitcast.14), channel_id=1, replica_groups=mesh['x'=4,'zl'=8,'y'=4,'zh'=2,'c'=2] {'x','y'}, dimensions={0} | all-to-all | bytes 2097152 | tf_op jit(solution)/shard_map/all_to_all | solution.py:156
  188.1 5.3 %collective-permute-start.20 = (bf16[4,4,256,128]{3,2,1,0:T(8,128)(2,1)S(1)}, bf16[4,4,256,128]{3,2,1,0:T(8,128)(2,1)S(1)}, u32[]{:S(2)}, u32[]{:S(2)}) collective-permute-start(bf16[4,4,256,128]{3,2,1,0:T(8,128)(2,1)S(1)} %bitcast.12), channel_id=1, source_target_pairs={{0,1},{1,0},{2,3},{3,2},{4,5},{5,4},{6,7},{7,6},{8,9},{9,8},{10,11... | collective-permute-start | bytes 3145736 | tf_op jit(solution)/shard_map/ppermute | solution.py:89
  193.4 2.3 collective-permute-done.20.refs_17_
  195.7 4.4 %shard_map.29 = bf16[4,4,256,128]{3,2,1,0:T(8,128)(2,1)S(1)} custom-call(bf16[512,256]{1,0:T(8,128)(2,1)S(1)} %convert_element_type.27.refs_0_, bf16[512,256]{1,0:T(8,128)(2,1)S(1)} %collective-permute-done.1.refs_1_, bf16[512,256]{1,0:T(8,128)(2,1)S(1)} %collective-permute-done.4.refs_2_, bf16[512,256]{1,0:T(8,128)(2,1)S(1)} %collective-permute-done.7.refs_3_, ...), custom_call_target="tpu_custom_call" | custom-call | flops 2147483648 | bytes 7340032 | tf_op jit(solution)/shard_map/pallas_call | solution.py:68
  200.1 17.3 %all_to_all.21 = bf16[4,4,256,128]{3,2,1,0:T(8,128)(2,1)S(1)} all-to-all(bf16[4,4,256,128]{3,2,1,0:T(8,128)(2,1)S(1)} %shard_map.29), channel_id=1, replica_groups=mesh['x'=4,'zl'=8,'y'=4,'zh'=2,'c'=2] {'x'}, dimensions={0} | all-to-all | bytes 2097152 | tf_op jit(solution)/shard_map/all_to_all | solution.py:158
  217.6 3.8 %collective-permute-start.22 = (bf16[512,128]{1,0:T(8,128)(2,1)S(1)}, bf16[512,128]{1,0:T(8,128)(2,1)S(1)}, u32[]{:S(2)}, u32[]{:S(2)}) collective-permute-start(bf16[512,128]{1,0:T(8,128)(2,1)S(1)} %bitcast.18), channel_id=1, source_target_pairs={{0,64},{16,80},{32,96},{48,112},{64,2},{80,18},{96,34},{112,50},{2... | collective-permute-start | bytes 393224 | tf_op jit(solution)/shard_map/ppermute | solution.py:18
  221.4 5.4 %collective-permute-start.21 = (bf16[512,128]{1,0:T(8,128)(2,1)S(1)}, bf16[512,128]{1,0:T(8,128)(2,1)S(1)}, u32[]{:S(2)}, u32[]{:S(2)}) collective-permute-start(bf16[512,128]{1,0:T(8,128)(2,1)S(1)} %bitcast.17), channel_id=1, source_target_pairs={{0,66},{16,82},{32,98},{48,114},{64,0},{80,16},{96,32},{112,48},{2... | collective-permute-start | bytes 393224 | tf_op jit(solution)/shard_map/ppermute | solution.py:18
  226.8 10.2 %collective-permute-done.22 = bf16[512,128]{1,0:T(8,128)(2,1)S(1)} collective-permute-done((bf16[512,128]{1,0:T(8,128)(2,1)S(1)}, bf16[512,128]{1,0:T(8,128)(2,1)S(1)}, u32[]{:S(2)}, u32[]{:S(2)}) %collective-permute-start.22) | collective-permute-done | bytes 131104 | tf_op jit(solution)/shard_map/ppermute | solution.py:18
  237.0 2.9 %collective-permute-done.21 = bf16[512,128]{1,0:T(8,128)(2,1)S(1)} collective-permute-done((bf16[512,128]{1,0:T(8,128)(2,1)S(1)}, bf16[512,128]{1,0:T(8,128)(2,1)S(1)}, u32[]{:S(2)}, u32[]{:S(2)}) %collective-permute-start.21) | collective-permute-done | bytes 131104 | tf_op jit(solution)/shard_map/ppermute | solution.py:18
  240.0 0.8 convert_add_fusion
  (55 shorter events, 3.1 us)
Async XLA Ops:
  0.0 15.0 %copy-start.16 = (f32[512,256]{1,0:T(8,128)S(1)}, f32[512,256]{1,0:T(8,128)}, u32[]{:S(2)}) copy-start(f32[512,256]{1,0:T(8,128)} %param.3) | copy-start | bytes 1572868
  1.1 24.7 %collective-permute-start.2 = (bf16[512,256]{1,0:T(8,128)(2,1)S(1)}, bf16[512,256]{1,0:T(8,128)(2,1)S(1)}, u32[]{:S(2)}, u32[]{:S(2)}) collective-permute-start(bf16[512,256]{1,0:T(8,128)(2,1)S(1)} %convert_element_type.27.refs_0_), channel_id=1, source_target_pairs={{0,114},{16,0},{32,16},{48,32},{64,48},{80,64},{96,80},{112,96},{2... | collective-permute-start | bytes 786440 | tf_op jit(solution)/shard_map/ppermute | solution.py:18
  13.1 12.7 %collective-permute-start.1 = (bf16[512,256]{1,0:T(8,128)(2,1)S(1)}, bf16[512,256]{1,0:T(8,128)(2,1)S(1)}, u32[]{:S(2)}, u32[]{:S(2)}) collective-permute-start(bf16[512,256]{1,0:T(8,128)(2,1)S(1)} %convert_element_type.27.refs_0_), channel_id=1, source_target_pairs={{0,16},{16,32},{32,48},{48,64},{64,80},{80,96},{96,112},{112,2},{2... | collective-permute-start | bytes 786440 | tf_op jit(solution)/shard_map/ppermute | solution.py:18
  15.1 10.7 %collective-permute-start = (bf16[512,128]{1,0:T(8,128)(2,1)S(1)}, bf16[512,128]{1,0:T(8,128)(2,1)S(1)}, u32[]{:S(2)}, u32[]{:S(2)}) collective-permute-start(bf16[512,128]{1,0:T(8,128)(2,1)S(1)} %get-tuple-element.44), channel_id=1, source_target_pairs={{0,32},{16,48},{32,64},{48,80},{64,96},{80,112},{96,2},{112,18},{2... | collective-permute-start | bytes 393224 | tf_op jit(solution)/shard_map/ppermute | solution.py:18
  25.8 16.7 %collective-permute-start.4 = (bf16[512,256]{1,0:T(8,128)(2,1)S(1)}, bf16[512,256]{1,0:T(8,128)(2,1)S(1)}, u32[]{:S(2)}, u32[]{:S(2)}) collective-permute-start(bf16[512,256]{1,0:T(8,128)(2,1)S(1)} %collective-permute-done.1.refs_1_), channel_id=1, source_target_pairs={{0,16},{16,32},{32,48},{48,64},{64,80},{80,96},{96,112},{112,2},{2... | collective-permute-start | bytes 786440 | tf_op jit(solution)/shard_map/ppermute | solution.py:18
  31.5 11.0 %collective-permute-start.5 = (bf16[512,256]{1,0:T(8,128)(2,1)S(1)}, bf16[512,256]{1,0:T(8,128)(2,1)S(1)}, u32[]{:S(2)}, u32[]{:S(2)}) collective-permute-start(bf16[512,256]{1,0:T(8,128)(2,1)S(1)} %collective-permute-done.2.refs_9_), channel_id=1, source_target_pairs={{0,114},{16,0},{32,16},{48,32},{64,48},{80,64},{96,80},{112,96},{2... | collective-permute-start | bytes 786440 | tf_op jit(solution)/shard_map/ppermute | solution.py:18
  33.4 9.1 %collective-permute-start.3 = (bf16[512,128]{1,0:T(8,128)(2,1)S(1)}, bf16[512,128]{1,0:T(8,128)(2,1)S(1)}, u32[]{:S(2)}, u32[]{:S(2)}) collective-permute-start(bf16[512,128]{1,0:T(8,128)(2,1)S(1)} %collective-permute-done), channel_id=1, source_target_pairs={{0,32},{16,48},{32,64},{48,80},{64,96},{80,112},{96,2},{112,18},{2... | collective-permute-start | bytes 393224 | tf_op jit(solution)/shard_map/ppermute | solution.py:29
  42.5 15.8 %collective-permute-start.7 = (bf16[512,256]{1,0:T(8,128)(2,1)S(1)}, bf16[512,256]{1,0:T(8,128)(2,1)S(1)}, u32[]{:S(2)}, u32[]{:S(2)}) collective-permute-start(bf16[512,256]{1,0:T(8,128)(2,1)S(1)} %collective-permute-done.4.refs_2_), channel_id=1, source_target_pairs={{0,16},{16,32},{32,48},{48,64},{64,80},{80,96},{96,112},{112,2},{2... | collective-permute-start | bytes 786440 | tf_op jit(solution)/shard_map/ppermute | solution.py:18
  45.9 12.4 %collective-permute-start.8 = (bf16[512,256]{1,0:T(8,128)(2,1)S(1)}, bf16[512,256]{1,0:T(8,128)(2,1)S(1)}, u32[]{:S(2)}, u32[]{:S(2)}) collective-permute-start(bf16[512,256]{1,0:T(8,128)(2,1)S(1)} %collective-permute-done.5.refs_10_), channel_id=1, source_target_pairs={{0,114},{16,0},{32,16},{48,32},{64,48},{80,64},{96,80},{112,96},{2... | collective-permute-start | bytes 786440 | tf_op jit(solution)/shard_map/ppermute | solution.py:18
  49.0 9.3 %collective-permute-start.6 = (bf16[512,128]{1,0:T(8,128)(2,1)S(1)}, bf16[512,128]{1,0:T(8,128)(2,1)S(1)}, u32[]{:S(2)}, u32[]{:S(2)}) collective-permute-start(bf16[512,128]{1,0:T(8,128)(2,1)S(1)} %get-tuple-element.25), channel_id=1, source_target_pairs={{0,98},{16,114},{32,0},{48,16},{64,32},{80,48},{96,64},{112,80},{2... | collective-permute-start | bytes 393224 | tf_op jit(solution)/shard_map/ppermute | solution.py:18
  58.3 13.6 %collective-permute-start.10 = (bf16[512,256]{1,0:T(8,128)(2,1)S(1)}, bf16[512,256]{1,0:T(8,128)(2,1)S(1)}, u32[]{:S(2)}, u32[]{:S(2)}) collective-permute-start(bf16[512,256]{1,0:T(8,128)(2,1)S(1)} %collective-permute-done.7.refs_3_), channel_id=1, source_target_pairs={{0,16},{16,32},{32,48},{48,64},{64,80},{80,96},{96,112},{112,2},{2... | collective-permute-start | bytes 786440 | tf_op jit(solution)/shard_map/ppermute | solution.py:18
  60.2 11.7 %collective-permute-start.11 = (bf16[512,256]{1,0:T(8,128)(2,1)S(1)}, bf16[512,256]{1,0:T(8,128)(2,1)S(1)}, u32[]{:S(2)}, u32[]{:S(2)}) collective-permute-start(bf16[512,256]{1,0:T(8,128)(2,1)S(1)} %collective-permute-done.8.refs_11_), channel_id=1, source_target_pairs={{0,114},{16,0},{32,16},{48,32},{64,48},{80,64},{96,80},{112,96},{2... | collective-permute-start | bytes 786440 | tf_op jit(solution)/shard_map/ppermute | solution.py:18
  64.8 7.1 %collective-permute-start.9 = (bf16[512,128]{1,0:T(8,128)(2,1)S(1)}, bf16[512,128]{1,0:T(8,128)(2,1)S(1)}, u32[]{:S(2)}, u32[]{:S(2)}) collective-permute-start(bf16[512,128]{1,0:T(8,128)(2,1)S(1)} %collective-permute-done.6), channel_id=1, source_target_pairs={{0,98},{16,114},{32,0},{48,16},{64,32},{80,48},{96,64},{112,80},{2... | collective-permute-start | bytes 393224 | tf_op jit(solution)/shard_map/ppermute | solution.py:29
  73.2 34.5 %all-to-all-start = ((bf16[4,4,256,128]{3,2,1,0:T(8,128)(2,1)}), bf16[4,4,256,128]{3,2,1,0:T(8,128)(2,1)S(1)}, u32[]{:S(2)}, u32[]{:S(2)}) async-start(bf16[4,4,256,128]{3,2,1,0:T(8,128)(2,1)} %stack.15), calls=%async_computation | async-start | bytes 2097152 | tf_op jit(solution)/shard_map/all_to_all | solution.py:145
  88.8 8.3 %collective-permute-start.12 = (bf16[512,256]{1,0:T(8,128)(2,1)S(1)}, bf16[512,256]{1,0:T(8,128)(2,1)S(1)}, u32[]{:S(2)}, u32[]{:S(2)}) collective-permute-start(bf16[512,256]{1,0:T(8,128)(2,1)S(1)} %collective-permute-done.10.refs_4_), channel_id=1, source_target_pairs={{0,16},{16,32},{32,48},{48,64},{64,80},{80,96},{96,112},{112,2},{2... | collective-permute-start | bytes 786440 | tf_op jit(solution)/shard_map/ppermute | solution.py:18
  90.7 9.0 %collective-permute-start.14 = (bf16[512,256]{1,0:T(8,128)(2,1)S(1)}, bf16[512,256]{1,0:T(8,128)(2,1)S(1)}, u32[]{:S(2)}, u32[]{:S(2)}) collective-permute-start(bf16[512,256]{1,0:T(8,128)(2,1)S(1)} %collective-permute-done.11.refs_12_), channel_id=1, source_target_pairs={{0,114},{16,0},{32,16},{48,32},{64,48},{80,64},{96,80},{112,96},{2... | collective-permute-start | bytes 786440 | tf_op jit(solution)/shard_map/ppermute | solution.py:18
  97.1 8.9 %collective-permute-start.13 = (bf16[512,256]{1,0:T(8,128)(2,1)S(1)}, bf16[512,256]{1,0:T(8,128)(2,1)S(1)}, u32[]{:S(2)}, u32[]{:S(2)}) collective-permute-start(bf16[512,256]{1,0:T(8,128)(2,1)S(1)} %collective-permute-done.12.refs_5_), channel_id=1, source_target_pairs={{0,16},{16,32},{32,48},{48,64},{64,80},{80,96},{96,112},{112,2},{2... | collective-permute-start | bytes 786440 | tf_op jit(solution)/shard_map/ppermute | solution.py:18
  99.0 0.7 copy-start
  99.7 8.0 %collective-permute-start.15 = (bf16[512,256]{1,0:T(8,128)(2,1)S(1)}, bf16[512,256]{1,0:T(8,128)(2,1)}, u32[]{:S(2)}, u32[]{:S(2)}) collective-permute-start(bf16[512,256]{1,0:T(8,128)(2,1)S(1)} %collective-permute-done.14.refs_13_), channel_id=1, source_target_pairs={{0,114},{16,0},{32,16},{48,32},{64,48},{80,64},{96,80},{112,96},{2... | collective-permute-start | bytes 786440 | tf_op jit(solution)/shard_map/ppermute | solution.py:18
  104.3 0.7 copy-start.3
  105.9 0.7 copy-start.6
  107.7 32.8 %collective-permute-start.19 = (bf16[4,4,256,128]{3,2,1,0:T(8,128)(2,1)S(1)}, bf16[4,4,256,128]{3,2,1,0:T(8,128)(2,1)S(1)}, u32[]{:S(2)}, u32[]{:S(2)}) collective-permute-start(bf16[4,4,256,128]{3,2,1,0:T(8,128)(2,1)S(1)} %all-to-all-done.refs_16_), channel_id=1, source_target_pairs={{0,1},{1,0},{2,3},{3,2},{4,5},{5,4},{6,7},{7,6},{8,9},{9,8},{10,11... | collective-permute-start | bytes 3145736 | tf_op jit(solution)/shard_map/ppermute | solution.py:89
  117.9 12.2 %collective-permute-start.16 = (bf16[512,256]{1,0:T(8,128)(2,1)}, bf16[512,256]{1,0:T(8,128)(2,1)S(1)}, u32[]{:S(2)}, u32[]{:S(2)}) collective-permute-start(bf16[512,256]{1,0:T(8,128)(2,1)} %copy-done.6), channel_id=1, source_target_pairs={{0,16},{16,32},{32,48},{48,64},{64,80},{80,96},{96,112},{112,2},{2... | collective-permute-start | bytes 786440 | tf_op jit(solution)/shard_map/ppermute | solution.py:18
  121.5 10.5 %collective-permute-start.18 = (bf16[512,256]{1,0:T(8,128)(2,1)}, bf16[512,256]{1,0:T(8,128)(2,1)S(1)}, u32[]{:S(2)}, u32[]{:S(2)}) collective-permute-start(bf16[512,256]{1,0:T(8,128)(2,1)} %collective-permute-done.15.refs_14_), channel_id=1, source_target_pairs={{0,114},{16,0},{32,16},{48,32},{64,48},{80,64},{96,80},{112,96},{2... | collective-permute-start | bytes 786440 | tf_op jit(solution)/shard_map/ppermute | solution.py:18
  130.1 18.3 %copy-start.9 = (bf16[512,256]{1,0:T(8,128)(2,1)}, bf16[512,256]{1,0:T(8,128)(2,1)S(1)}, u32[]{:S(2)}) copy-start(bf16[512,256]{1,0:T(8,128)(2,1)S(1)} %collective-permute-done.16.refs_7_) | copy-start | bytes 786436
  130.1 10.4 %collective-permute-start.17 = (bf16[512,256]{1,0:T(8,128)(2,1)S(1)}, bf16[512,256]{1,0:T(8,128)(2,1)S(1)}, u32[]{:S(2)}, u32[]{:S(2)}) collective-permute-start(bf16[512,256]{1,0:T(8,128)(2,1)S(1)} %collective-permute-done.16.refs_7_), channel_id=1, source_target_pairs={{0,16},{16,32},{32,48},{48,64},{64,80},{80,96},{96,112},{112,2},{2... | collective-permute-start | bytes 786440 | tf_op jit(solution)/shard_map/ppermute | solution.py:18
  132.1 16.4 %copy-start.11 = (bf16[512,256]{1,0:T(8,128)(2,1)}, bf16[512,256]{1,0:T(8,128)(2,1)S(1)}, u32[]{:S(2)}) copy-start(bf16[512,256]{1,0:T(8,128)(2,1)S(1)} %collective-permute-done.18.refs_15_) | copy-start | bytes 786436
  140.5 8.0 %copy-start.13 = (bf16[512,256]{1,0:T(8,128)(2,1)}, bf16[512,256]{1,0:T(8,128)(2,1)S(1)}, u32[]{:S(2)}) copy-start(bf16[512,256]{1,0:T(8,128)(2,1)S(1)} %collective-permute-done.17.refs_8_) | copy-start | bytes 786436
  140.5 1.0 copy-start.1
  141.5 0.9 copy-start.4
  142.5 0.9 copy-start.7
  148.5 20.3 %all-to-all-start.1 = ((bf16[16,256,128]{2,1,0:T(8,128)(2,1)}), bf16[16,256,128]{2,1,0:T(8,128)(2,1)S(1)}, u32[]{:S(2)}, u32[]{:S(2)}) async-start(bf16[16,256,128]{2,1,0:T(8,128)(2,1)} %bitcast.3), calls=%async_computation.1 | async-start | bytes 2097152 | tf_op jit(solution)/shard_map/all_to_all | solution.py:151
  169.4 26.3 %copy-start.2 = (bf16[512,256]{1,0:T(8,128)(2,1)S(1)}, bf16[512,256]{1,0:T(8,128)(2,1)}, u32[]{:S(2)}) copy-start(bf16[512,256]{1,0:T(8,128)(2,1)} %copy-done) | copy-start | bytes 786436
  169.4 26.3 %copy-start.5 = (bf16[512,256]{1,0:T(8,128)(2,1)S(1)}, bf16[512,256]{1,0:T(8,128)(2,1)}, u32[]{:S(2)}) copy-start(bf16[512,256]{1,0:T(8,128)(2,1)} %copy-done.3) | copy-start | bytes 786436
  169.4 26.2 %copy-start.8 = (bf16[512,256]{1,0:T(8,128)(2,1)S(1)}, bf16[512,256]{1,0:T(8,128)(2,1)}, u32[]{:S(2)}) copy-start(bf16[512,256]{1,0:T(8,128)(2,1)} %copy-done.6) | copy-start | bytes 786436
  169.4 26.2 %copy-start.10 = (bf16[512,256]{1,0:T(8,128)(2,1)S(1)}, bf16[512,256]{1,0:T(8,128)(2,1)}, u32[]{:S(2)}) copy-start(bf16[512,256]{1,0:T(8,128)(2,1)} %copy-done.9) | copy-start | bytes 786436
  169.4 26.2 %copy-start.12 = (bf16[512,256]{1,0:T(8,128)(2,1)S(1)}, bf16[512,256]{1,0:T(8,128)(2,1)}, u32[]{:S(2)}) copy-start(bf16[512,256]{1,0:T(8,128)(2,1)} %copy-done.11) | copy-start | bytes 786436
  169.4 26.2 %copy-start.14 = (bf16[512,256]{1,0:T(8,128)(2,1)S(1)}, bf16[512,256]{1,0:T(8,128)(2,1)}, u32[]{:S(2)}) copy-start(bf16[512,256]{1,0:T(8,128)(2,1)} %copy-done.13) | copy-start | bytes 786436
  188.1 7.6 %collective-permute-start.20 = (bf16[4,4,256,128]{3,2,1,0:T(8,128)(2,1)S(1)}, bf16[4,4,256,128]{3,2,1,0:T(8,128)(2,1)S(1)}, u32[]{:S(2)}, u32[]{:S(2)}) collective-permute-start(bf16[4,4,256,128]{3,2,1,0:T(8,128)(2,1)S(1)} %bitcast.12), channel_id=1, source_target_pairs={{0,1},{1,0},{2,3},{3,2},{4,5},{5,4},{6,7},{7,6},{8,9},{9,8},{10,11... | collective-permute-start | bytes 3145736 | tf_op jit(solution)/shard_map/ppermute | solution.py:89
  217.3 22.7 %copy-start.15 = (f32[512,256]{1,0:T(8,128)S(1)}, f32[512,256]{1,0:T(8,128)}, u32[]{:S(2)}) copy-start(f32[512,256]{1,0:T(8,128)} %param.2) | copy-start | bytes 1572868
  217.6 19.4 %collective-permute-start.22 = (bf16[512,128]{1,0:T(8,128)(2,1)S(1)}, bf16[512,128]{1,0:T(8,128)(2,1)S(1)}, u32[]{:S(2)}, u32[]{:S(2)}) collective-permute-start(bf16[512,128]{1,0:T(8,128)(2,1)S(1)} %bitcast.18), channel_id=1, source_target_pairs={{0,64},{16,80},{32,96},{48,112},{64,2},{80,18},{96,34},{112,50},{2... | collective-permute-start | bytes 393224 | tf_op jit(solution)/shard_map/ppermute | solution.py:18
  221.4 18.5 %collective-permute-start.21 = (bf16[512,128]{1,0:T(8,128)(2,1)S(1)}, bf16[512,128]{1,0:T(8,128)(2,1)S(1)}, u32[]{:S(2)}, u32[]{:S(2)}) collective-permute-start(bf16[512,128]{1,0:T(8,128)(2,1)S(1)} %bitcast.17), channel_id=1, source_target_pairs={{0,66},{16,82},{32,98},{48,114},{64,0},{80,16},{96,32},{112,48},{2... | collective-permute-start | bytes 393224 | tf_op jit(solution)/shard_map/ppermute | solution.py:18

commit v5 on v2

v5 whole, which is shorter than its diff:
```python
import functools

import jax
import jax.numpy as jnp
from jax import lax
from jax.experimental import pallas as pl
from jax.experimental.pallas import tpu as pltpu
from jax.sharding import Mesh
from jax.sharding import PartitionSpec as P

AXES = ("x", "zl", "y", "zh", "c")
SIZES = (4, 8, 4, 2, 2)
PLANE = ("x", "y")
SWAP = [(0, 1), (1, 0)]


def flat_id(x, zl, y, zh, c):
    return (((x * 8 + zl) * 4 + y) * 2 + zh) * 2 + c


Z_RINGS = [
    [flat_id(x, z % 8, y, z // 8, c) for z in range(16)]
    for x in range(4)
    for y in range(4)
    for c in range(2)
]


def dot_kernel(flips, z_ref, own_ref, other_ref, out_ref, left, sem):
    groups, _, depth, width = own_ref.shape
    c = lax.axis_index("c")
    firsts = [0, 8] if flips is None else [(lax.axis_index("zh") ^ flips) * 8]
    copies = []
    for b, first in enumerate(firsts):
        for n in range(8):
            chunk = (n % 4) // 2 * 4 + (c ^ (n // 4)) * 2 + n % 2
            copies.append(
                pltpu.make_async_copy(z_ref.at[first + chunk], left.at[b * 8 + n], sem.at[b * 8 + n])
            )
    for copy in copies:
        copy.start()
    for s in range(out_ref.shape[1]):
        b, rows = s // 2, slice(s % 2 * depth, (s % 2 + 1) * depth)
        total = None
        for n in range(8):
            if s % 2 == 0:
                copies[b * 8 + n].wait()
            part = (own_ref, other_ref)[n // 4]
            right = jnp.concatenate([part[j, n % 4] for j in range(groups)], axis=1)
            term = jnp.dot(left[b * 8 + n, rows, :], right, preferred_element_type=jnp.float32)
            total = term if total is None else total + term
        for j in range(groups):
            out_ref[j, s] = total[:, j * width : (j + 1) * width].astype(out_ref.dtype)


def dot_right(flips, z_rows, own, other):
    groups, steps, depth, width = own.shape
    chunks = 16 if flips is None else 8
    steps = chunks // 4
    return pl.pallas_call(
        functools.partial(dot_kernel, flips),
        in_specs=[pl.BlockSpec(memory_space=pl.ANY)] + [pl.BlockSpec(memory_space=pltpu.VMEM)] * 2,
        out_specs=pl.BlockSpec(memory_space=pltpu.VMEM),
        out_shape=jax.ShapeDtypeStruct((groups, steps, depth, width), jnp.bfloat16),
        scratch_shapes=[
            pltpu.VMEM((chunks,) + z_rows.shape[1:], jnp.bfloat16),
            pltpu.SemaphoreType.DMA((chunks,)),
        ],
        compiler_params=pltpu.CompilerParams(vmem_limit_bytes=(56 if flips is None else 32) * 2**20),
        cost_estimate=pl.CostEstimate(
            flops=2 * z_rows.size * groups * width * chunks // 16,
            bytes_accessed=2 * (z_rows.size * chunks // 16 + 3 * own.size),
            transcendentals=0,
        ),
    )(z_rows, own, other)


def other_core(block):
    return lax.ppermute(block, "c", SWAP)


def make_shift(product, order, first_col):
    at = lax.axis_index
    rows = product.shape[1]
    row_ids = (
        lax.broadcasted_iota(jnp.int32, product.shape, 0) * 2048
        + at("y") // 2 * 1024
        + at("c") * 512
        + at("y") % 2 * rows
        + lax.broadcasted_iota(jnp.int32, product.shape, 1)
    )
    col_ids = first_col + lax.broadcasted_iota(jnp.int32, product.shape, 2)
    ident = jnp.where(row_ids == col_ids, 1.5, 0.0).astype(jnp.float32)
    poly = lax.reduce_precision(ident - 0.5 / order * product, 8, 7)
    return (poly - ident).astype(jnp.bfloat16)


def shards(z_iter, y_iter):
    at = lax.axis_index
    order = z_iter.shape[1] * lax.axis_size("x") * lax.axis_size("zl")
    z_half = z_iter.astype(jnp.bfloat16)
    y_half = y_iter.astype(jnp.bfloat16)
    z_rows = lax.all_gather(z_half, AXES, axis_index_groups=Z_RINGS)

    zh = at("zh")
    low = zh == 0
    first_col = at("x") * 2048 + at("zl") * 256 + zh * 128
    left, right = y_half[:, :128], y_half[:, 128:]
    mine = jnp.where(low, left, right)
    yours = lax.ppermute(jnp.where(low, right, left), "zh", SWAP)
    y_both = jnp.stack([jnp.where(low, mine, yours), jnp.where(low, yours, mine)])
    y_both = y_both.reshape(4, 256, 128)

    turn = [(i * 4 + j, j * 4 + i) for i in range(4) for j in range(4)]
    turned = lax.ppermute(y_both, PLANE, turn)
    y_own = lax.all_to_all(jnp.stack([turned] * 4), "y", 0, 0, tiled=True)
    part = dot_right(None, z_rows, y_own, other_core(y_own))

    part = lax.all_to_all(part.reshape(16, 256, 128), PLANE, 0, 0, tiled=True)
    product = part.reshape(4, 4, 256, 128).astype(jnp.float32).sum(0)
    shift = make_shift(product, order, first_col)

    spread = jnp.broadcast_to(shift[:, None], (4, 4, 256, 128)).reshape(16, 256, 128)
    own = lax.all_to_all(spread, PLANE, 0, 0, tiled=True).reshape(4, 4, 256, 128)
    other = other_core(own)

    def result(flips):
        part = dot_right(flips, z_rows, own, other)
        part = lax.all_to_all(part, "x", 0, 0, tiled=True)
        return part.astype(jnp.float32).sum(0).reshape(512, 128)

    yours = lax.ppermute(result(1).astype(jnp.bfloat16), "zh", SWAP).astype(jnp.float32)
    mine = result(0)
    part = jnp.concatenate([jnp.where(low, mine, yours), jnp.where(low, yours, mine)], axis=1)
    return 1.5 * z_half.astype(jnp.float32) + part


def solution(mesh):
    fine = Mesh(mesh.devices.reshape(SIZES), AXES)
    spec = P(("y", "zh", "c"), ("x", "zl"))
    return jax.shard_map(
        shards,
        mesh=fine,
        in_specs=(spec, spec),
        out_specs=spec,
        check_vma=False,
    )
```

time: 198 us -> 194 us (0.980)
  the two profiles are of different devices: /device:TPU:1 before, /device:TPU:2 now
where the time goes in v5:
time: 194 us; the launch traced here: 193 us
  waiting for transfers between devices  76.4 us (39%)
  starting transfers between devices  48.2 us (25%)
  blocking collectives  36 us (19%)
  between operations  13.5 us (7%)
  Pallas kernels  12 us (6%)
  other arithmetic  4.36 us (2%)
  local copies, waits for them, and re-layouts  2.6 us (1%)
    all_gather x1, waiting for transfers between devices, shards(): z_rows = lax.all_gather(z_half, AXES, axis_index_groups=Z_RINGS)  28.1 us
    all_to_all x1, blocking collectives, shards(): y_own = lax.all_to_all(jnp.stack([turned] * 4), 'y', 0, 0, tiled=True)  19.9 us
    all_to_all x1, blocking collectives, shards(): lax.all_to_all(spread, PLANE, 0, 0, tiled=True).reshape(4, 4, 256, 128)  16.1 us
    ppermute x1, starting transfers between devices, shards(): yours = lax.ppermute(jnp.where(low, right, left), 'zh', SWAP)  15.7 us
    ppermute x1, waiting for transfers between devices, shards(): lax.ppermute(result(1).astype(jnp.bfloat16), 'zh', SWAP).astype(jnp.float32)  15 us
    pallas_call x3, Pallas kernels, dot_right(): pl.pallas_call(functools.partial(dot_kernel, flips), in_specs=[pl.BlockSp...  12 us
    all_to_all x1, waiting for transfers between devices, shards(): part = lax.all_to_all(part.reshape(16, 256, 128), PLANE, 0, 0, tiled=True)  11 us
    all_to_all x2, starting transfers between devices, result(): part = lax.all_to_all(part, 'x', 0, 0, tiled=True)  10.6 us
  transfers between devices with their start and end apart: 9, of which 9 were waited for; matrix products, arithmetic and copies ran while one was open for 1% of the time, Pallas kernels for 1%

profile of v5, /device:TPU:2, one launch (start us, length us, event | category | flops | bytes accessed | tf_op | source)
XLA Modules:
  0.0 193.1 jit_solution(939717048532557410)
XLA Ops:
  6.5 0.0 all-gather.3.cloned.1.call-start
  6.5 1.8 convert_element_type.33
  8.3 0.0 all-gather.3.cloned.1.call-update
  8.3 1.1 convert_element_type.35
  9.4 15.7 %collective-permute-start = (bf16[512,128]{1,0:T(8,128)(2,1)S(1)}, bf16[512,128]{1,0:T(8,128)(2,1)S(1)}, u32[]{:S(2)}, u32[]{:S(2)}) collective-permute-start(bf16[512,128]{1,0:T(8,128)(2,1)S(1)} %broadcast_select_fusion), channel_id=1, source_target_pairs={{0,2},{2,0},{1,3},{3,1},{4,6},{6,4},{5,7},{7,5},{8,10},{10,8},{9,1... | collective-permute-start | bytes 393224 | tf_op jit(solution)/shard_map/ppermute | solution.py:110
  25.2 3.8 %collective-permute-done = bf16[512,128]{1,0:T(8,128)(2,1)S(1)} collective-permute-done((bf16[512,128]{1,0:T(8,128)(2,1)S(1)}, bf16[512,128]{1,0:T(8,128)(2,1)S(1)}, u32[]{:S(2)}, u32[]{:S(2)}) %collective-permute-start) | collective-permute-done | bytes 131104 | tf_op jit(solution)/shard_map/ppermute | solution.py:110
  29.0 3.5 %collective-permute-start.1 = (bf16[4,256,128]{2,1,0:T(8,128)(2,1)S(1)}, bf16[4,256,128]{2,1,0:T(8,128)(2,1)S(1)}, u32[]{:S(2)}, u32[]{:S(2)}) collective-permute-start(bf16[4,256,128]{2,1,0:T(8,128)(2,1)S(1)} %bitcast.24), channel_id=1, source_target_pairs={{0,0},{4,128},{8,256},{12,384},{128,4},{132,132},{136,260},{140,38... | collective-permute-start | bytes 786440 | tf_op jit(solution)/shard_map/ppermute | solution.py:115
  32.5 9.1 %collective-permute-done.1 = bf16[4,256,128]{2,1,0:T(8,128)(2,1)S(1)} collective-permute-done((bf16[4,256,128]{2,1,0:T(8,128)(2,1)S(1)}, bf16[4,256,128]{2,1,0:T(8,128)(2,1)S(1)}, u32[]{:S(2)}, u32[]{:S(2)}) %collective-permute-start.1) | collective-permute-done | bytes 262176 | tf_op jit(solution)/shard_map/ppermute | solution.py:115
  41.6 0.2 stack.19
  41.8 19.9 %all_to_all.25.own_ref = bf16[4,4,256,128]{3,2,1,0:T(8,128)(2,1)S(1)} all-to-all(bf16[4,4,256,128]{3,2,1,0:T(8,128)(2,1)S(1)} %stack.19), channel_id=1, replica_groups=mesh['x'=4,'zl'=8,'y'=4,'zh'=2,'c'=2] {'y'}, dimensions={0} | all-to-all | bytes 2097152 | tf_op jit(solution)/shard_map/all_to_all | solution.py:116
  61.7 0.0 copy-start.3
  61.7 1.9 collective-permute-start.2
  63.6 2.6 %collective-permute-done.2.other_ref = bf16[4,4,256,128]{3,2,1,0:T(8,128)(2,1)S(1)} collective-permute-done((bf16[4,4,256,128]{3,2,1,0:T(8,128)(2,1)S(1)}, bf16[4,4,256,128]{3,2,1,0:T(8,128)(2,1)S(1)}, u32[]{:S(2)}, u32[]{:S(2)}) %collective-permute-start.2) | collective-permute-done | bytes 1048608 | tf_op jit(solution)/shard_map/ppermute | solution.py:79
  66.2 0.0 copy-start.4
  66.2 28.1 %all-gather.3.cloned.1.call-done = bf16[8192,256]{1,0:T(8,128)(2,1)} async-done(((bf16[512,256]{1,0:T(8,128)(2,1)}), bf16[8192,256]{1,0:T(8,128)(2,1)}) %all-gather.3.cloned.1.call-update) | async-done | bytes 4194320 | tf_op jit(solution)/shard_map/all_gather | solution.py:103
  94.3 0.0 copy-done.3
  94.3 0.0 copy-done.4
  94.3 6.8 %shard_map.28 = bf16[4,4,256,128]{3,2,1,0:T(8,128)(2,1)} custom-call(bf16[16,512,256]{2,1,0:T(8,128)(2,1)} %bitcast.15, bf16[4,4,256,128]{3,2,1,0:T(8,128)(2,1)} %copy-done.3, bf16[4,4,256,128]{3,2,1,0:T(8,128)(2,1)} %copy-done.4), custom_call_target="tpu_custom_call" | custom-call | flops 2147483648 | bytes 7340032 | tf_op jit(solution)/shard_map/pallas_call | solution.py:60
  101.1 7.3 %all-to-all-start.1 = ((bf16[16,256,128]{2,1,0:T(8,128)(2,1)}), bf16[16,256,128]{2,1,0:T(8,128)(2,1)S(1)}, u32[]{:S(2)}, u32[]{:S(2)}) async-start(bf16[16,256,128]{2,1,0:T(8,128)(2,1)} %bitcast.23), calls=%async_computation.1 | async-start | bytes 2097152 | tf_op jit(solution)/shard_map/all_to_all | solution.py:119
  108.5 11.0 %all-to-all-done.1 = bf16[16,256,128]{2,1,0:T(8,128)(2,1)S(1)} async-done(((bf16[16,256,128]{2,1,0:T(8,128)(2,1)}), bf16[16,256,128]{2,1,0:T(8,128)(2,1)S(1)}, u32[]{:S(2)}, u32[]{:S(2)}) %all-to-all-start.1) | async-done | bytes 1048608 | tf_op jit(solution)/shard_map/all_to_all | solution.py:119
  119.4 0.0 copy-start
  119.4 0.2 convert_reduce_fusion
  119.6 0.2 fusion.1
  119.8 0.2 broadcast_in_dim.16
  120.0 16.1 %all_to_all.26 = bf16[16,256,128]{2,1,0:T(8,128)(2,1)S(1)} all-to-all(bf16[16,256,128]{2,1,0:T(8,128)(2,1)S(1)} %bitcast.21), channel_id=1, replica_groups=mesh['x'=4,'zl'=8,'y'=4,'zh'=2,'c'=2] {'x','y'}, dimensions={0} | all-to-all | bytes 2097152 | tf_op jit(solution)/shard_map/all_to_all | solution.py:124
  136.1 1.9 collective-permute-start.3
  138.0 2.6 %collective-permute-done.3.other_ref = bf16[4,4,256,128]{3,2,1,0:T(8,128)(2,1)S(1)} collective-permute-done((bf16[4,4,256,128]{3,2,1,0:T(8,128)(2,1)S(1)}, bf16[4,4,256,128]{3,2,1,0:T(8,128)(2,1)S(1)}, u32[]{:S(2)}, u32[]{:S(2)}) %collective-permute-start.3) | collective-permute-done | bytes 1048608 | tf_op jit(solution)/shard_map/ppermute | solution.py:79
  140.6 0.0 copy-done
  140.6 2.6 %shard_map.30 = bf16[4,2,256,128]{3,2,1,0:T(8,128)(2,1)} custom-call(bf16[16,512,256]{2,1,0:T(8,128)(2,1)S(1)} %bitcast.16, bf16[4,4,256,128]{3,2,1,0:T(8,128)(2,1)S(1)} %bitcast.19, bf16[4,4,256,128]{3,2,1,0:T(8,128)(2,1)S(1)} %collective-permute-done.3.other_ref), custom_call_target="tpu_custom_call" | custom-call | flops 1073741824 | bytes 5242880 | tf_op jit(solution)/shard_map/pallas_call | solution.py:60
  143.2 5.7 %all-to-all-start.4 = ((bf16[4,2,256,128]{3,2,1,0:T(8,128)(2,1)}), bf16[4,2,256,128]{3,2,1,0:T(8,128)(2,1)S(1)}, u32[]{:S(2)}, u32[]{:S(2)}) async-start(bf16[4,2,256,128]{3,2,1,0:T(8,128)(2,1)} %shard_map.30), calls=%async_computation.4 | async-start | bytes 1048576 | tf_op jit(solution)/shard_map/all_to_all | solution.py:129
  149.0 0.0 copy-start.1
  149.0 2.2 %copy-done.1 = bf16[8192,256]{1,0:T(8,128)(2,1)S(1)} copy-done((bf16[8192,256]{1,0:T(8,128)(2,1)S(1)}, bf16[8192,256]{1,0:T(8,128)(2,1)}, u32[]{:S(2)}) %copy-start.1) | copy-done | bytes 4194328
  151.2 0.0 copy-start.2
  151.2 2.6 %shard_map.29 = bf16[4,2,256,128]{3,2,1,0:T(8,128)(2,1)} custom-call(bf16[16,512,256]{2,1,0:T(8,128)(2,1)S(1)} %bitcast.17, bf16[4,4,256,128]{3,2,1,0:T(8,128)(2,1)S(1)} %bitcast.20, bf16[4,4,256,128]{3,2,1,0:T(8,128)(2,1)S(1)} %collective-permute-done.3.other_ref), custom_call_target="tpu_custom_call" | custom-call | flops 1073741824 | bytes 5242880 | tf_op jit(solution)/shard_map/pallas_call | solution.py:60
  153.7 3.9 %all-to-all-done.4 = bf16[4,2,256,128]{3,2,1,0:T(8,128)(2,1)S(1)} async-done(((bf16[4,2,256,128]{3,2,1,0:T(8,128)(2,1)}), bf16[4,2,256,128]{3,2,1,0:T(8,128)(2,1)S(1)}, u32[]{:S(2)}, u32[]{:S(2)}) %all-to-all-start.4) | async-done | bytes 524320 | tf_op jit(solution)/shard_map/all_to_all | solution.py:129
  157.6 4.9 %all-to-all-start.3 = ((bf16[4,2,256,128]{3,2,1,0:T(8,128)(2,1)}), bf16[4,2,256,128]{3,2,1,0:T(8,128)(2,1)S(1)}, u32[]{:S(2)}, u32[]{:S(2)}) async-start(bf16[4,2,256,128]{3,2,1,0:T(8,128)(2,1)} %shard_map.29), calls=%async_computation.3 | async-start | bytes 1048576 | tf_op jit(solution)/shard_map/all_to_all | solution.py:129
  162.5 0.1 reduce_sum.32
  162.6 7.3 %collective-permute-start.4 = (bf16[512,128]{1,0:T(8,128)(2,1)S(1)}, bf16[512,128]{1,0:T(8,128)(2,1)S(1)}, u32[]{:S(2)}, u32[]{:S(2)}) collective-permute-start(bf16[512,128]{1,0:T(8,128)(2,1)S(1)} %bitcast.25), channel_id=1, source_target_pairs={{0,2},{2,0},{1,3},{3,1},{4,6},{6,4},{5,7},{7,5},{8,10},{10,8},{9,1... | collective-permute-start | bytes 393224 | tf_op jit(solution)/shard_map/ppermute | solution.py:132
  169.8 0.4 all-to-all-done.3
  170.3 0.1 convert_reduce_fusion.1
  170.4 15.0 %collective-permute-done.4 = bf16[512,128]{1,0:T(8,128)(2,1)S(1)} collective-permute-done((bf16[512,128]{1,0:T(8,128)(2,1)S(1)}, bf16[512,128]{1,0:T(8,128)(2,1)S(1)}, u32[]{:S(2)}, u32[]{:S(2)}) %collective-permute-start.4) | collective-permute-done | bytes 131104 | tf_op jit(solution)/shard_map/ppermute | solution.py:132
  185.4 0.0 copy-done.2
  185.4 0.9 maximum_add_fusion
  (6 shorter events, 0.1 us)
Async XLA Ops:
  6.5 87.7 %all-gather.3.cloned.1.call-start = ((), (), s32[]{:S(2)}) async-start(), calls=%async_computation.5 | async-start | bytes 4456448 | tf_op jit(solution)/shard_map/all_gather | solution.py:103
  9.4 19.5 %collective-permute-start = (bf16[512,128]{1,0:T(8,128)(2,1)S(1)}, bf16[512,128]{1,0:T(8,128)(2,1)S(1)}, u32[]{:S(2)}, u32[]{:S(2)}) collective-permute-start(bf16[512,128]{1,0:T(8,128)(2,1)S(1)} %broadcast_select_fusion), channel_id=1, source_target_pairs={{0,2},{2,0},{1,3},{3,1},{4,6},{6,4},{5,7},{7,5},{8,10},{10,8},{9,1... | collective-permute-start | bytes 393224 | tf_op jit(solution)/shard_map/ppermute | solution.py:110
  29.0 12.5 %collective-permute-start.1 = (bf16[4,256,128]{2,1,0:T(8,128)(2,1)S(1)}, bf16[4,256,128]{2,1,0:T(8,128)(2,1)S(1)}, u32[]{:S(2)}, u32[]{:S(2)}) collective-permute-start(bf16[4,256,128]{2,1,0:T(8,128)(2,1)S(1)} %bitcast.24), channel_id=1, source_target_pairs={{0,0},{4,128},{8,256},{12,384},{128,4},{132,132},{136,260},{140,38... | collective-permute-start | bytes 786440 | tf_op jit(solution)/shard_map/ppermute | solution.py:115
  61.7 32.6 %copy-start.3 = (bf16[4,4,256,128]{3,2,1,0:T(8,128)(2,1)}, bf16[4,4,256,128]{3,2,1,0:T(8,128)(2,1)S(1)}, u32[]{:S(2)}) copy-start(bf16[4,4,256,128]{3,2,1,0:T(8,128)(2,1)S(1)} %all_to_all.25.own_ref) | copy-start | bytes 3145732
  61.7 4.5 %collective-permute-start.2 = (bf16[4,4,256,128]{3,2,1,0:T(8,128)(2,1)S(1)}, bf16[4,4,256,128]{3,2,1,0:T(8,128)(2,1)S(1)}, u32[]{:S(2)}, u32[]{:S(2)}) collective-permute-start(bf16[4,4,256,128]{3,2,1,0:T(8,128)(2,1)S(1)} %all_to_all.25.own_ref), channel_id=1, source_target_pairs={{0,1},{1,0},{2,3},{3,2},{4,5},{5,4},{6,7},{7,6},{8,9},{9,8},{10,11... | collective-permute-start | bytes 3145736 | tf_op jit(solution)/shard_map/ppermute | solution.py:79
  66.2 28.1 %copy-start.4 = (bf16[4,4,256,128]{3,2,1,0:T(8,128)(2,1)}, bf16[4,4,256,128]{3,2,1,0:T(8,128)(2,1)S(1)}, u32[]{:S(2)}) copy-start(bf16[4,4,256,128]{3,2,1,0:T(8,128)(2,1)S(1)} %collective-permute-done.2.other_ref) | copy-start | bytes 3145732
  101.1 18.3 %all-to-all-start.1 = ((bf16[16,256,128]{2,1,0:T(8,128)(2,1)}), bf16[16,256,128]{2,1,0:T(8,128)(2,1)S(1)}, u32[]{:S(2)}, u32[]{:S(2)}) async-start(bf16[16,256,128]{2,1,0:T(8,128)(2,1)} %bitcast.23), calls=%async_computation.1 | async-start | bytes 2097152 | tf_op jit(solution)/shard_map/all_to_all | solution.py:119
  119.4 21.2 %copy-start = (bf16[8192,256]{1,0:T(8,128)(2,1)S(1)}, bf16[8192,256]{1,0:T(8,128)(2,1)}, u32[]{:S(2)}) copy-start(bf16[8192,256]{1,0:T(8,128)(2,1)} %all-gather.3.cloned.1.call-done) | copy-start | bytes 12582916
  136.1 4.5 %collective-permute-start.3 = (bf16[4,4,256,128]{3,2,1,0:T(8,128)(2,1)S(1)}, bf16[4,4,256,128]{3,2,1,0:T(8,128)(2,1)S(1)}, u32[]{:S(2)}, u32[]{:S(2)}) collective-permute-start(bf16[4,4,256,128]{3,2,1,0:T(8,128)(2,1)S(1)} %bitcast.18), channel_id=1, source_target_pairs={{0,1},{1,0},{2,3},{3,2},{4,5},{5,4},{6,7},{7,6},{8,9},{9,8},{10,11... | collective-permute-start | bytes 3145736 | tf_op jit(solution)/shard_map/ppermute | solution.py:79
  143.2 14.4 %all-to-all-start.4 = ((bf16[4,2,256,128]{3,2,1,0:T(8,128)(2,1)}), bf16[4,2,256,128]{3,2,1,0:T(8,128)(2,1)S(1)}, u32[]{:S(2)}, u32[]{:S(2)}) async-start(bf16[4,2,256,128]{3,2,1,0:T(8,128)(2,1)} %shard_map.30), calls=%async_computation.4 | async-start | bytes 1048576 | tf_op jit(solution)/shard_map/all_to_all | solution.py:129
  149.0 2.2 %copy-start.1 = (bf16[8192,256]{1,0:T(8,128)(2,1)S(1)}, bf16[8192,256]{1,0:T(8,128)(2,1)}, u32[]{:S(2)}) copy-start(bf16[8192,256]{1,0:T(8,128)(2,1)} %all-gather.3.cloned.1.call-done) | copy-start | bytes 12582916
  151.2 34.2 %copy-start.2 = (f32[512,256]{1,0:T(8,128)S(1)}, f32[512,256]{1,0:T(8,128)}, u32[]{:S(2)}) copy-start(f32[512,256]{1,0:T(8,128)} %param.2) | copy-start | bytes 1572868
  157.6 12.7 %all-to-all-start.3 = ((bf16[4,2,256,128]{3,2,1,0:T(8,128)(2,1)}), bf16[4,2,256,128]{3,2,1,0:T(8,128)(2,1)S(1)}, u32[]{:S(2)}, u32[]{:S(2)}) async-start(bf16[4,2,256,128]{3,2,1,0:T(8,128)(2,1)} %shard_map.29), calls=%async_computation.3 | async-start | bytes 1048576 | tf_op jit(solution)/shard_map/all_to_all | solution.py:129
  162.6 22.8 %collective-permute-start.4 = (bf16[512,128]{1,0:T(8,128)(2,1)S(1)}, bf16[512,128]{1,0:T(8,128)(2,1)S(1)}, u32[]{:S(2)}, u32[]{:S(2)}) collective-permute-start(bf16[512,128]{1,0:T(8,128)(2,1)S(1)} %bitcast.25), channel_id=1, source_target_pairs={{0,2},{2,0},{1,3},{3,1},{4,6},{6,4},{5,7},{7,5},{8,10},{10,8},{9,1... | collective-permute-start | bytes 393224 | tf_op jit(solution)/shard_map/ppermute | solution.py:132
Sparse Core Ops, SparseCore 0:
  9.4 84.8 all-gather.2

commit v6 on v5

--- a/solution.py
+++ b/solution.py
@@ -29,47 +29,79 @@
 def dot_kernel(flips, z_ref, own_ref, other_ref, out_ref, left, sem):
     groups, _, depth, width = own_ref.shape
     c = lax.axis_index("c")
-    firsts = [0, 8] if flips is None else [(lax.axis_index("zh") ^ flips) * 8]
+    first = (lax.axis_index("zh") ^ flips) * 8
     copies = []
-    for b, first in enumerate(firsts):
-        for n in range(8):
-            chunk = (n % 4) // 2 * 4 + (c ^ (n // 4)) * 2 + n % 2
-            copies.append(
-                pltpu.make_async_copy(z_ref.at[first + chunk], left.at[b * 8 + n], sem.at[b * 8 + n])
-            )
+    for n in range(8):
+        chunk = (n % 4) // 2 * 4 + (c ^ (n // 4)) * 2 + n % 2
+        copies.append(pltpu.make_async_copy(z_ref.at[first + chunk], left.at[n], sem.at[n]))
     for copy in copies:
         copy.start()
-    for s in range(out_ref.shape[1]):
-        b, rows = s // 2, slice(s % 2 * depth, (s % 2 + 1) * depth)
+    for s in range(2):
         total = None
         for n in range(8):
-            if s % 2 == 0:
-                copies[b * 8 + n].wait()
+            if s == 0:
+                copies[n].wait()
             part = (own_ref, other_ref)[n // 4]
             right = jnp.concatenate([part[j, n % 4] for j in range(groups)], axis=1)
-            term = jnp.dot(left[b * 8 + n, rows, :], right, preferred_element_type=jnp.float32)
+            rows = left[n, s * depth : (s + 1) * depth, :]
+            term = jnp.dot(rows, right, preferred_element_type=jnp.float32)
             total = term if total is None else total + term
         for j in range(groups):
             out_ref[j, s] = total[:, j * width : (j + 1) * width].astype(out_ref.dtype)
 
 
+def dot_all_kernel(z_ref, own_ref, other_ref, out_ref, right):
+    groups, _, depth, width = own_ref.shape
+    c = lax.axis_index("c")
+
+    @pl.when(pl.program_id(0) == 0)
+    def _():
+        for ref, core in ((own_ref, c), (other_ref, 1 - c)):
+            for n in range(4):
+                for j in range(groups):
+                    right[n // 2 * 4 + core * 2 + n % 2, :, j * width : (j + 1) * width] = ref[j, n]
+
+    total = jnp.dot(z_ref[0], right[0], preferred_element_type=jnp.float32)
+    for k in range(1, 8):
+        total += jnp.dot(z_ref[k], right[k], preferred_element_type=jnp.float32)
+    for j in range(groups):
+        out_ref[j, 0] = total[:, j * width : (j + 1) * width].astype(out_ref.dtype)
+
+
+def dot_right_all(z_rows, own, other):
+    groups, steps, depth, width = own.shape
+    whole = pl.BlockSpec(own.shape, lambda s: (0, 0, 0, 0))
+    return pl.pallas_call(
+        dot_all_kernel,
+        grid=(steps,),
+        in_specs=[pl.BlockSpec((8, depth, depth), lambda s: (s // 2, s % 2, 0)), whole, whole],
+        out_specs=pl.BlockSpec((groups, 1, depth, width), lambda s: (0, s, 0, 0)),
+        out_shape=jax.ShapeDtypeStruct(own.shape, jnp.bfloat16),
+        scratch_shapes=[pltpu.VMEM((8, depth, groups * width), jnp.bfloat16)],
+        compiler_params=pltpu.CompilerParams(vmem_limit_bytes=56 * 2**20),
+        cost_estimate=pl.CostEstimate(
+            flops=2 * z_rows.size * groups * width,
+            bytes_accessed=2 * (z_rows.size + 3 * own.size),
+            transcendentals=0,
+        ),
+    )(z_rows, own, other)
+
+
 def dot_right(flips, z_rows, own, other):
     groups, steps, depth, width = own.shape
-    chunks = 16 if flips is None else 8
-    steps = chunks // 4
     return pl.pallas_call(
         functools.partial(dot_kernel, flips),
         in_specs=[pl.BlockSpec(memory_space=pl.ANY)] + [pl.BlockSpec(memory_space=pltpu.VMEM)] * 2,
         out_specs=pl.BlockSpec(memory_space=pltpu.VMEM),
-        out_shape=jax.ShapeDtypeStruct((groups, steps, depth, width), jnp.bfloat16),
+        out_shape=jax.ShapeDtypeStruct((groups, 2, depth, width), jnp.bfloat16),
         scratch_shapes=[
-            pltpu.VMEM((chunks,) + z_rows.shape[1:], jnp.bfloat16),
-            pltpu.SemaphoreType.DMA((chunks,)),
+            pltpu.VMEM((8,) + z_rows.shape[1:], jnp.bfloat16),
+            pltpu.SemaphoreType.DMA((8,)),
         ],
-        compiler_params=pltpu.CompilerParams(vmem_limit_bytes=(56 if flips is None else 32) * 2**20),
+        compiler_params=pltpu.CompilerParams(vmem_limit_bytes=32 * 2**20),
         cost_estimate=pl.CostEstimate(
-            flops=2 * z_rows.size * groups * width * chunks // 16,
-            bytes_accessed=2 * (z_rows.size * chunks // 16 + 3 * own.size),
+            flops=z_rows.size * groups * width,
+            bytes_accessed=z_rows.size + 5 * own.size,
             transcendentals=0,
         ),
     )(z_rows, own, other)
@@ -114,7 +146,7 @@
     turn = [(i * 4 + j, j * 4 + i) for i in range(4) for j in range(4)]
     turned = lax.ppermute(y_both, PLANE, turn)
     y_own = lax.all_to_all(jnp.stack([turned] * 4), "y", 0, 0, tiled=True)
-    part = dot_right(None, z_rows, y_own, other_core(y_own))
+    part = dot_right_all(z_rows, y_own, other_core(y_own))
 
     part = lax.all_to_all(part.reshape(16, 256, 128), PLANE, 0, 0, tiled=True)
     product = part.reshape(4, 4, 256, 128).astype(jnp.float32).sum(0)
@@ -124,13 +156,14 @@
     own = lax.all_to_all(spread, PLANE, 0, 0, tiled=True).reshape(4, 4, 256, 128)
     other = other_core(own)
 
-    def result(flips):
-        part = dot_right(flips, z_rows, own, other)
+    def sum_x(part):
         part = lax.all_to_all(part, "x", 0, 0, tiled=True)
         return part.astype(jnp.float32).sum(0).reshape(512, 128)
 
-    yours = lax.ppermute(result(1).astype(jnp.bfloat16), "zh", SWAP).astype(jnp.float32)
-    mine = result(0)
+    yours = sum_x(dot_right(1, z_rows, own, other)).astype(jnp.bfloat16)
+    mine = dot_right(0, z_rows, own, other)
+    yours = lax.ppermute(yours, "zh", SWAP).astype(jnp.float32)
+    mine = sum_x(mine)
     part = jnp.concatenate([jnp.where(low, mine, yours), jnp.where(low, yours, mine)], axis=1)
     return 1.5 * z_half.astype(jnp.float32) + part
 

time: 194 us -> 193 us (level)
    pallas_call x3 -> x2, Pallas kernels: 12 us -> 5.16 us  [dot_right(): pl.pallas_call(functools.partial(dot_kernel, flips), in_specs=[pl.BlockSp...]
    pallas_call x0 -> x1, Pallas kernels: none -> 6.56 us  [dot_right_all(): pl.pallas_call(dot_all_kernel, grid=(steps,), in_specs=[pl.BlockSpec((8,...]
where the time goes in v6:
time: 193 us
  waiting for transfers between devices  76.3 us (40%)
  starting transfers between devices  48.2 us (25%)
  blocking collectives  36 us (19%)
  between operations  13.5 us (7%)
  Pallas kernels  11.7 us (6%)
  other arithmetic  4.36 us (2%)
  local copies, waits for them, and re-layouts  2.6 us (1%)
    all_gather x1, waiting for transfers between devices, shards(): z_rows = lax.all_gather(z_half, AXES, axis_index_groups=Z_RINGS)  28.1 us
    all_to_all x1, blocking collectives, shards(): y_own = lax.all_to_all(jnp.stack([turned] * 4), 'y', 0, 0, tiled=True)  19.9 us
    all_to_all x1, blocking collectives, shards(): lax.all_to_all(spread, PLANE, 0, 0, tiled=True).reshape(4, 4, 256, 128)  16.1 us
    ppermute x1, starting transfers between devices, shards(): yours = lax.ppermute(jnp.where(low, right, left), 'zh', SWAP)  15.7 us
    ppermute x1, waiting for transfers between devices, shards(): yours = lax.ppermute(yours, 'zh', SWAP).astype(jnp.float32)  15 us
    all_to_all x1, waiting for transfers between devices, shards(): part = lax.all_to_all(part.reshape(16, 256, 128), PLANE, 0, 0, tiled=True)  11 us
    all_to_all x2, starting transfers between devices, sum_x(): part = lax.all_to_all(part, 'x', 0, 0, tiled=True)  10.7 us
    ppermute x1, waiting for transfers between devices, shards(): turned = lax.ppermute(y_both, PLANE, turn)  9.07 us
  transfers between devices with their start and end apart: 9, of which 9 were waited for; matrix products, arithmetic and copies ran while one was open for 1% of the time, Pallas kernels for 1%

profile of v6, /device:TPU:2, one launch (start us, length us, event | category | flops | bytes accessed | tf_op | source)
XLA Modules:
  0.0 192.8 jit_solution(4829927510651416568)
XLA Ops:
  6.5 0.0 all-gather.3.cloned.1.call-start
  6.5 1.8 convert_element_type.33
  8.3 0.0 all-gather.3.cloned.1.call-update
  8.3 1.1 convert_element_type.35
  9.4 15.7 %collective-permute-start = (bf16[512,128]{1,0:T(8,128)(2,1)S(1)}, bf16[512,128]{1,0:T(8,128)(2,1)S(1)}, u32[]{:S(2)}, u32[]{:S(2)}) collective-permute-start(bf16[512,128]{1,0:T(8,128)(2,1)S(1)} %broadcast_select_fusion), channel_id=1, source_target_pairs={{0,2},{2,0},{1,3},{3,1},{4,6},{6,4},{5,7},{7,5},{8,10},{10,8},{9,1... | collective-permute-start | bytes 393224 | tf_op jit(solution)/shard_map/ppermute | solution.py:142
  25.2 3.8 %collective-permute-done = bf16[512,128]{1,0:T(8,128)(2,1)S(1)} collective-permute-done((bf16[512,128]{1,0:T(8,128)(2,1)S(1)}, bf16[512,128]{1,0:T(8,128)(2,1)S(1)}, u32[]{:S(2)}, u32[]{:S(2)}) %collective-permute-start) | collective-permute-done | bytes 131104 | tf_op jit(solution)/shard_map/ppermute | solution.py:142
  29.0 3.5 %collective-permute-start.1 = (bf16[4,256,128]{2,1,0:T(8,128)(2,1)S(1)}, bf16[4,256,128]{2,1,0:T(8,128)(2,1)S(1)}, u32[]{:S(2)}, u32[]{:S(2)}) collective-permute-start(bf16[4,256,128]{2,1,0:T(8,128)(2,1)S(1)} %bitcast.24), channel_id=1, source_target_pairs={{0,0},{4,128},{8,256},{12,384},{128,4},{132,132},{136,260},{140,38... | collective-permute-start | bytes 786440 | tf_op jit(solution)/shard_map/ppermute | solution.py:147
  32.5 9.1 %collective-permute-done.1 = bf16[4,256,128]{2,1,0:T(8,128)(2,1)S(1)} collective-permute-done((bf16[4,256,128]{2,1,0:T(8,128)(2,1)S(1)}, bf16[4,256,128]{2,1,0:T(8,128)(2,1)S(1)}, u32[]{:S(2)}, u32[]{:S(2)}) %collective-permute-start.1) | collective-permute-done | bytes 262176 | tf_op jit(solution)/shard_map/ppermute | solution.py:147
  41.6 0.2 stack.19
  41.8 19.9 %all_to_all.25.own_ref = bf16[4,4,256,128]{3,2,1,0:T(8,128)(2,1)S(1)} all-to-all(bf16[4,4,256,128]{3,2,1,0:T(8,128)(2,1)S(1)} %stack.19), channel_id=1, replica_groups=mesh['x'=4,'zl'=8,'y'=4,'zh'=2,'c'=2] {'y'}, dimensions={0} | all-to-all | bytes 2097152 | tf_op jit(solution)/shard_map/all_to_all | solution.py:148
  61.7 0.0 copy-start.3
  61.7 1.9 collective-permute-start.2
  63.6 2.6 %collective-permute-done.2.other_ref = bf16[4,4,256,128]{3,2,1,0:T(8,128)(2,1)S(1)} collective-permute-done((bf16[4,4,256,128]{3,2,1,0:T(8,128)(2,1)S(1)}, bf16[4,4,256,128]{3,2,1,0:T(8,128)(2,1)S(1)}, u32[]{:S(2)}, u32[]{:S(2)}) %collective-permute-start.2) | collective-permute-done | bytes 1048608 | tf_op jit(solution)/shard_map/ppermute | solution.py:111
  66.2 0.0 copy-start.4
  66.2 28.1 %all-gather.3.cloned.1.call-done = bf16[8192,256]{1,0:T(8,128)(2,1)} async-done(((bf16[512,256]{1,0:T(8,128)(2,1)}), bf16[8192,256]{1,0:T(8,128)(2,1)}) %all-gather.3.cloned.1.call-update) | async-done | bytes 4194320 | tf_op jit(solution)/shard_map/all_gather | solution.py:135
  94.3 0.0 copy-done.3
  94.3 0.0 copy-done.4
  94.3 6.6 %shard_map.28 = bf16[4,4,256,128]{3,2,1,0:T(8,128)(2,1)} custom-call(bf16[16,512,256]{2,1,0:T(8,128)(2,1)} %bitcast.15, bf16[4,4,256,128]{3,2,1,0:T(8,128)(2,1)} %copy-done.3, bf16[4,4,256,128]{3,2,1,0:T(8,128)(2,1)} %copy-done.4), custom_call_target="tpu_custom_call" | custom-call | flops 2147483648 | bytes 7340032 | tf_op jit(solution)/shard_map/pallas_call | solution.py:74
  100.9 7.3 %all-to-all-start.1 = ((bf16[16,256,128]{2,1,0:T(8,128)(2,1)}), bf16[16,256,128]{2,1,0:T(8,128)(2,1)S(1)}, u32[]{:S(2)}, u32[]{:S(2)}) async-start(bf16[16,256,128]{2,1,0:T(8,128)(2,1)} %bitcast.23), calls=%async_computation.1 | async-start | bytes 2097152 | tf_op jit(solution)/shard_map/all_to_all | solution.py:151
  108.2 11.0 %all-to-all-done.1 = bf16[16,256,128]{2,1,0:T(8,128)(2,1)S(1)} async-done(((bf16[16,256,128]{2,1,0:T(8,128)(2,1)}), bf16[16,256,128]{2,1,0:T(8,128)(2,1)S(1)}, u32[]{:S(2)}, u32[]{:S(2)}) %all-to-all-start.1) | async-done | bytes 1048608 | tf_op jit(solution)/shard_map/all_to_all | solution.py:151
  119.1 0.0 copy-start
  119.1 0.2 convert_reduce_fusion
  119.3 0.2 fusion.1
  119.5 0.2 broadcast_in_dim.16
  119.7 16.1 %all_to_all.26 = bf16[16,256,128]{2,1,0:T(8,128)(2,1)S(1)} all-to-all(bf16[16,256,128]{2,1,0:T(8,128)(2,1)S(1)} %bitcast.21), channel_id=1, replica_groups=mesh['x'=4,'zl'=8,'y'=4,'zh'=2,'c'=2] {'x','y'}, dimensions={0} | all-to-all | bytes 2097152 | tf_op jit(solution)/shard_map/all_to_all | solution.py:156
  135.8 1.9 collective-permute-start.3
  137.7 2.6 %collective-permute-done.3.other_ref = bf16[4,4,256,128]{3,2,1,0:T(8,128)(2,1)S(1)} collective-permute-done((bf16[4,4,256,128]{3,2,1,0:T(8,128)(2,1)S(1)}, bf16[4,4,256,128]{3,2,1,0:T(8,128)(2,1)S(1)}, u32[]{:S(2)}, u32[]{:S(2)}) %collective-permute-start.3) | collective-permute-done | bytes 1048608 | tf_op jit(solution)/shard_map/ppermute | solution.py:111
  140.4 0.0 copy-done
  140.4 2.6 %shard_map.30 = bf16[4,2,256,128]{3,2,1,0:T(8,128)(2,1)} custom-call(bf16[16,512,256]{2,1,0:T(8,128)(2,1)S(1)} %bitcast.16, bf16[4,4,256,128]{3,2,1,0:T(8,128)(2,1)S(1)} %bitcast.19, bf16[4,4,256,128]{3,2,1,0:T(8,128)(2,1)S(1)} %collective-permute-done.3.other_ref), custom_call_target="tpu_custom_call" | custom-call | flops 1073741824 | bytes 4718592 | tf_op jit(solution)/shard_map/pallas_call | solution.py:92
  143.0 5.8 %all-to-all-start.4 = ((bf16[4,2,256,128]{3,2,1,0:T(8,128)(2,1)}), bf16[4,2,256,128]{3,2,1,0:T(8,128)(2,1)S(1)}, u32[]{:S(2)}, u32[]{:S(2)}) async-start(bf16[4,2,256,128]{3,2,1,0:T(8,128)(2,1)} %shard_map.30), calls=%async_computation.4 | async-start | bytes 1048576 | tf_op jit(solution)/shard_map/all_to_all | solution.py:160
  148.7 0.0 copy-start.1
  148.7 2.2 %copy-done.1 = bf16[8192,256]{1,0:T(8,128)(2,1)S(1)} copy-done((bf16[8192,256]{1,0:T(8,128)(2,1)S(1)}, bf16[8192,256]{1,0:T(8,128)(2,1)}, u32[]{:S(2)}) %copy-start.1) | copy-done | bytes 4194328
  150.9 0.0 copy-start.2
  150.9 2.6 %shard_map.29 = bf16[4,2,256,128]{3,2,1,0:T(8,128)(2,1)} custom-call(bf16[16,512,256]{2,1,0:T(8,128)(2,1)S(1)} %bitcast.17, bf16[4,4,256,128]{3,2,1,0:T(8,128)(2,1)S(1)} %bitcast.20, bf16[4,4,256,128]{3,2,1,0:T(8,128)(2,1)S(1)} %collective-permute-done.3.other_ref), custom_call_target="tpu_custom_call" | custom-call | flops 1073741824 | bytes 4718592 | tf_op jit(solution)/shard_map/pallas_call | solution.py:92
  153.5 3.8 %all-to-all-done.4 = bf16[4,2,256,128]{3,2,1,0:T(8,128)(2,1)S(1)} async-done(((bf16[4,2,256,128]{3,2,1,0:T(8,128)(2,1)}), bf16[4,2,256,128]{3,2,1,0:T(8,128)(2,1)S(1)}, u32[]{:S(2)}, u32[]{:S(2)}) %all-to-all-start.4) | async-done | bytes 524320 | tf_op jit(solution)/shard_map/all_to_all | solution.py:160
  157.3 4.9 %all-to-all-start.3 = ((bf16[4,2,256,128]{3,2,1,0:T(8,128)(2,1)}), bf16[4,2,256,128]{3,2,1,0:T(8,128)(2,1)S(1)}, u32[]{:S(2)}, u32[]{:S(2)}) async-start(bf16[4,2,256,128]{3,2,1,0:T(8,128)(2,1)} %shard_map.29), calls=%async_computation.3 | async-start | bytes 1048576 | tf_op jit(solution)/shard_map/all_to_all | solution.py:160
  162.2 0.1 reduce_sum.32
  162.3 7.3 %collective-permute-start.4 = (bf16[512,128]{1,0:T(8,128)(2,1)S(1)}, bf16[512,128]{1,0:T(8,128)(2,1)S(1)}, u32[]{:S(2)}, u32[]{:S(2)}) collective-permute-start(bf16[512,128]{1,0:T(8,128)(2,1)S(1)} %bitcast.25), channel_id=1, source_target_pairs={{0,2},{2,0},{1,3},{3,1},{4,6},{6,4},{5,7},{7,5},{8,10},{10,8},{9,1... | collective-permute-start | bytes 393224 | tf_op jit(solution)/shard_map/ppermute | solution.py:165
  169.6 0.4 all-to-all-done.3
  169.9 0.1 convert_reduce_fusion.1
  170.0 15.0 %collective-permute-done.4 = bf16[512,128]{1,0:T(8,128)(2,1)S(1)} collective-permute-done((bf16[512,128]{1,0:T(8,128)(2,1)S(1)}, bf16[512,128]{1,0:T(8,128)(2,1)S(1)}, u32[]{:S(2)}, u32[]{:S(2)}) %collective-permute-start.4) | collective-permute-done | bytes 131104 | tf_op jit(solution)/shard_map/ppermute | solution.py:165
  185.0 0.0 copy-done.2
  185.1 0.9 maximum_add_fusion
  (6 shorter events, 0.1 us)
Async XLA Ops:
  6.5 87.7 %all-gather.3.cloned.1.call-start = ((), (), s32[]{:S(2)}) async-start(), calls=%async_computation.5 | async-start | bytes 4456448 | tf_op jit(solution)/shard_map/all_gather | solution.py:135
  9.4 19.5 %collective-permute-start = (bf16[512,128]{1,0:T(8,128)(2,1)S(1)}, bf16[512,128]{1,0:T(8,128)(2,1)S(1)}, u32[]{:S(2)}, u32[]{:S(2)}) collective-permute-start(bf16[512,128]{1,0:T(8,128)(2,1)S(1)} %broadcast_select_fusion), channel_id=1, source_target_pairs={{0,2},{2,0},{1,3},{3,1},{4,6},{6,4},{5,7},{7,5},{8,10},{10,8},{9,1... | collective-permute-start | bytes 393224 | tf_op jit(solution)/shard_map/ppermute | solution.py:142
  29.0 12.5 %collective-permute-start.1 = (bf16[4,256,128]{2,1,0:T(8,128)(2,1)S(1)}, bf16[4,256,128]{2,1,0:T(8,128)(2,1)S(1)}, u32[]{:S(2)}, u32[]{:S(2)}) collective-permute-start(bf16[4,256,128]{2,1,0:T(8,128)(2,1)S(1)} %bitcast.24), channel_id=1, source_target_pairs={{0,0},{4,128},{8,256},{12,384},{128,4},{132,132},{136,260},{140,38... | collective-permute-start | bytes 786440 | tf_op jit(solution)/shard_map/ppermute | solution.py:147
  61.7 32.6 %copy-start.3 = (bf16[4,4,256,128]{3,2,1,0:T(8,128)(2,1)}, bf16[4,4,256,128]{3,2,1,0:T(8,128)(2,1)S(1)}, u32[]{:S(2)}) copy-start(bf16[4,4,256,128]{3,2,1,0:T(8,128)(2,1)S(1)} %all_to_all.25.own_ref) | copy-start | bytes 3145732
  61.7 4.5 %collective-permute-start.2 = (bf16[4,4,256,128]{3,2,1,0:T(8,128)(2,1)S(1)}, bf16[4,4,256,128]{3,2,1,0:T(8,128)(2,1)S(1)}, u32[]{:S(2)}, u32[]{:S(2)}) collective-permute-start(bf16[4,4,256,128]{3,2,1,0:T(8,128)(2,1)S(1)} %all_to_all.25.own_ref), channel_id=1, source_target_pairs={{0,1},{1,0},{2,3},{3,2},{4,5},{5,4},{6,7},{7,6},{8,9},{9,8},{10,11... | collective-permute-start | bytes 3145736 | tf_op jit(solution)/shard_map/ppermute | solution.py:111
  66.2 28.1 %copy-start.4 = (bf16[4,4,256,128]{3,2,1,0:T(8,128)(2,1)}, bf16[4,4,256,128]{3,2,1,0:T(8,128)(2,1)S(1)}, u32[]{:S(2)}) copy-start(bf16[4,4,256,128]{3,2,1,0:T(8,128)(2,1)S(1)} %collective-permute-done.2.other_ref) | copy-start | bytes 3145732
  100.9 18.3 %all-to-all-start.1 = ((bf16[16,256,128]{2,1,0:T(8,128)(2,1)}), bf16[16,256,128]{2,1,0:T(8,128)(2,1)S(1)}, u32[]{:S(2)}, u32[]{:S(2)}) async-start(bf16[16,256,128]{2,1,0:T(8,128)(2,1)} %bitcast.23), calls=%async_computation.1 | async-start | bytes 2097152 | tf_op jit(solution)/shard_map/all_to_all | solution.py:151
  119.1 21.2 %copy-start = (bf16[8192,256]{1,0:T(8,128)(2,1)S(1)}, bf16[8192,256]{1,0:T(8,128)(2,1)}, u32[]{:S(2)}) copy-start(bf16[8192,256]{1,0:T(8,128)(2,1)} %all-gather.3.cloned.1.call-done) | copy-start | bytes 12582916
  135.8 4.5 %collective-permute-start.3 = (bf16[4,4,256,128]{3,2,1,0:T(8,128)(2,1)S(1)}, bf16[4,4,256,128]{3,2,1,0:T(8,128)(2,1)S(1)}, u32[]{:S(2)}, u32[]{:S(2)}) collective-permute-start(bf16[4,4,256,128]{3,2,1,0:T(8,128)(2,1)S(1)} %bitcast.18), channel_id=1, source_target_pairs={{0,1},{1,0},{2,3},{3,2},{4,5},{5,4},{6,7},{7,6},{8,9},{9,8},{10,11... | collective-permute-start | bytes 3145736 | tf_op jit(solution)/shard_map/ppermute | solution.py:111
  143.0 14.3 %all-to-all-start.4 = ((bf16[4,2,256,128]{3,2,1,0:T(8,128)(2,1)}), bf16[4,2,256,128]{3,2,1,0:T(8,128)(2,1)S(1)}, u32[]{:S(2)}, u32[]{:S(2)}) async-start(bf16[4,2,256,128]{3,2,1,0:T(8,128)(2,1)} %shard_map.30), calls=%async_computation.4 | async-start | bytes 1048576 | tf_op jit(solution)/shard_map/all_to_all | solution.py:160
  148.7 2.2 %copy-start.1 = (bf16[8192,256]{1,0:T(8,128)(2,1)S(1)}, bf16[8192,256]{1,0:T(8,128)(2,1)}, u32[]{:S(2)}) copy-start(bf16[8192,256]{1,0:T(8,128)(2,1)} %all-gather.3.cloned.1.call-done) | copy-start | bytes 12582916
  150.9 34.1 %copy-start.2 = (f32[512,256]{1,0:T(8,128)S(1)}, f32[512,256]{1,0:T(8,128)}, u32[]{:S(2)}) copy-start(f32[512,256]{1,0:T(8,128)} %param.2) | copy-start | bytes 1572868
  157.3 12.6 %all-to-all-start.3 = ((bf16[4,2,256,128]{3,2,1,0:T(8,128)(2,1)}), bf16[4,2,256,128]{3,2,1,0:T(8,128)(2,1)S(1)}, u32[]{:S(2)}, u32[]{:S(2)}) async-start(bf16[4,2,256,128]{3,2,1,0:T(8,128)(2,1)} %shard_map.29), calls=%async_computation.3 | async-start | bytes 1048576 | tf_op jit(solution)/shard_map/all_to_all | solution.py:160
  162.3 22.7 %collective-permute-start.4 = (bf16[512,128]{1,0:T(8,128)(2,1)S(1)}, bf16[512,128]{1,0:T(8,128)(2,1)S(1)}, u32[]{:S(2)}, u32[]{:S(2)}) collective-permute-start(bf16[512,128]{1,0:T(8,128)(2,1)S(1)} %bitcast.25), channel_id=1, source_target_pairs={{0,2},{2,0},{1,3},{3,1},{4,6},{6,4},{5,7},{7,5},{8,10},{10,8},{9,1... | collective-permute-start | bytes 393224 | tf_op jit(solution)/shard_map/ppermute | solution.py:165
Sparse Core Ops, SparseCore 0:
  9.4 84.8 all-gather.2

commit v7 on v6

--- a/solution.py
+++ b/solution.py
@@ -50,41 +50,51 @@
             out_ref[j, s] = total[:, j * width : (j + 1) * width].astype(out_ref.dtype)
 
 
-def dot_all_kernel(z_ref, own_ref, other_ref, out_ref, right):
-    groups, _, depth, width = own_ref.shape
-    c = lax.axis_index("c")
-
-    @pl.when(pl.program_id(0) == 0)
-    def _():
-        for ref, core in ((own_ref, c), (other_ref, 1 - c)):
-            for n in range(4):
-                for j in range(groups):
-                    right[n // 2 * 4 + core * 2 + n % 2, :, j * width : (j + 1) * width] = ref[j, n]
-
-    total = jnp.dot(z_ref[0], right[0], preferred_element_type=jnp.float32)
-    for k in range(1, 8):
-        total += jnp.dot(z_ref[k], right[k], preferred_element_type=jnp.float32)
-    for j in range(groups):
-        out_ref[j, 0] = total[:, j * width : (j + 1) * width].astype(out_ref.dtype)
+def dot_all_kernel(z_ref, right_ref, out_ref, left, sem):
+    groups, _, depth, width = out_ref.shape
+    copies = [pltpu.make_async_copy(z_ref.at[n], left.at[n], sem.at[n]) for n in range(16)]
+    for copy in copies:
+        copy.start()
+    for zh in range(2):
+        for h in range(2):
+            cols = slice(h * 2 * width, (h + 1) * 2 * width)
+            total = None
+            for k in range(8):
+                if h == 0:
+                    copies[zh * 8 + k].wait()
+                term = jnp.dot(
+                    left[zh * 8 + k], right_ref[k, :, cols], preferred_element_type=jnp.float32
+                )
+                total = term if total is None else total + term
+            total = total.astype(out_ref.dtype)
+            for s in range(2):
+                for j in range(2):
+                    block = total[s * depth : (s + 1) * depth, j * width : (j + 1) * width]
+                    out_ref[h * 2 + j, zh * 2 + s] = block
 
 
 def dot_right_all(z_rows, own, other):
     groups, steps, depth, width = own.shape
-    whole = pl.BlockSpec(own.shape, lambda s: (0, 0, 0, 0))
+    first = lax.axis_index("c") == 0
+    right = jnp.stack([jnp.where(first, own, other), jnp.where(first, other, own)])
+    right = right.reshape(2, groups, 2, 2, depth, width).transpose(2, 0, 3, 4, 1, 5)
+    right = right.reshape(8, depth, groups * width)
     return pl.pallas_call(
         dot_all_kernel,
-        grid=(steps,),
-        in_specs=[pl.BlockSpec((8, depth, depth), lambda s: (s // 2, s % 2, 0)), whole, whole],
-        out_specs=pl.BlockSpec((groups, 1, depth, width), lambda s: (0, s, 0, 0)),
+        in_specs=[pl.BlockSpec(memory_space=pl.ANY), pl.BlockSpec(memory_space=pltpu.VMEM)],
+        out_specs=pl.BlockSpec(memory_space=pltpu.VMEM),
         out_shape=jax.ShapeDtypeStruct(own.shape, jnp.bfloat16),
-        scratch_shapes=[pltpu.VMEM((8, depth, groups * width), jnp.bfloat16)],
-        compiler_params=pltpu.CompilerParams(vmem_limit_bytes=56 * 2**20),
+        scratch_shapes=[
+            pltpu.VMEM(z_rows.shape, jnp.bfloat16),
+            pltpu.SemaphoreType.DMA((16,)),
+        ],
+        compiler_params=pltpu.CompilerParams(vmem_limit_bytes=48 * 2**20),
         cost_estimate=pl.CostEstimate(
             flops=2 * z_rows.size * groups * width,
             bytes_accessed=2 * (z_rows.size + 3 * own.size),
             transcendentals=0,
         ),
-    )(z_rows, own, other)
+    )(z_rows, right)
 
 
 def dot_right(flips, z_rows, own, other):
@@ -111,18 +121,21 @@
     return lax.ppermute(block, "c", SWAP)
 
 
-def make_shift(product, order, first_col):
+def make_ident(shape, first_col):
     at = lax.axis_index
-    rows = product.shape[1]
+    rows = shape[1]
     row_ids = (
-        lax.broadcasted_iota(jnp.int32, product.shape, 0) * 2048
+        lax.broadcasted_iota(jnp.int32, shape, 0) * 2048
         + at("y") // 2 * 1024
         + at("c") * 512
         + at("y") % 2 * rows
-        + lax.broadcasted_iota(jnp.int32, product.shape, 1)
+        + lax.broadcasted_iota(jnp.int32, shape, 1)
     )
-    col_ids = first_col + lax.broadcasted_iota(jnp.int32, product.shape, 2)
-    ident = jnp.where(row_ids == col_ids, 1.5, 0.0).astype(jnp.float32)
+    col_ids = first_col + lax.broadcasted_iota(jnp.int32, shape, 2)
+    return jnp.where(row_ids == col_ids, 1.5, 0.0).astype(jnp.float32)
+
+
+def make_shift(product, order, ident):
     poly = lax.reduce_precision(ident - 0.5 / order * product, 8, 7)
     return (poly - ident).astype(jnp.bfloat16)
 
@@ -146,11 +159,13 @@
     turn = [(i * 4 + j, j * 4 + i) for i in range(4) for j in range(4)]
     turned = lax.ppermute(y_both, PLANE, turn)
     y_own = lax.all_to_all(jnp.stack([turned] * 4), "y", 0, 0, tiled=True)
-    part = dot_right_all(z_rows, y_own, other_core(y_own))
+    y_other = other_core(y_own)
+    y_other, ident = lax.optimization_barrier((y_other, make_ident((4, 256, 128), first_col)))
+    part = dot_right_all(z_rows, y_own, y_other)
 
     part = lax.all_to_all(part.reshape(16, 256, 128), PLANE, 0, 0, tiled=True)
     product = part.reshape(4, 4, 256, 128).astype(jnp.float32).sum(0)
-    shift = make_shift(product, order, first_col)
+    shift = make_shift(product, order, ident)
 
     spread = jnp.broadcast_to(shift[:, None], (4, 4, 256, 128)).reshape(16, 256, 128)
     own = lax.all_to_all(spread, PLANE, 0, 0, tiled=True).reshape(4, 4, 256, 128)

time: 193 us -> 193 us (level)
  waiting for transfers between devices: 76.3 us -> 57.9 us
  blocking collectives: 36 us -> 54.1 us
  starting transfers between devices: 48.2 us -> 40.9 us
  local copies, waits for them, and re-layouts: 2.6 us -> 6.97 us
  other arithmetic: 4.36 us -> 7.33 us
    all_to_all x0 -> x1, blocking collectives: none -> 17.8 us  [shards(): part = lax.all_to_all(part.reshape(16, 256, 128), PLANE, 0, 0, tiled=True)]
    all_to_all x1 -> x0, waiting for transfers between devices: 11 us -> none  [shards(): part = lax.all_to_all(part.reshape(16, 256, 128), PLANE, 0, 0, tiled=True)]
    all_gather x1, waiting for transfers between devices: 28.1 us -> 20.7 us  [shards(): z_rows = lax.all_gather(z_half, AXES, axis_index_groups=Z_RINGS)]
    all_to_all x1 -> x0, starting transfers between devices: 7.3 us -> none  [shards(): part = lax.all_to_all(part.reshape(16, 256, 128), PLANE, 0, 0, tiled=True)]
    transpose x0 -> x1, other arithmetic: none -> 2.83 us  [dot_right_all(): right.reshape(2, groups, 2, 2, depth, width).transpose(2, 0, 3, 4, 1, 5)]
    reshape x0 -> x1, local copies, waits for them, and re-layouts: none -> 2.75 us  [dot_right_all(): right = right.reshape(8, depth, groups * width)]
  transfers between devices with their start and end apart: 9 -> 8, of which waited for: 9 -> 8; matrix products, arithmetic and copies ran while one was open for 1% -> 5% of each run, Pallas kernels for 1% -> 1%
where the time goes in v7:
time: 193 us; the launch traced here: 192 us
  waiting for transfers between devices  57.9 us (30%)
  blocking collectives  54.1 us (28%)
  starting transfers between devices  40.9 us (21%)
  between operations  13.6 us (7%)
  Pallas kernels  11.1 us (6%)
  other arithmetic  7.33 us (4%)
  local copies, waits for them, and re-layouts  6.97 us (4%)
    all_gather x1, waiting for transfers between devices, shards(): z_rows = lax.all_gather(z_half, AXES, axis_index_groups=Z_RINGS)  20.7 us
    all_to_all x1, blocking collectives, shards(): y_own = lax.all_to_all(jnp.stack([turned] * 4), 'y', 0, 0, tiled=True)  19.9 us
    all_to_all x1, blocking collectives, shards(): part = lax.all_to_all(part.reshape(16, 256, 128), PLANE, 0, 0, tiled=True)  17.8 us
    all_to_all x1, blocking collectives, shards(): lax.all_to_all(spread, PLANE, 0, 0, tiled=True).reshape(4, 4, 256, 128)  16.4 us
    ppermute x1, starting transfers between devices, shards(): yours = lax.ppermute(jnp.where(low, right, left), 'zh', SWAP)  15.7 us
    ppermute x1, waiting for transfers between devices, shards(): yours = lax.ppermute(yours, 'zh', SWAP).astype(jnp.float32)  15 us
    all_to_all x2, starting transfers between devices, sum_x(): part = lax.all_to_all(part, 'x', 0, 0, tiled=True)  10.7 us
    ppermute x1, waiting for transfers between devices, shards(): turned = lax.ppermute(y_both, PLANE, turn)  9.07 us
  transfers between devices with their start and end apart: 8, of which 8 were waited for; matrix products, arithmetic and copies ran while one was open for 5% of the time, Pallas kernels for 1%

profile of v7, /device:TPU:2, one launch (start us, length us, event | category | flops | bytes accessed | tf_op | source)
XLA Modules:
  0.0 192.0 jit_solution(11094379175872001201)
XLA Ops:
  6.5 0.0 all-gather.3.cloned.1.call-start
  6.5 1.8 convert_element_type.29
  8.3 0.0 all-gather.3.cloned.1.call-update
  8.3 1.1 convert_element_type.31
  9.4 15.7 %collective-permute-start = (bf16[512,128]{1,0:T(8,128)(2,1)S(1)}, bf16[512,128]{1,0:T(8,128)(2,1)S(1)}, u32[]{:S(2)}, u32[]{:S(2)}) collective-permute-start(bf16[512,128]{1,0:T(8,128)(2,1)S(1)} %broadcast_select_fusion.2), channel_id=1, source_target_pairs={{0,2},{2,0},{1,3},{3,1},{4,6},{6,4},{5,7},{7,5},{8,10},{10,8},{9,1... | collective-permute-start | bytes 393224 | tf_op jit(solution)/shard_map/ppermute | solution.py:155
  25.2 3.8 %collective-permute-done = bf16[512,128]{1,0:T(8,128)(2,1)S(1)} collective-permute-done((bf16[512,128]{1,0:T(8,128)(2,1)S(1)}, bf16[512,128]{1,0:T(8,128)(2,1)S(1)}, u32[]{:S(2)}, u32[]{:S(2)}) %collective-permute-start) | collective-permute-done | bytes 131104 | tf_op jit(solution)/shard_map/ppermute | solution.py:155
  29.0 3.5 %collective-permute-start.1 = (bf16[4,256,128]{2,1,0:T(8,128)(2,1)S(1)}, bf16[4,256,128]{2,1,0:T(8,128)(2,1)S(1)}, u32[]{:S(2)}, u32[]{:S(2)}) collective-permute-start(bf16[4,256,128]{2,1,0:T(8,128)(2,1)S(1)} %bitcast.30), channel_id=1, source_target_pairs={{0,0},{4,128},{8,256},{12,384},{128,4},{132,132},{136,260},{140,38... | collective-permute-start | bytes 786440 | tf_op jit(solution)/shard_map/ppermute | solution.py:160
  32.5 9.1 %collective-permute-done.1 = bf16[4,256,128]{2,1,0:T(8,128)(2,1)S(1)} collective-permute-done((bf16[4,256,128]{2,1,0:T(8,128)(2,1)S(1)}, bf16[4,256,128]{2,1,0:T(8,128)(2,1)S(1)}, u32[]{:S(2)}, u32[]{:S(2)}) %collective-permute-start.1) | collective-permute-done | bytes 262176 | tf_op jit(solution)/shard_map/ppermute | solution.py:160
  41.6 0.2 stack.28
  41.8 19.9 %all_to_all.25 = bf16[4,4,256,128]{3,2,1,0:T(8,128)(2,1)S(1)} all-to-all(bf16[4,4,256,128]{3,2,1,0:T(8,128)(2,1)S(1)} %stack.28), channel_id=1, replica_groups=mesh['x'=4,'zl'=8,'y'=4,'zh'=2,'c'=2] {'y'}, dimensions={0} | all-to-all | bytes 2097152 | tf_op jit(solution)/shard_map/all_to_all | solution.py:161
  61.7 1.9 collective-permute-start.2
  63.6 0.1 fusion
  63.8 2.4 %collective-permute-done.2 = bf16[4,4,256,128]{3,2,1,0:T(8,128)(2,1)S(1)} collective-permute-done((bf16[4,4,256,128]{3,2,1,0:T(8,128)(2,1)S(1)}, bf16[4,4,256,128]{3,2,1,0:T(8,128)(2,1)S(1)}, u32[]{:S(2)}, u32[]{:S(2)}) %collective-permute-start.2) | collective-permute-done | bytes 1048608 | tf_op jit(solution)/shard_map/ppermute | solution.py:121
  66.2 0.1 broadcast_select_fusion.1
  66.3 0.8 copy.3
  67.2 0.8 copy.4
  68.0 2.8 %maximum_bitcast_fusion = bf16[2,2,2,256,4,128]{5,4,3,2,1,0:T(4,128)(2,1)} fusion(bf16[1,4,2,2,256,128]{5,1,4,3,0,2:T(4,128)(2,1)S(1)} %copy.4, bf16[1,4,2,2,256,128]{5,1,4,3,0,2:T(4,128)(2,1)S(1)} %copy.3), kind=kLoop, calls=%fused_computation | loop fusion | flops 1048576 | bytes 4194304 | tf_op jit(solution)/shard_map/transpose | solution.py:80
  70.8 2.8 %reshape.32.right_ref = bf16[8,256,512]{2,1,0:T(8,128)(2,1)S(1)} reshape(bf16[2,2,2,256,4,128]{5,4,3,2,1,0:T(4,128)(2,1)} %maximum_bitcast_fusion) | data formatting | bytes 4194304 | tf_op jit(solution)/shard_map/reshape | solution.py:81
  73.6 20.7 %all-gather.3.cloned.1.call-done = bf16[8192,256]{1,0:T(8,128)(2,1)} async-done(((bf16[512,256]{1,0:T(8,128)(2,1)}), bf16[8192,256]{1,0:T(8,128)(2,1)}) %all-gather.3.cloned.1.call-update) | async-done | bytes 4194320 | tf_op jit(solution)/shard_map/all_gather | solution.py:148
  94.3 6.0 %shard_map.28 = bf16[4,4,256,128]{3,2,1,0:T(8,128)(2,1)S(1)} custom-call(bf16[16,512,256]{2,1,0:T(8,128)(2,1)} %bitcast.19, bf16[8,256,512]{2,1,0:T(8,128)(2,1)S(1)} %reshape.32.right_ref), custom_call_target="tpu_custom_call" | custom-call | flops 2147483648 | bytes 7340032 | tf_op jit(solution)/shard_map/pallas_call | solution.py:82
  100.2 17.8 %all_to_all.26 = bf16[16,256,128]{2,1,0:T(8,128)(2,1)S(1)} all-to-all(bf16[16,256,128]{2,1,0:T(8,128)(2,1)S(1)} %bitcast.25), channel_id=1, replica_groups=mesh['x'=4,'zl'=8,'y'=4,'zh'=2,'c'=2] {'x','y'}, dimensions={0} | all-to-all | bytes 2097152 | tf_op jit(solution)/shard_map/all_to_all | solution.py:166
  118.0 0.2 convert_reduce_fusion
  118.2 0.0 copy-start
  118.2 0.1 subtract_convert_fusion
  118.3 0.2 broadcast_in_dim.16
  118.5 16.4 %all_to_all.27 = bf16[16,256,128]{2,1,0:T(8,128)(2,1)S(1)} all-to-all(bf16[16,256,128]{2,1,0:T(8,128)(2,1)S(1)} %bitcast.28), channel_id=1, replica_groups=mesh['x'=4,'zl'=8,'y'=4,'zh'=2,'c'=2] {'x','y'}, dimensions={0} | all-to-all | bytes 2097152 | tf_op jit(solution)/shard_map/all_to_all | solution.py:171
  134.9 1.9 collective-permute-start.3
  136.9 2.6 %collective-permute-done.3.other_ref = bf16[4,4,256,128]{3,2,1,0:T(8,128)(2,1)S(1)} collective-permute-done((bf16[4,4,256,128]{3,2,1,0:T(8,128)(2,1)S(1)}, bf16[4,4,256,128]{3,2,1,0:T(8,128)(2,1)S(1)}, u32[]{:S(2)}, u32[]{:S(2)}) %collective-permute-start.3) | collective-permute-done | bytes 1048608 | tf_op jit(solution)/shard_map/ppermute | solution.py:121
  139.5 0.0 copy-done
  139.5 2.6 %shard_map.30 = bf16[4,2,256,128]{3,2,1,0:T(8,128)(2,1)} custom-call(bf16[16,512,256]{2,1,0:T(8,128)(2,1)S(1)} %bitcast.20, bf16[4,4,256,128]{3,2,1,0:T(8,128)(2,1)S(1)} %bitcast.23, bf16[4,4,256,128]{3,2,1,0:T(8,128)(2,1)S(1)} %collective-permute-done.3.other_ref), custom_call_target="tpu_custom_call" | custom-call | flops 1073741824 | bytes 4718592 | tf_op jit(solution)/shard_map/pallas_call | solution.py:102
  142.1 5.8 %all-to-all-start.4 = ((bf16[4,2,256,128]{3,2,1,0:T(8,128)(2,1)}), bf16[4,2,256,128]{3,2,1,0:T(8,128)(2,1)S(1)}, u32[]{:S(2)}, u32[]{:S(2)}) async-start(bf16[4,2,256,128]{3,2,1,0:T(8,128)(2,1)} %shard_map.30), calls=%async_computation.4 | async-start | bytes 1048576 | tf_op jit(solution)/shard_map/all_to_all | solution.py:175
  147.8 0.0 copy-start.1
  147.8 2.2 %copy-done.1 = bf16[8192,256]{1,0:T(8,128)(2,1)S(1)} copy-done((bf16[8192,256]{1,0:T(8,128)(2,1)S(1)}, bf16[8192,256]{1,0:T(8,128)(2,1)}, u32[]{:S(2)}) %copy-start.1) | copy-done | bytes 4194328
  150.0 2.6 %shard_map.29 = bf16[4,2,256,128]{3,2,1,0:T(8,128)(2,1)} custom-call(bf16[16,512,256]{2,1,0:T(8,128)(2,1)S(1)} %bitcast.21, bf16[4,4,256,128]{3,2,1,0:T(8,128)(2,1)S(1)} %bitcast.24, bf16[4,4,256,128]{3,2,1,0:T(8,128)(2,1)S(1)} %collective-permute-done.3.other_ref), custom_call_target="tpu_custom_call" | custom-call | flops 1073741824 | bytes 4718592 | tf_op jit(solution)/shard_map/pallas_call | solution.py:102
  152.6 0.0 copy-start.2
  152.6 3.8 %all-to-all-done.4 = bf16[4,2,256,128]{3,2,1,0:T(8,128)(2,1)S(1)} async-done(((bf16[4,2,256,128]{3,2,1,0:T(8,128)(2,1)}), bf16[4,2,256,128]{3,2,1,0:T(8,128)(2,1)S(1)}, u32[]{:S(2)}, u32[]{:S(2)}) %all-to-all-start.4) | async-done | bytes 524320 | tf_op jit(solution)/shard_map/all_to_all | solution.py:175
  156.4 4.9 %all-to-all-start.3 = ((bf16[4,2,256,128]{3,2,1,0:T(8,128)(2,1)}), bf16[4,2,256,128]{3,2,1,0:T(8,128)(2,1)S(1)}, u32[]{:S(2)}, u32[]{:S(2)}) async-start(bf16[4,2,256,128]{3,2,1,0:T(8,128)(2,1)} %shard_map.29), calls=%async_computation.3 | async-start | bytes 1048576 | tf_op jit(solution)/shard_map/all_to_all | solution.py:175
  161.3 0.1 reduce_sum.32
  161.4 7.3 %collective-permute-start.4 = (bf16[512,128]{1,0:T(8,128)(2,1)S(1)}, bf16[512,128]{1,0:T(8,128)(2,1)S(1)}, u32[]{:S(2)}, u32[]{:S(2)}) collective-permute-start(bf16[512,128]{1,0:T(8,128)(2,1)S(1)} %bitcast.31), channel_id=1, source_target_pairs={{0,2},{2,0},{1,3},{3,1},{4,6},{6,4},{5,7},{7,5},{8,10},{10,8},{9,1... | collective-permute-start | bytes 393224 | tf_op jit(solution)/shard_map/ppermute | solution.py:180
  168.7 0.4 all-to-all-done.3
  169.1 0.1 convert_reduce_fusion.1
  169.2 15.0 %collective-permute-done.4 = bf16[512,128]{1,0:T(8,128)(2,1)S(1)} collective-permute-done((bf16[512,128]{1,0:T(8,128)(2,1)S(1)}, bf16[512,128]{1,0:T(8,128)(2,1)S(1)}, u32[]{:S(2)}, u32[]{:S(2)}) %collective-permute-start.4) | collective-permute-done | bytes 131104 | tf_op jit(solution)/shard_map/ppermute | solution.py:180
  184.2 0.0 copy-done.2
  184.3 0.9 maximum_add_fusion
  (6 shorter events, 0.1 us)
Async XLA Ops:
  6.5 87.7 %all-gather.3.cloned.1.call-start = ((), (), s32[]{:S(2)}) async-start(), calls=%async_computation.5 | async-start | bytes 4456448 | tf_op jit(solution)/shard_map/all_gather | solution.py:148
  9.4 19.5 %collective-permute-start = (bf16[512,128]{1,0:T(8,128)(2,1)S(1)}, bf16[512,128]{1,0:T(8,128)(2,1)S(1)}, u32[]{:S(2)}, u32[]{:S(2)}) collective-permute-start(bf16[512,128]{1,0:T(8,128)(2,1)S(1)} %broadcast_select_fusion.2), channel_id=1, source_target_pairs={{0,2},{2,0},{1,3},{3,1},{4,6},{6,4},{5,7},{7,5},{8,10},{10,8},{9,1... | collective-permute-start | bytes 393224 | tf_op jit(solution)/shard_map/ppermute | solution.py:155
  29.0 12.5 %collective-permute-start.1 = (bf16[4,256,128]{2,1,0:T(8,128)(2,1)S(1)}, bf16[4,256,128]{2,1,0:T(8,128)(2,1)S(1)}, u32[]{:S(2)}, u32[]{:S(2)}) collective-permute-start(bf16[4,256,128]{2,1,0:T(8,128)(2,1)S(1)} %bitcast.30), channel_id=1, source_target_pairs={{0,0},{4,128},{8,256},{12,384},{128,4},{132,132},{136,260},{140,38... | collective-permute-start | bytes 786440 | tf_op jit(solution)/shard_map/ppermute | solution.py:160
  61.7 4.5 %collective-permute-start.2 = (bf16[4,4,256,128]{3,2,1,0:T(8,128)(2,1)S(1)}, bf16[4,4,256,128]{3,2,1,0:T(8,128)(2,1)S(1)}, u32[]{:S(2)}, u32[]{:S(2)}) collective-permute-start(bf16[4,4,256,128]{3,2,1,0:T(8,128)(2,1)S(1)} %all_to_all.25), channel_id=1, source_target_pairs={{0,1},{1,0},{2,3},{3,2},{4,5},{5,4},{6,7},{7,6},{8,9},{9,8},{10,11... | collective-permute-start | bytes 3145736 | tf_op jit(solution)/shard_map/ppermute | solution.py:121
  118.2 21.3 %copy-start = (bf16[8192,256]{1,0:T(8,128)(2,1)S(1)}, bf16[8192,256]{1,0:T(8,128)(2,1)}, u32[]{:S(2)}) copy-start(bf16[8192,256]{1,0:T(8,128)(2,1)} %all-gather.3.cloned.1.call-done) | copy-start | bytes 12582916
  134.9 4.5 %collective-permute-start.3 = (bf16[4,4,256,128]{3,2,1,0:T(8,128)(2,1)S(1)}, bf16[4,4,256,128]{3,2,1,0:T(8,128)(2,1)S(1)}, u32[]{:S(2)}, u32[]{:S(2)}) collective-permute-start(bf16[4,4,256,128]{3,2,1,0:T(8,128)(2,1)S(1)} %bitcast.22), channel_id=1, source_target_pairs={{0,1},{1,0},{2,3},{3,2},{4,5},{5,4},{6,7},{7,6},{8,9},{9,8},{10,11... | collective-permute-start | bytes 3145736 | tf_op jit(solution)/shard_map/ppermute | solution.py:121
  142.1 14.4 %all-to-all-start.4 = ((bf16[4,2,256,128]{3,2,1,0:T(8,128)(2,1)}), bf16[4,2,256,128]{3,2,1,0:T(8,128)(2,1)S(1)}, u32[]{:S(2)}, u32[]{:S(2)}) async-start(bf16[4,2,256,128]{3,2,1,0:T(8,128)(2,1)} %shard_map.30), calls=%async_computation.4 | async-start | bytes 1048576 | tf_op jit(solution)/shard_map/all_to_all | solution.py:175
  147.8 2.2 %copy-start.1 = (bf16[8192,256]{1,0:T(8,128)(2,1)S(1)}, bf16[8192,256]{1,0:T(8,128)(2,1)}, u32[]{:S(2)}) copy-start(bf16[8192,256]{1,0:T(8,128)(2,1)} %all-gather.3.cloned.1.call-done) | copy-start | bytes 12582916
  152.6 31.7 %copy-start.2 = (f32[512,256]{1,0:T(8,128)S(1)}, f32[512,256]{1,0:T(8,128)}, u32[]{:S(2)}) copy-start(f32[512,256]{1,0:T(8,128)} %param.2) | copy-start | bytes 1572868
  156.4 12.7 %all-to-all-start.3 = ((bf16[4,2,256,128]{3,2,1,0:T(8,128)(2,1)}), bf16[4,2,256,128]{3,2,1,0:T(8,128)(2,1)S(1)}, u32[]{:S(2)}, u32[]{:S(2)}) async-start(bf16[4,2,256,128]{3,2,1,0:T(8,128)(2,1)} %shard_map.29), calls=%async_computation.3 | async-start | bytes 1048576 | tf_op jit(solution)/shard_map/all_to_all | solution.py:175
  161.4 22.8 %collective-permute-start.4 = (bf16[512,128]{1,0:T(8,128)(2,1)S(1)}, bf16[512,128]{1,0:T(8,128)(2,1)S(1)}, u32[]{:S(2)}, u32[]{:S(2)}) collective-permute-start(bf16[512,128]{1,0:T(8,128)(2,1)S(1)} %bitcast.31), channel_id=1, source_target_pairs={{0,2},{2,0},{1,3},{3,1},{4,6},{6,4},{5,7},{7,5},{8,10},{10,8},{9,1... | collective-permute-start | bytes 393224 | tf_op jit(solution)/shard_map/ppermute | solution.py:180
Sparse Core Ops, SparseCore 0:
  9.4 84.8 all-gather.2

commit v8 on v7

--- a/solution.py
+++ b/solution.py
@@ -178,9 +178,11 @@
     yours = sum_x(dot_right(1, z_rows, own, other)).astype(jnp.bfloat16)
     mine = dot_right(0, z_rows, own, other)
     yours = lax.ppermute(yours, "zh", SWAP).astype(jnp.float32)
-    mine = sum_x(mine)
+    mine = lax.cond(
+        at("c") < 2, sum_x, lambda part: jnp.zeros((512, 128), jnp.float32), mine
+    )
     part = jnp.concatenate([jnp.where(low, mine, yours), jnp.where(low, yours, mine)], axis=1)
-    return 1.5 * z_half.astype(jnp.float32) + part
+    return 1.5 * lax.reduce_precision(z_iter, 8, 7) + part
 
 
 def solution(mesh):

time: 193 us -> 186 us (0.964)
  the two profiles are of different devices: /device:TPU:2 before, /device:TPU:1 now
where the time goes in v8:
time: 186 us; the launch traced here: 185 us
  blocking collectives  91 us (49%)
  starting transfers between devices  41.6 us (22%)
  waiting for transfers between devices  15.2 us (8%)
  between operations  13.7 us (7%)
  Pallas kernels  9.54 us (5%)
  other arithmetic  7.33 us (4%)
  local copies, waits for them, and re-layouts  6.96 us (4%)
    all_to_all x1, blocking collectives, shards(): y_own = lax.all_to_all(jnp.stack([turned] * 4), 'y', 0, 0, tiled=True)  35.7 us
    all_to_all x2, blocking collectives, sum_x(): part = lax.all_to_all(part, 'x', 0, 0, tiled=True)  22.2 us
    all_to_all x1, blocking collectives, shards(): part = lax.all_to_all(part.reshape(16, 256, 128), PLANE, 0, 0, tiled=True)  18.1 us
    ppermute x2, starting transfers between devices, other_core(): return lax.ppermute(block, 'c', SWAP)  17.7 us
    ppermute x1, starting transfers between devices, shards(): yours = lax.ppermute(jnp.where(low, right, left), 'zh', SWAP)  16.3 us
    all_to_all x1, blocking collectives, shards(): lax.all_to_all(spread, PLANE, 0, 0, tiled=True).reshape(4, 4, 256, 128)  15 us
    all_gather x1, waiting for transfers between devices, shards(): z_rows = lax.all_gather(z_half, AXES, axis_index_groups=Z_RINGS)  8.19 us
    ppermute x1, starting transfers between devices, shards(): yours = lax.ppermute(yours, 'zh', SWAP).astype(jnp.float32)  6.97 us
  transfers between devices with their start and end apart: 6, of which 4 were waited for; matrix products, arithmetic and copies ran while one was open for 5% of the time, Pallas kernels for 1%

profile of v8, /device:TPU:1, one launch (start us, length us, event | category | flops | bytes accessed | tf_op | source)
XLA Modules:
  0.0 185.3 jit_solution(8681213695923608549)
XLA Ops:
  6.5 0.0 all-gather.3.cloned.1.call-start
  6.5 1.8 convert_element_type.30
  8.3 0.0 all-gather.3.cloned.1.call-update
  8.3 1.1 convert_element_type.31
  9.4 16.3 %collective-permute-start = (bf16[512,128]{1,0:T(8,128)(2,1)S(1)}, bf16[512,128]{1,0:T(8,128)(2,1)S(1)}, u32[]{:S(2)}, u32[]{:S(2)}) collective-permute-start(bf16[512,128]{1,0:T(8,128)(2,1)S(1)} %broadcast_select_fusion.2), channel_id=1, source_target_pairs={{0,2},{2,0},{1,3},{3,1},{4,6},{6,4},{5,7},{7,5},{8,10},{10,8},{9,1... | collective-permute-start | bytes 393224 | tf_op jit(solution)/shard_map/ppermute | solution.py:155
  25.7 2.6 %collective-permute-done = bf16[512,128]{1,0:T(8,128)(2,1)S(1)} collective-permute-done((bf16[512,128]{1,0:T(8,128)(2,1)S(1)}, bf16[512,128]{1,0:T(8,128)(2,1)S(1)}, u32[]{:S(2)}, u32[]{:S(2)}) %collective-permute-start) | collective-permute-done | bytes 131104 | tf_op jit(solution)/shard_map/ppermute | solution.py:155
  28.4 0.7 collective-permute-start.1
  29.1 0.0 collective-permute-done.1
  29.1 0.2 stack.28
  29.3 35.7 %all_to_all.25 = bf16[4,4,256,128]{3,2,1,0:T(8,128)(2,1)S(1)} all-to-all(bf16[4,4,256,128]{3,2,1,0:T(8,128)(2,1)S(1)} %stack.28), channel_id=1, replica_groups=mesh['x'=4,'zl'=8,'y'=4,'zh'=2,'c'=2] {'y'}, dimensions={0} | all-to-all | bytes 2097152 | tf_op jit(solution)/shard_map/all_to_all | solution.py:161
  65.0 4.4 %collective-permute-start.2 = (bf16[4,4,256,128]{3,2,1,0:T(8,128)(2,1)S(1)}, bf16[4,4,256,128]{3,2,1,0:T(8,128)(2,1)S(1)}, u32[]{:S(2)}, u32[]{:S(2)}) collective-permute-start(bf16[4,4,256,128]{3,2,1,0:T(8,128)(2,1)S(1)} %all_to_all.25), channel_id=1, source_target_pairs={{0,1},{1,0},{2,3},{3,2},{4,5},{5,4},{6,7},{7,6},{8,9},{9,8},{10,11... | collective-permute-start | bytes 3145736 | tf_op jit(solution)/shard_map/ppermute | solution.py:121
  69.5 0.1 fusion
  69.7 2.1 %collective-permute-done.2 = bf16[4,4,256,128]{3,2,1,0:T(8,128)(2,1)S(1)} collective-permute-done((bf16[4,4,256,128]{3,2,1,0:T(8,128)(2,1)S(1)}, bf16[4,4,256,128]{3,2,1,0:T(8,128)(2,1)S(1)}, u32[]{:S(2)}, u32[]{:S(2)}) %collective-permute-start.2) | collective-permute-done | bytes 1048608 | tf_op jit(solution)/shard_map/ppermute | solution.py:121
  71.7 0.1 broadcast_select_fusion.1
  71.9 0.8 copy.3
  72.7 0.8 copy.4
  73.5 2.8 %maximum_bitcast_fusion = bf16[2,2,2,256,4,128]{5,4,3,2,1,0:T(4,128)(2,1)} fusion(bf16[1,4,2,2,256,128]{5,1,4,3,0,2:T(4,128)(2,1)S(1)} %copy.4, bf16[1,4,2,2,256,128]{5,1,4,3,0,2:T(4,128)(2,1)S(1)} %copy.3), kind=kLoop, calls=%fused_computation.1 | loop fusion | flops 1048576 | bytes 4194304 | tf_op jit(solution)/shard_map/transpose | solution.py:80
  76.4 2.7 %reshape.32.right_ref = bf16[8,256,512]{2,1,0:T(8,128)(2,1)S(1)} reshape(bf16[2,2,2,256,4,128]{5,4,3,2,1,0:T(4,128)(2,1)} %maximum_bitcast_fusion) | data formatting | bytes 4194304 | tf_op jit(solution)/shard_map/reshape | solution.py:81
  79.1 8.2 %all-gather.3.cloned.1.call-done = bf16[8192,256]{1,0:T(8,128)(2,1)} async-done(((bf16[512,256]{1,0:T(8,128)(2,1)}), bf16[8192,256]{1,0:T(8,128)(2,1)}) %all-gather.3.cloned.1.call-update) | async-done | bytes 4194320 | tf_op jit(solution)/shard_map/all_gather | solution.py:148
  87.3 6.0 %shard_map.28 = bf16[4,4,256,128]{3,2,1,0:T(8,128)(2,1)S(1)} custom-call(bf16[16,512,256]{2,1,0:T(8,128)(2,1)} %bitcast.17, bf16[8,256,512]{2,1,0:T(8,128)(2,1)S(1)} %reshape.32.right_ref), custom_call_target="tpu_custom_call" | custom-call | flops 2147483648 | bytes 7340032 | tf_op jit(solution)/shard_map/pallas_call | solution.py:82
  93.3 18.1 %all_to_all.26 = bf16[16,256,128]{2,1,0:T(8,128)(2,1)S(1)} all-to-all(bf16[16,256,128]{2,1,0:T(8,128)(2,1)S(1)} %bitcast.23), channel_id=1, replica_groups=mesh['x'=4,'zl'=8,'y'=4,'zh'=2,'c'=2] {'x','y'}, dimensions={0} | all-to-all | bytes 2097152 | tf_op jit(solution)/shard_map/all_to_all | solution.py:166
  111.4 0.2 convert_reduce_fusion.1
  111.6 0.0 copy-start
  111.6 0.1 subtract_convert_fusion
  111.7 0.2 broadcast_in_dim.16
  111.9 15.0 %all_to_all.27 = bf16[16,256,128]{2,1,0:T(8,128)(2,1)S(1)} all-to-all(bf16[16,256,128]{2,1,0:T(8,128)(2,1)S(1)} %bitcast.26), channel_id=1, replica_groups=mesh['x'=4,'zl'=8,'y'=4,'zh'=2,'c'=2] {'x','y'}, dimensions={0} | all-to-all | bytes 2097152 | tf_op jit(solution)/shard_map/all_to_all | solution.py:171
  126.9 13.2 %collective-permute-start.3 = (bf16[4,4,256,128]{3,2,1,0:T(8,128)(2,1)S(1)}, bf16[4,4,256,128]{3,2,1,0:T(8,128)(2,1)S(1)}, u32[]{:S(2)}, u32[]{:S(2)}) collective-permute-start(bf16[4,4,256,128]{3,2,1,0:T(8,128)(2,1)S(1)} %bitcast.20), channel_id=1, source_target_pairs={{0,1},{1,0},{2,3},{3,2},{4,5},{5,4},{6,7},{7,6},{8,9},{9,8},{10,11... | collective-permute-start | bytes 3145736 | tf_op jit(solution)/shard_map/ppermute | solution.py:121
  140.1 2.3 %collective-permute-done.3.other_ref = bf16[4,4,256,128]{3,2,1,0:T(8,128)(2,1)S(1)} collective-permute-done((bf16[4,4,256,128]{3,2,1,0:T(8,128)(2,1)S(1)}, bf16[4,4,256,128]{3,2,1,0:T(8,128)(2,1)S(1)}, u32[]{:S(2)}, u32[]{:S(2)}) %collective-permute-start.3) | collective-permute-done | bytes 1048608 | tf_op jit(solution)/shard_map/ppermute | solution.py:121
  142.4 0.0 copy-done
  142.4 1.8 shard_map.30
  144.2 11.6 %all_to_all.28 = bf16[4,2,256,128]{3,2,1,0:T(8,128)(2,1)S(1)} all-to-all(bf16[4,2,256,128]{3,2,1,0:T(8,128)(2,1)S(1)} %shard_map.30), channel_id=1, replica_groups=mesh['x'=4,'zl'=8,'y'=4,'zh'=2,'c'=2] {'x'}, dimensions={0} | all-to-all | bytes 1048576 | tf_op jit(solution)/shard_map/all_to_all | solution.py:175
  155.8 0.1 reduce_sum.31
  155.9 7.0 %collective-permute-start.4 = (bf16[512,128]{1,0:T(8,128)(2,1)S(1)}, bf16[512,128]{1,0:T(8,128)(2,1)S(1)}, u32[]{:S(2)}, u32[]{:S(2)}) collective-permute-start(bf16[512,128]{1,0:T(8,128)(2,1)S(1)} %bitcast.30), channel_id=1, source_target_pairs={{0,2},{2,0},{1,3},{3,1},{4,6},{6,4},{5,7},{7,5},{8,10},{10,8},{9,1... | collective-permute-start | bytes 393224 | tf_op jit(solution)/shard_map/ppermute | solution.py:180
  162.9 0.0 copy-start.1
  162.9 2.2 %copy-done.1 = bf16[8192,256]{1,0:T(8,128)(2,1)S(1)} copy-done((bf16[8192,256]{1,0:T(8,128)(2,1)S(1)}, bf16[8192,256]{1,0:T(8,128)(2,1)}, u32[]{:S(2)}) %copy-start.1) | copy-done | bytes 4194328
  165.1 1.8 shard_map.29
  166.9 0.0 copy-start.2
  166.9 10.6 %conditional.1 = (f32[512,128]{1,0:T(8,128)S(1)}) conditional(s32[]{:T(128)} %convert_element_type.29, () %tuple.12, bf16[4,2,256,128]{3,2,1,0:T(8,128)(2,1)S(1)} %shard_map.29), branch_computations={%region_1.2_spmd, %region_2.4_spmd} | conditional | flops 458752 | bytes 1835016 | solution.py:181
  166.9 10.6 %all_to_all.24 = bf16[4,2,256,128]{3,2,1,0:T(8,128)(2,1)S(1)} all-to-all(bf16[4,2,256,128]{3,2,1,0:T(8,128)(2,1)S(1)} %param.1), channel_id=1, replica_groups=mesh['x'=4,'zl'=8,'y'=4,'zh'=2,'c'=2] {'x'}, dimensions={0} | all-to-all | bytes 1048576 | tf_op jit(solution)/shard_map/cond/branch_1_fun/all_to_all | solution.py:175
  177.5 0.1 convert_reduce_fusion
  177.5 0.0 collective-permute-done.4
  177.6 0.0 copy-done.2
  177.6 0.9 maximum_add_fusion
  (6 shorter events, 0.1 us)
Async XLA Ops:
  6.5 80.8 %all-gather.3.cloned.1.call-start = ((), (), s32[]{:S(2)}) async-start(), calls=%async_computation.5 | async-start | bytes 4456448 | tf_op jit(solution)/shard_map/all_gather | solution.py:148
  9.4 18.9 %collective-permute-start = (bf16[512,128]{1,0:T(8,128)(2,1)S(1)}, bf16[512,128]{1,0:T(8,128)(2,1)S(1)}, u32[]{:S(2)}, u32[]{:S(2)}) collective-permute-start(bf16[512,128]{1,0:T(8,128)(2,1)S(1)} %broadcast_select_fusion.2), channel_id=1, source_target_pairs={{0,2},{2,0},{1,3},{3,1},{4,6},{6,4},{5,7},{7,5},{8,10},{10,8},{9,1... | collective-permute-start | bytes 393224 | tf_op jit(solution)/shard_map/ppermute | solution.py:155
  28.4 0.7 collective-permute-start.1
  65.0 6.7 %collective-permute-start.2 = (bf16[4,4,256,128]{3,2,1,0:T(8,128)(2,1)S(1)}, bf16[4,4,256,128]{3,2,1,0:T(8,128)(2,1)S(1)}, u32[]{:S(2)}, u32[]{:S(2)}) collective-permute-start(bf16[4,4,256,128]{3,2,1,0:T(8,128)(2,1)S(1)} %all_to_all.25), channel_id=1, source_target_pairs={{0,1},{1,0},{2,3},{3,2},{4,5},{5,4},{6,7},{7,6},{8,9},{9,8},{10,11... | collective-permute-start | bytes 3145736 | tf_op jit(solution)/shard_map/ppermute | solution.py:121
  111.6 30.8 %copy-start = (bf16[8192,256]{1,0:T(8,128)(2,1)S(1)}, bf16[8192,256]{1,0:T(8,128)(2,1)}, u32[]{:S(2)}) copy-start(bf16[8192,256]{1,0:T(8,128)(2,1)} %all-gather.3.cloned.1.call-done) | copy-start | bytes 12582916
  126.9 15.5 %collective-permute-start.3 = (bf16[4,4,256,128]{3,2,1,0:T(8,128)(2,1)S(1)}, bf16[4,4,256,128]{3,2,1,0:T(8,128)(2,1)S(1)}, u32[]{:S(2)}, u32[]{:S(2)}) collective-permute-start(bf16[4,4,256,128]{3,2,1,0:T(8,128)(2,1)S(1)} %bitcast.20), channel_id=1, source_target_pairs={{0,1},{1,0},{2,3},{3,2},{4,5},{5,4},{6,7},{7,6},{8,9},{9,8},{10,11... | collective-permute-start | bytes 3145736 | tf_op jit(solution)/shard_map/ppermute | solution.py:121
  155.9 21.6 %collective-permute-start.4 = (bf16[512,128]{1,0:T(8,128)(2,1)S(1)}, bf16[512,128]{1,0:T(8,128)(2,1)S(1)}, u32[]{:S(2)}, u32[]{:S(2)}) collective-permute-start(bf16[512,128]{1,0:T(8,128)(2,1)S(1)} %bitcast.30), channel_id=1, source_target_pairs={{0,2},{2,0},{1,3},{3,1},{4,6},{6,4},{5,7},{7,5},{8,10},{10,8},{9,1... | collective-permute-start | bytes 393224 | tf_op jit(solution)/shard_map/ppermute | solution.py:180
  162.9 2.2 %copy-start.1 = (bf16[8192,256]{1,0:T(8,128)(2,1)S(1)}, bf16[8192,256]{1,0:T(8,128)(2,1)}, u32[]{:S(2)}) copy-start(bf16[8192,256]{1,0:T(8,128)(2,1)} %all-gather.3.cloned.1.call-done) | copy-start | bytes 12582916
  166.9 10.7 %copy-start.2 = (f32[512,256]{1,0:T(8,128)S(1)}, f32[512,256]{1,0:T(8,128)}, u32[]{:S(2)}) copy-start(f32[512,256]{1,0:T(8,128)} %param.4) | copy-start | bytes 1572868
Sparse Core Ops, SparseCore 0:
  9.4 77.8 all-gather.2

commit v9 on v8

--- a/solution.py
+++ b/solution.py
@@ -26,24 +26,17 @@
 ]
 
 
-def dot_kernel(flips, z_ref, own_ref, other_ref, out_ref, left, sem):
+def dot_kernel(flips, z_ref, own_ref, other_ref, out_ref):
     groups, _, depth, width = own_ref.shape
     c = lax.axis_index("c")
     first = (lax.axis_index("zh") ^ flips) * 8
-    copies = []
-    for n in range(8):
-        chunk = (n % 4) // 2 * 4 + (c ^ (n // 4)) * 2 + n % 2
-        copies.append(pltpu.make_async_copy(z_ref.at[first + chunk], left.at[n], sem.at[n]))
-    for copy in copies:
-        copy.start()
     for s in range(2):
         total = None
         for n in range(8):
-            if s == 0:
-                copies[n].wait()
             part = (own_ref, other_ref)[n // 4]
             right = jnp.concatenate([part[j, n % 4] for j in range(groups)], axis=1)
-            rows = left[n, s * depth : (s + 1) * depth, :]
+            chunk = first + (n % 4) // 2 * 4 + (c ^ (n // 4)) * 2 + n % 2
+            rows = z_ref[chunk, s * depth : (s + 1) * depth, :]
             term = jnp.dot(rows, right, preferred_element_type=jnp.float32)
             total = term if total is None else total + term
         for j in range(groups):
@@ -53,7 +46,8 @@
 def dot_all_kernel(z_ref, right_ref, out_ref, left, sem):
     groups, _, depth, width = out_ref.shape
     copies = [pltpu.make_async_copy(z_ref.at[n], left.at[n], sem.at[n]) for n in range(16)]
-    for copy in copies:
+    ahead = 4
+    for copy in copies[:ahead]:
         copy.start()
     for zh in range(2):
         for h in range(2):
@@ -62,6 +56,8 @@
             for k in range(8):
                 if h == 0:
                     copies[zh * 8 + k].wait()
+                    if zh * 8 + k + ahead < 16:
+                        copies[zh * 8 + k + ahead].start()
                 term = jnp.dot(
                     left[zh * 8 + k], right_ref[k, :, cols], preferred_element_type=jnp.float32
                 )
@@ -101,13 +97,9 @@
     groups, steps, depth, width = own.shape
     return pl.pallas_call(
         functools.partial(dot_kernel, flips),
-        in_specs=[pl.BlockSpec(memory_space=pl.ANY)] + [pl.BlockSpec(memory_space=pltpu.VMEM)] * 2,
+        in_specs=[pl.BlockSpec(memory_space=pltpu.VMEM)] * 3,
         out_specs=pl.BlockSpec(memory_space=pltpu.VMEM),
         out_shape=jax.ShapeDtypeStruct((groups, 2, depth, width), jnp.bfloat16),
-        scratch_shapes=[
-            pltpu.VMEM((8,) + z_rows.shape[1:], jnp.bfloat16),
-            pltpu.SemaphoreType.DMA((8,)),
-        ],
         compiler_params=pltpu.CompilerParams(vmem_limit_bytes=32 * 2**20),
         cost_estimate=pl.CostEstimate(
             flops=z_rows.size * groups * width,

time: 186 us -> 186 us (level)
  no operation moved by 1% of the time
where the time goes in v9:
time: 186 us; the launch traced here: 185 us
  blocking collectives  91 us (49%)
  starting transfers between devices  41.6 us (22%)
  waiting for transfers between devices  15.2 us (8%)
  between operations  13.7 us (7%)
  Pallas kernels  9.12 us (5%)
  other arithmetic  7.33 us (4%)
  local copies, waits for them, and re-layouts  6.96 us (4%)
    all_to_all x1, blocking collectives, shards(): y_own = lax.all_to_all(jnp.stack([turned] * 4), 'y', 0, 0, tiled=True)  35.7 us
    all_to_all x2, blocking collectives, sum_x(): part = lax.all_to_all(part, 'x', 0, 0, tiled=True)  22.2 us
    all_to_all x1, blocking collectives, shards(): part = lax.all_to_all(part.reshape(16, 256, 128), PLANE, 0, 0, tiled=True)  18.1 us
    ppermute x2, starting transfers between devices, other_core(): return lax.ppermute(block, 'c', SWAP)  17.7 us
    ppermute x1, starting transfers between devices, shards(): yours = lax.ppermute(jnp.where(low, right, left), 'zh', SWAP)  16.3 us
    all_to_all x1, blocking collectives, shards(): lax.all_to_all(spread, PLANE, 0, 0, tiled=True).reshape(4, 4, 256, 128)  15 us
    all_gather x1, waiting for transfers between devices, shards(): z_rows = lax.all_gather(z_half, AXES, axis_index_groups=Z_RINGS)  8.19 us
    ppermute x1, starting transfers between devices, shards(): yours = lax.ppermute(yours, 'zh', SWAP).astype(jnp.float32)  6.98 us
  transfers between devices with their start and end apart: 6, of which 4 were waited for; matrix products, arithmetic and copies ran while one was open for 5% of the time, Pallas kernels for 1%

profile of v9, /device:TPU:1, one launch (start us, length us, event | category | flops | bytes accessed | tf_op | source)
XLA Modules:
  0.0 184.9 jit_solution(2729596377320640787)
XLA Ops:
  6.5 0.0 all-gather.3.cloned.1.call-start
  6.5 1.8 convert_element_type.30
  8.3 0.0 all-gather.3.cloned.1.call-update
  8.3 1.1 convert_element_type.31
  9.4 16.3 %collective-permute-start = (bf16[512,128]{1,0:T(8,128)(2,1)S(1)}, bf16[512,128]{1,0:T(8,128)(2,1)S(1)}, u32[]{:S(2)}, u32[]{:S(2)}) collective-permute-start(bf16[512,128]{1,0:T(8,128)(2,1)S(1)} %broadcast_select_fusion.2), channel_id=1, source_target_pairs={{0,2},{2,0},{1,3},{3,1},{4,6},{6,4},{5,7},{7,5},{8,10},{10,8},{9,1... | collective-permute-start | bytes 393224 | tf_op jit(solution)/shard_map/ppermute | solution.py:147
  25.7 2.6 %collective-permute-done = bf16[512,128]{1,0:T(8,128)(2,1)S(1)} collective-permute-done((bf16[512,128]{1,0:T(8,128)(2,1)S(1)}, bf16[512,128]{1,0:T(8,128)(2,1)S(1)}, u32[]{:S(2)}, u32[]{:S(2)}) %collective-permute-start) | collective-permute-done | bytes 131104 | tf_op jit(solution)/shard_map/ppermute | solution.py:147
  28.4 0.7 collective-permute-start.1
  29.1 0.0 collective-permute-done.1
  29.1 0.2 stack.28
  29.3 35.7 %all_to_all.25 = bf16[4,4,256,128]{3,2,1,0:T(8,128)(2,1)S(1)} all-to-all(bf16[4,4,256,128]{3,2,1,0:T(8,128)(2,1)S(1)} %stack.28), channel_id=1, replica_groups=mesh['x'=4,'zl'=8,'y'=4,'zh'=2,'c'=2] {'y'}, dimensions={0} | all-to-all | bytes 2097152 | tf_op jit(solution)/shard_map/all_to_all | solution.py:153
  65.0 4.4 %collective-permute-start.2 = (bf16[4,4,256,128]{3,2,1,0:T(8,128)(2,1)S(1)}, bf16[4,4,256,128]{3,2,1,0:T(8,128)(2,1)S(1)}, u32[]{:S(2)}, u32[]{:S(2)}) collective-permute-start(bf16[4,4,256,128]{3,2,1,0:T(8,128)(2,1)S(1)} %all_to_all.25), channel_id=1, source_target_pairs={{0,1},{1,0},{2,3},{3,2},{4,5},{5,4},{6,7},{7,6},{8,9},{9,8},{10,11... | collective-permute-start | bytes 3145736 | tf_op jit(solution)/shard_map/ppermute | solution.py:113
  69.5 0.1 fusion
  69.7 2.1 %collective-permute-done.2 = bf16[4,4,256,128]{3,2,1,0:T(8,128)(2,1)S(1)} collective-permute-done((bf16[4,4,256,128]{3,2,1,0:T(8,128)(2,1)S(1)}, bf16[4,4,256,128]{3,2,1,0:T(8,128)(2,1)S(1)}, u32[]{:S(2)}, u32[]{:S(2)}) %collective-permute-start.2) | collective-permute-done | bytes 1048608 | tf_op jit(solution)/shard_map/ppermute | solution.py:113
  71.7 0.1 broadcast_select_fusion.1
  71.9 0.8 copy.3
  72.7 0.8 copy.4
  73.5 2.8 %maximum_bitcast_fusion = bf16[2,2,2,256,4,128]{5,4,3,2,1,0:T(4,128)(2,1)} fusion(bf16[1,4,2,2,256,128]{5,1,4,3,0,2:T(4,128)(2,1)S(1)} %copy.4, bf16[1,4,2,2,256,128]{5,1,4,3,0,2:T(4,128)(2,1)S(1)} %copy.3), kind=kLoop, calls=%fused_computation.1 | loop fusion | flops 1048576 | bytes 4194304 | tf_op jit(solution)/shard_map/transpose | solution.py:76
  76.4 2.7 %reshape.32.right_ref = bf16[8,256,512]{2,1,0:T(8,128)(2,1)S(1)} reshape(bf16[2,2,2,256,4,128]{5,4,3,2,1,0:T(4,128)(2,1)} %maximum_bitcast_fusion) | data formatting | bytes 4194304 | tf_op jit(solution)/shard_map/reshape | solution.py:77
  79.1 8.2 %all-gather.3.cloned.1.call-done = bf16[8192,256]{1,0:T(8,128)(2,1)} async-done(((bf16[512,256]{1,0:T(8,128)(2,1)}), bf16[8192,256]{1,0:T(8,128)(2,1)}) %all-gather.3.cloned.1.call-update) | async-done | bytes 4194320 | tf_op jit(solution)/shard_map/all_gather | solution.py:140
  87.3 6.6 %shard_map.28 = bf16[4,4,256,128]{3,2,1,0:T(8,128)(2,1)S(1)} custom-call(bf16[16,512,256]{2,1,0:T(8,128)(2,1)} %bitcast.17, bf16[8,256,512]{2,1,0:T(8,128)(2,1)S(1)} %reshape.32.right_ref), custom_call_target="tpu_custom_call" | custom-call | flops 2147483648 | bytes 7340032 | tf_op jit(solution)/shard_map/pallas_call | solution.py:78
  93.9 18.1 %all_to_all.26 = bf16[16,256,128]{2,1,0:T(8,128)(2,1)S(1)} all-to-all(bf16[16,256,128]{2,1,0:T(8,128)(2,1)S(1)} %bitcast.23), channel_id=1, replica_groups=mesh['x'=4,'zl'=8,'y'=4,'zh'=2,'c'=2] {'x','y'}, dimensions={0} | all-to-all | bytes 2097152 | tf_op jit(solution)/shard_map/all_to_all | solution.py:158
  112.1 0.2 convert_reduce_fusion.1
  112.2 0.0 copy-start
  112.2 0.1 subtract_convert_fusion
  112.3 0.2 broadcast_in_dim.16
  112.5 15.0 %all_to_all.27 = bf16[16,256,128]{2,1,0:T(8,128)(2,1)S(1)} all-to-all(bf16[16,256,128]{2,1,0:T(8,128)(2,1)S(1)} %bitcast.26), channel_id=1, replica_groups=mesh['x'=4,'zl'=8,'y'=4,'zh'=2,'c'=2] {'x','y'}, dimensions={0} | all-to-all | bytes 2097152 | tf_op jit(solution)/shard_map/all_to_all | solution.py:163
  127.5 13.2 %collective-permute-start.3 = (bf16[4,4,256,128]{3,2,1,0:T(8,128)(2,1)S(1)}, bf16[4,4,256,128]{3,2,1,0:T(8,128)(2,1)S(1)}, u32[]{:S(2)}, u32[]{:S(2)}) collective-permute-start(bf16[4,4,256,128]{3,2,1,0:T(8,128)(2,1)S(1)} %bitcast.20), channel_id=1, source_target_pairs={{0,1},{1,0},{2,3},{3,2},{4,5},{5,4},{6,7},{7,6},{8,9},{9,8},{10,11... | collective-permute-start | bytes 3145736 | tf_op jit(solution)/shard_map/ppermute | solution.py:113
  140.8 2.3 %collective-permute-done.3.other_ref = bf16[4,4,256,128]{3,2,1,0:T(8,128)(2,1)S(1)} collective-permute-done((bf16[4,4,256,128]{3,2,1,0:T(8,128)(2,1)S(1)}, bf16[4,4,256,128]{3,2,1,0:T(8,128)(2,1)S(1)}, u32[]{:S(2)}, u32[]{:S(2)}) %collective-permute-start.3) | collective-permute-done | bytes 1048608 | tf_op jit(solution)/shard_map/ppermute | solution.py:113
  143.0 0.0 copy-done
  143.0 1.2 shard_map.30
  144.3 11.6 %all_to_all.28 = bf16[4,2,256,128]{3,2,1,0:T(8,128)(2,1)S(1)} all-to-all(bf16[4,2,256,128]{3,2,1,0:T(8,128)(2,1)S(1)} %shard_map.30), channel_id=1, replica_groups=mesh['x'=4,'zl'=8,'y'=4,'zh'=2,'c'=2] {'x'}, dimensions={0} | all-to-all | bytes 1048576 | tf_op jit(solution)/shard_map/all_to_all | solution.py:167
  155.9 0.1 reduce_sum.31
  156.0 7.0 %collective-permute-start.4 = (bf16[512,128]{1,0:T(8,128)(2,1)S(1)}, bf16[512,128]{1,0:T(8,128)(2,1)S(1)}, u32[]{:S(2)}, u32[]{:S(2)}) collective-permute-start(bf16[512,128]{1,0:T(8,128)(2,1)S(1)} %bitcast.30), channel_id=1, source_target_pairs={{0,2},{2,0},{1,3},{3,1},{4,6},{6,4},{5,7},{7,5},{8,10},{10,8},{9,1... | collective-permute-start | bytes 393224 | tf_op jit(solution)/shard_map/ppermute | solution.py:172
  163.0 0.0 copy-start.1
  163.0 2.2 %copy-done.1 = bf16[8192,256]{1,0:T(8,128)(2,1)S(1)} copy-done((bf16[8192,256]{1,0:T(8,128)(2,1)S(1)}, bf16[8192,256]{1,0:T(8,128)(2,1)}, u32[]{:S(2)}) %copy-start.1) | copy-done | bytes 4194328
  165.2 1.2 shard_map.29
  166.4 0.0 copy-start.2
  166.5 10.6 %conditional.1 = (f32[512,128]{1,0:T(8,128)S(1)}) conditional(s32[]{:T(128)} %convert_element_type.29, () %tuple.12, bf16[4,2,256,128]{3,2,1,0:T(8,128)(2,1)S(1)} %shard_map.29), branch_computations={%region_1.2_spmd, %region_2.4_spmd} | conditional | flops 458752 | bytes 1835016 | solution.py:173
  166.5 10.6 %all_to_all.24 = bf16[4,2,256,128]{3,2,1,0:T(8,128)(2,1)S(1)} all-to-all(bf16[4,2,256,128]{3,2,1,0:T(8,128)(2,1)S(1)} %param.1), channel_id=1, replica_groups=mesh['x'=4,'zl'=8,'y'=4,'zh'=2,'c'=2] {'x'}, dimensions={0} | all-to-all | bytes 1048576 | tf_op jit(solution)/shard_map/cond/branch_1_fun/all_to_all | solution.py:167
  177.0 0.1 convert_reduce_fusion
  177.1 0.0 collective-permute-done.4
  177.2 0.0 copy-done.2
  177.2 0.9 maximum_add_fusion
  (6 shorter events, 0.1 us)
Async XLA Ops:
  6.5 80.8 %all-gather.3.cloned.1.call-start = ((), (), s32[]{:S(2)}) async-start(), calls=%async_computation.5 | async-start | bytes 4456448 | tf_op jit(solution)/shard_map/all_gather | solution.py:140
  9.4 18.9 %collective-permute-start = (bf16[512,128]{1,0:T(8,128)(2,1)S(1)}, bf16[512,128]{1,0:T(8,128)(2,1)S(1)}, u32[]{:S(2)}, u32[]{:S(2)}) collective-permute-start(bf16[512,128]{1,0:T(8,128)(2,1)S(1)} %broadcast_select_fusion.2), channel_id=1, source_target_pairs={{0,2},{2,0},{1,3},{3,1},{4,6},{6,4},{5,7},{7,5},{8,10},{10,8},{9,1... | collective-permute-start | bytes 393224 | tf_op jit(solution)/shard_map/ppermute | solution.py:147
  28.4 0.7 collective-permute-start.1
  65.0 6.7 %collective-permute-start.2 = (bf16[4,4,256,128]{3,2,1,0:T(8,128)(2,1)S(1)}, bf16[4,4,256,128]{3,2,1,0:T(8,128)(2,1)S(1)}, u32[]{:S(2)}, u32[]{:S(2)}) collective-permute-start(bf16[4,4,256,128]{3,2,1,0:T(8,128)(2,1)S(1)} %all_to_all.25), channel_id=1, source_target_pairs={{0,1},{1,0},{2,3},{3,2},{4,5},{5,4},{6,7},{7,6},{8,9},{9,8},{10,11... | collective-permute-start | bytes 3145736 | tf_op jit(solution)/shard_map/ppermute | solution.py:113
  112.2 30.8 %copy-start = (bf16[8192,256]{1,0:T(8,128)(2,1)S(1)}, bf16[8192,256]{1,0:T(8,128)(2,1)}, u32[]{:S(2)}) copy-start(bf16[8192,256]{1,0:T(8,128)(2,1)} %all-gather.3.cloned.1.call-done) | copy-start | bytes 12582916
  127.5 15.5 %collective-permute-start.3 = (bf16[4,4,256,128]{3,2,1,0:T(8,128)(2,1)S(1)}, bf16[4,4,256,128]{3,2,1,0:T(8,128)(2,1)S(1)}, u32[]{:S(2)}, u32[]{:S(2)}) collective-permute-start(bf16[4,4,256,128]{3,2,1,0:T(8,128)(2,1)S(1)} %bitcast.20), channel_id=1, source_target_pairs={{0,1},{1,0},{2,3},{3,2},{4,5},{5,4},{6,7},{7,6},{8,9},{9,8},{10,11... | collective-permute-start | bytes 3145736 | tf_op jit(solution)/shard_map/ppermute | solution.py:113
  156.0 21.1 %collective-permute-start.4 = (bf16[512,128]{1,0:T(8,128)(2,1)S(1)}, bf16[512,128]{1,0:T(8,128)(2,1)S(1)}, u32[]{:S(2)}, u32[]{:S(2)}) collective-permute-start(bf16[512,128]{1,0:T(8,128)(2,1)S(1)} %bitcast.30), channel_id=1, source_target_pairs={{0,2},{2,0},{1,3},{3,1},{4,6},{6,4},{5,7},{7,5},{8,10},{10,8},{9,1... | collective-permute-start | bytes 393224 | tf_op jit(solution)/shard_map/ppermute | solution.py:172
  163.0 2.2 %copy-start.1 = (bf16[8192,256]{1,0:T(8,128)(2,1)S(1)}, bf16[8192,256]{1,0:T(8,128)(2,1)}, u32[]{:S(2)}) copy-start(bf16[8192,256]{1,0:T(8,128)(2,1)} %all-gather.3.cloned.1.call-done) | copy-start | bytes 12582916
  166.4 10.7 %copy-start.2 = (f32[512,256]{1,0:T(8,128)S(1)}, f32[512,256]{1,0:T(8,128)}, u32[]{:S(2)}) copy-start(f32[512,256]{1,0:T(8,128)} %param.4) | copy-start | bytes 1572868
Sparse Core Ops, SparseCore 0:
  9.4 77.8 all-gather.2

commit v10 on v9

--- a/solution.py
+++ b/solution.py
@@ -46,27 +46,19 @@
 def dot_all_kernel(z_ref, right_ref, out_ref, left, sem):
     groups, _, depth, width = out_ref.shape
     copies = [pltpu.make_async_copy(z_ref.at[n], left.at[n], sem.at[n]) for n in range(16)]
-    ahead = 4
-    for copy in copies[:ahead]:
+    for copy in copies:
         copy.start()
     for zh in range(2):
-        for h in range(2):
-            cols = slice(h * 2 * width, (h + 1) * 2 * width)
-            total = None
-            for k in range(8):
-                if h == 0:
-                    copies[zh * 8 + k].wait()
-                    if zh * 8 + k + ahead < 16:
-                        copies[zh * 8 + k + ahead].start()
-                term = jnp.dot(
-                    left[zh * 8 + k], right_ref[k, :, cols], preferred_element_type=jnp.float32
-                )
-                total = term if total is None else total + term
-            total = total.astype(out_ref.dtype)
-            for s in range(2):
-                for j in range(2):
-                    block = total[s * depth : (s + 1) * depth, j * width : (j + 1) * width]
-                    out_ref[h * 2 + j, zh * 2 + s] = block
+        total = None
+        for k in range(8):
+            copies[zh * 8 + k].wait()
+            term = jnp.dot(left[zh * 8 + k], right_ref[k], preferred_element_type=jnp.float32)
+            total = term if total is None else total + term
+        total = total.astype(out_ref.dtype)
+        for s in range(2):
+            for j in range(groups):
+                block = total[s * depth : (s + 1) * depth, j * width : (j + 1) * width]
+                out_ref[j, zh * 2 + s] = block
 
 
 def dot_right_all(z_rows, own, other):

time: 186 us -> 184 us (0.989)
  Pallas kernels: 9.12 us -> 6.78 us
    pallas_call x1, Pallas kernels: 6.62 us -> 4.29 us  [dot_right_all(): pl.pallas_call(dot_all_kernel, in_specs=[pl.BlockSpec(memory_space=pl.ANY...]
where the time goes in v10:
time: 184 us; the launch traced here: 183 us
  blocking collectives  91 us (49%)
  starting transfers between devices  41.6 us (23%)
  waiting for transfers between devices  15.2 us (8%)
  between operations  13.7 us (7%)
  other arithmetic  7.33 us (4%)
  local copies, waits for them, and re-layouts  6.96 us (4%)
  Pallas kernels  6.78 us (4%)
    all_to_all x1, blocking collectives, shards(): y_own = lax.all_to_all(jnp.stack([turned] * 4), 'y', 0, 0, tiled=True)  35.7 us
    all_to_all x2, blocking collectives, sum_x(): part = lax.all_to_all(part, 'x', 0, 0, tiled=True)  22.2 us
    all_to_all x1, blocking collectives, shards(): part = lax.all_to_all(part.reshape(16, 256, 128), PLANE, 0, 0, tiled=True)  18.1 us
    ppermute x2, starting transfers between devices, other_core(): return lax.ppermute(block, 'c', SWAP)  17.7 us
    ppermute x1, starting transfers between devices, shards(): yours = lax.ppermute(jnp.where(low, right, left), 'zh', SWAP)  16.3 us
    all_to_all x1, blocking collectives, shards(): lax.all_to_all(spread, PLANE, 0, 0, tiled=True).reshape(4, 4, 256, 128)  15 us
    all_gather x1, waiting for transfers between devices, shards(): z_rows = lax.all_gather(z_half, AXES, axis_index_groups=Z_RINGS)  8.19 us
    ppermute x1, starting transfers between devices, shards(): yours = lax.ppermute(yours, 'zh', SWAP).astype(jnp.float32)  6.97 us
  transfers between devices with their start and end apart: 6, of which 4 were waited for; matrix products, arithmetic and copies ran while one was open for 5% of the time, Pallas kernels for 1%

profile of v10, /device:TPU:1, one launch (start us, length us, event | category | flops | bytes accessed | tf_op | source)
XLA Modules:
  0.0 182.5 jit_solution(16774519829051752379)
XLA Ops:
  6.5 0.0 all-gather.3.cloned.1.call-start
  6.5 1.8 convert_element_type.30
  8.3 0.0 all-gather.3.cloned.1.call-update
  8.3 1.1 convert_element_type.31
  9.4 16.3 %collective-permute-start = (bf16[512,128]{1,0:T(8,128)(2,1)S(1)}, bf16[512,128]{1,0:T(8,128)(2,1)S(1)}, u32[]{:S(2)}, u32[]{:S(2)}) collective-permute-start(bf16[512,128]{1,0:T(8,128)(2,1)S(1)} %broadcast_select_fusion.2), channel_id=1, source_target_pairs={{0,2},{2,0},{1,3},{3,1},{4,6},{6,4},{5,7},{7,5},{8,10},{10,8},{9,1... | collective-permute-start | bytes 393224 | tf_op jit(solution)/shard_map/ppermute | solution.py:139
  25.7 2.6 %collective-permute-done = bf16[512,128]{1,0:T(8,128)(2,1)S(1)} collective-permute-done((bf16[512,128]{1,0:T(8,128)(2,1)S(1)}, bf16[512,128]{1,0:T(8,128)(2,1)S(1)}, u32[]{:S(2)}, u32[]{:S(2)}) %collective-permute-start) | collective-permute-done | bytes 131104 | tf_op jit(solution)/shard_map/ppermute | solution.py:139
  28.4 0.7 collective-permute-start.1
  29.1 0.0 collective-permute-done.1
  29.1 0.2 stack.28
  29.3 35.7 %all_to_all.25 = bf16[4,4,256,128]{3,2,1,0:T(8,128)(2,1)S(1)} all-to-all(bf16[4,4,256,128]{3,2,1,0:T(8,128)(2,1)S(1)} %stack.28), channel_id=1, replica_groups=mesh['x'=4,'zl'=8,'y'=4,'zh'=2,'c'=2] {'y'}, dimensions={0} | all-to-all | bytes 2097152 | tf_op jit(solution)/shard_map/all_to_all | solution.py:145
  65.0 4.4 %collective-permute-start.2 = (bf16[4,4,256,128]{3,2,1,0:T(8,128)(2,1)S(1)}, bf16[4,4,256,128]{3,2,1,0:T(8,128)(2,1)S(1)}, u32[]{:S(2)}, u32[]{:S(2)}) collective-permute-start(bf16[4,4,256,128]{3,2,1,0:T(8,128)(2,1)S(1)} %all_to_all.25), channel_id=1, source_target_pairs={{0,1},{1,0},{2,3},{3,2},{4,5},{5,4},{6,7},{7,6},{8,9},{9,8},{10,11... | collective-permute-start | bytes 3145736 | tf_op jit(solution)/shard_map/ppermute | solution.py:105
  69.5 0.1 fusion
  69.7 2.1 %collective-permute-done.2 = bf16[4,4,256,128]{3,2,1,0:T(8,128)(2,1)S(1)} collective-permute-done((bf16[4,4,256,128]{3,2,1,0:T(8,128)(2,1)S(1)}, bf16[4,4,256,128]{3,2,1,0:T(8,128)(2,1)S(1)}, u32[]{:S(2)}, u32[]{:S(2)}) %collective-permute-start.2) | collective-permute-done | bytes 1048608 | tf_op jit(solution)/shard_map/ppermute | solution.py:105
  71.7 0.1 broadcast_select_fusion.1
  71.9 0.8 copy.3
  72.7 0.8 copy.4
  73.5 2.8 %maximum_bitcast_fusion = bf16[2,2,2,256,4,128]{5,4,3,2,1,0:T(4,128)(2,1)} fusion(bf16[1,4,2,2,256,128]{5,1,4,3,0,2:T(4,128)(2,1)S(1)} %copy.4, bf16[1,4,2,2,256,128]{5,1,4,3,0,2:T(4,128)(2,1)S(1)} %copy.3), kind=kLoop, calls=%fused_computation.1 | loop fusion | flops 1048576 | bytes 4194304 | tf_op jit(solution)/shard_map/transpose | solution.py:68
  76.4 2.7 %reshape.32.right_ref = bf16[8,256,512]{2,1,0:T(8,128)(2,1)S(1)} reshape(bf16[2,2,2,256,4,128]{5,4,3,2,1,0:T(4,128)(2,1)} %maximum_bitcast_fusion) | data formatting | bytes 4194304 | tf_op jit(solution)/shard_map/reshape | solution.py:69
  79.1 8.2 %all-gather.3.cloned.1.call-done = bf16[8192,256]{1,0:T(8,128)(2,1)} async-done(((bf16[512,256]{1,0:T(8,128)(2,1)}), bf16[8192,256]{1,0:T(8,128)(2,1)}) %all-gather.3.cloned.1.call-update) | async-done | bytes 4194320 | tf_op jit(solution)/shard_map/all_gather | solution.py:132
  87.3 4.3 %shard_map.28 = bf16[4,4,256,128]{3,2,1,0:T(8,128)(2,1)S(1)} custom-call(bf16[16,512,256]{2,1,0:T(8,128)(2,1)} %bitcast.17, bf16[8,256,512]{2,1,0:T(8,128)(2,1)S(1)} %reshape.32.right_ref), custom_call_target="tpu_custom_call" | custom-call | flops 2147483648 | bytes 7340032 | tf_op jit(solution)/shard_map/pallas_call | solution.py:70
  91.6 18.1 %all_to_all.26 = bf16[16,256,128]{2,1,0:T(8,128)(2,1)S(1)} all-to-all(bf16[16,256,128]{2,1,0:T(8,128)(2,1)S(1)} %bitcast.23), channel_id=1, replica_groups=mesh['x'=4,'zl'=8,'y'=4,'zh'=2,'c'=2] {'x','y'}, dimensions={0} | all-to-all | bytes 2097152 | tf_op jit(solution)/shard_map/all_to_all | solution.py:150
  109.7 0.2 convert_reduce_fusion.1
  109.9 0.0 copy-start
  109.9 0.1 subtract_convert_fusion
  110.0 0.2 broadcast_in_dim.16
  110.2 15.0 %all_to_all.27 = bf16[16,256,128]{2,1,0:T(8,128)(2,1)S(1)} all-to-all(bf16[16,256,128]{2,1,0:T(8,128)(2,1)S(1)} %bitcast.26), channel_id=1, replica_groups=mesh['x'=4,'zl'=8,'y'=4,'zh'=2,'c'=2] {'x','y'}, dimensions={0} | all-to-all | bytes 2097152 | tf_op jit(solution)/shard_map/all_to_all | solution.py:155
  125.2 13.3 %collective-permute-start.3 = (bf16[4,4,256,128]{3,2,1,0:T(8,128)(2,1)S(1)}, bf16[4,4,256,128]{3,2,1,0:T(8,128)(2,1)S(1)}, u32[]{:S(2)}, u32[]{:S(2)}) collective-permute-start(bf16[4,4,256,128]{3,2,1,0:T(8,128)(2,1)S(1)} %bitcast.20), channel_id=1, source_target_pairs={{0,1},{1,0},{2,3},{3,2},{4,5},{5,4},{6,7},{7,6},{8,9},{9,8},{10,11... | collective-permute-start | bytes 3145736 | tf_op jit(solution)/shard_map/ppermute | solution.py:105
  138.4 2.3 %collective-permute-done.3.other_ref = bf16[4,4,256,128]{3,2,1,0:T(8,128)(2,1)S(1)} collective-permute-done((bf16[4,4,256,128]{3,2,1,0:T(8,128)(2,1)S(1)}, bf16[4,4,256,128]{3,2,1,0:T(8,128)(2,1)S(1)}, u32[]{:S(2)}, u32[]{:S(2)}) %collective-permute-start.3) | collective-permute-done | bytes 1048608 | tf_op jit(solution)/shard_map/ppermute | solution.py:105
  140.7 0.0 copy-done
  140.7 1.2 shard_map.30
  142.0 11.6 %all_to_all.28 = bf16[4,2,256,128]{3,2,1,0:T(8,128)(2,1)S(1)} all-to-all(bf16[4,2,256,128]{3,2,1,0:T(8,128)(2,1)S(1)} %shard_map.30), channel_id=1, replica_groups=mesh['x'=4,'zl'=8,'y'=4,'zh'=2,'c'=2] {'x'}, dimensions={0} | all-to-all | bytes 1048576 | tf_op jit(solution)/shard_map/all_to_all | solution.py:159
  153.6 0.1 reduce_sum.31
  153.7 7.0 %collective-permute-start.4 = (bf16[512,128]{1,0:T(8,128)(2,1)S(1)}, bf16[512,128]{1,0:T(8,128)(2,1)S(1)}, u32[]{:S(2)}, u32[]{:S(2)}) collective-permute-start(bf16[512,128]{1,0:T(8,128)(2,1)S(1)} %bitcast.30), channel_id=1, source_target_pairs={{0,2},{2,0},{1,3},{3,1},{4,6},{6,4},{5,7},{7,5},{8,10},{10,8},{9,1... | collective-permute-start | bytes 393224 | tf_op jit(solution)/shard_map/ppermute | solution.py:164
  160.7 0.0 copy-start.1
  160.7 2.2 %copy-done.1 = bf16[8192,256]{1,0:T(8,128)(2,1)S(1)} copy-done((bf16[8192,256]{1,0:T(8,128)(2,1)S(1)}, bf16[8192,256]{1,0:T(8,128)(2,1)}, u32[]{:S(2)}) %copy-start.1) | copy-done | bytes 4194328
  162.8 1.2 shard_map.29
  164.1 0.0 copy-start.2
  164.1 10.6 %conditional.1 = (f32[512,128]{1,0:T(8,128)S(1)}) conditional(s32[]{:T(128)} %convert_element_type.29, () %tuple.12, bf16[4,2,256,128]{3,2,1,0:T(8,128)(2,1)S(1)} %shard_map.29), branch_computations={%region_1.2_spmd, %region_2.4_spmd} | conditional | flops 458752 | bytes 1835016 | solution.py:165
  164.1 10.6 %all_to_all.24 = bf16[4,2,256,128]{3,2,1,0:T(8,128)(2,1)S(1)} all-to-all(bf16[4,2,256,128]{3,2,1,0:T(8,128)(2,1)S(1)} %param.1), channel_id=1, replica_groups=mesh['x'=4,'zl'=8,'y'=4,'zh'=2,'c'=2] {'x'}, dimensions={0} | all-to-all | bytes 1048576 | tf_op jit(solution)/shard_map/cond/branch_1_fun/all_to_all | solution.py:159
  174.7 0.1 convert_reduce_fusion
  174.7 0.0 collective-permute-done.4
  174.8 0.0 copy-done.2
  174.8 0.9 maximum_add_fusion
  (6 shorter events, 0.1 us)
Async XLA Ops:
  6.5 80.8 %all-gather.3.cloned.1.call-start = ((), (), s32[]{:S(2)}) async-start(), calls=%async_computation.5 | async-start | bytes 4456448 | tf_op jit(solution)/shard_map/all_gather | solution.py:132
  9.4 18.9 %collective-permute-start = (bf16[512,128]{1,0:T(8,128)(2,1)S(1)}, bf16[512,128]{1,0:T(8,128)(2,1)S(1)}, u32[]{:S(2)}, u32[]{:S(2)}) collective-permute-start(bf16[512,128]{1,0:T(8,128)(2,1)S(1)} %broadcast_select_fusion.2), channel_id=1, source_target_pairs={{0,2},{2,0},{1,3},{3,1},{4,6},{6,4},{5,7},{7,5},{8,10},{10,8},{9,1... | collective-permute-start | bytes 393224 | tf_op jit(solution)/shard_map/ppermute | solution.py:139
  28.4 0.7 collective-permute-start.1
  65.0 6.7 %collective-permute-start.2 = (bf16[4,4,256,128]{3,2,1,0:T(8,128)(2,1)S(1)}, bf16[4,4,256,128]{3,2,1,0:T(8,128)(2,1)S(1)}, u32[]{:S(2)}, u32[]{:S(2)}) collective-permute-start(bf16[4,4,256,128]{3,2,1,0:T(8,128)(2,1)S(1)} %all_to_all.25), channel_id=1, source_target_pairs={{0,1},{1,0},{2,3},{3,2},{4,5},{5,4},{6,7},{7,6},{8,9},{9,8},{10,11... | collective-permute-start | bytes 3145736 | tf_op jit(solution)/shard_map/ppermute | solution.py:105
  109.9 30.8 %copy-start = (bf16[8192,256]{1,0:T(8,128)(2,1)S(1)}, bf16[8192,256]{1,0:T(8,128)(2,1)}, u32[]{:S(2)}) copy-start(bf16[8192,256]{1,0:T(8,128)(2,1)} %all-gather.3.cloned.1.call-done) | copy-start | bytes 12582916
  125.2 15.5 %collective-permute-start.3 = (bf16[4,4,256,128]{3,2,1,0:T(8,128)(2,1)S(1)}, bf16[4,4,256,128]{3,2,1,0:T(8,128)(2,1)S(1)}, u32[]{:S(2)}, u32[]{:S(2)}) collective-permute-start(bf16[4,4,256,128]{3,2,1,0:T(8,128)(2,1)S(1)} %bitcast.20), channel_id=1, source_target_pairs={{0,1},{1,0},{2,3},{3,2},{4,5},{5,4},{6,7},{7,6},{8,9},{9,8},{10,11... | collective-permute-start | bytes 3145736 | tf_op jit(solution)/shard_map/ppermute | solution.py:105
  153.7 21.1 %collective-permute-start.4 = (bf16[512,128]{1,0:T(8,128)(2,1)S(1)}, bf16[512,128]{1,0:T(8,128)(2,1)S(1)}, u32[]{:S(2)}, u32[]{:S(2)}) collective-permute-start(bf16[512,128]{1,0:T(8,128)(2,1)S(1)} %bitcast.30), channel_id=1, source_target_pairs={{0,2},{2,0},{1,3},{3,1},{4,6},{6,4},{5,7},{7,5},{8,10},{10,8},{9,1... | collective-permute-start | bytes 393224 | tf_op jit(solution)/shard_map/ppermute | solution.py:164
  160.7 2.2 %copy-start.1 = (bf16[8192,256]{1,0:T(8,128)(2,1)S(1)}, bf16[8192,256]{1,0:T(8,128)(2,1)}, u32[]{:S(2)}) copy-start(bf16[8192,256]{1,0:T(8,128)(2,1)} %all-gather.3.cloned.1.call-done) | copy-start | bytes 12582916
  164.1 10.7 %copy-start.2 = (f32[512,256]{1,0:T(8,128)S(1)}, f32[512,256]{1,0:T(8,128)}, u32[]{:S(2)}) copy-start(f32[512,256]{1,0:T(8,128)} %param.4) | copy-start | bytes 1572868
Sparse Core Ops, SparseCore 0:
  9.4 77.8 all-gather.2

commit v11 on v10

--- a/solution.py
+++ b/solution.py
@@ -159,8 +159,10 @@
         part = lax.all_to_all(part, "x", 0, 0, tiled=True)
         return part.astype(jnp.float32).sum(0).reshape(512, 128)
 
-    yours = sum_x(dot_right(1, z_rows, own, other)).astype(jnp.bfloat16)
+    yours = dot_right(1, z_rows, own, other)
     mine = dot_right(0, z_rows, own, other)
+    yours, mine = lax.optimization_barrier((yours, mine))
+    yours = sum_x(yours).astype(jnp.bfloat16)
     yours = lax.ppermute(yours, "zh", SWAP).astype(jnp.float32)
     mine = lax.cond(
         at("c") < 2, sum_x, lambda part: jnp.zeros((512, 128), jnp.float32), mine

time: 184 us -> 185 us (level)
  local copies, waits for them, and re-layouts: 6.96 us -> 4.78 us
    unnamed x6 -> x4, local copies, waits for them, and re-layouts: 2.19 us -> 0.01 us
  transfers between devices with their start and end apart: 6 -> 6, of which waited for: 4 -> 5; matrix products, arithmetic and copies ran while one was open for 5% -> 5% of each run, Pallas kernels for 1% -> 0%
where the time goes in v11:
time: 185 us; the launch traced here: 182 us
  blocking collectives  90.7 us (49%)
  starting transfers between devices  41.7 us (23%)
  waiting for transfers between devices  17 us (9%)
  between operations  13.6 us (7%)
  other arithmetic  7.33 us (4%)
  Pallas kernels  6.78 us (4%)
  local copies, waits for them, and re-layouts  4.78 us (3%)
    all_to_all x1, blocking collectives, shards(): y_own = lax.all_to_all(jnp.stack([turned] * 4), 'y', 0, 0, tiled=True)  35.7 us
    all_to_all x2, blocking collectives, sum_x(): part = lax.all_to_all(part, 'x', 0, 0, tiled=True)  21.8 us
    all_to_all x1, blocking collectives, shards(): part = lax.all_to_all(part.reshape(16, 256, 128), PLANE, 0, 0, tiled=True)  18.1 us
    ppermute x2, starting transfers between devices, other_core(): return lax.ppermute(block, 'c', SWAP)  17.7 us
    ppermute x1, starting transfers between devices, shards(): yours = lax.ppermute(jnp.where(low, right, left), 'zh', SWAP)  16.3 us
    all_to_all x1, blocking collectives, shards(): lax.all_to_all(spread, PLANE, 0, 0, tiled=True).reshape(4, 4, 256, 128)  15 us
    all_gather x1, waiting for transfers between devices, shards(): z_rows = lax.all_gather(z_half, AXES, axis_index_groups=Z_RINGS)  8.19 us
    ppermute x1, starting transfers between devices, shards(): yours = lax.ppermute(yours, 'zh', SWAP).astype(jnp.float32)  7.11 us
  transfers between devices with their start and end apart: 6, of which 5 were waited for; matrix products, arithmetic and copies ran while one was open for 5% of the time, Pallas kernels for 0%

profile of v11, /device:TPU:1, one launch (start us, length us, event | category | flops | bytes accessed | tf_op | source)
XLA Modules:
  0.0 181.9 jit_solution(3964285366241501500)
XLA Ops:
  6.5 0.0 all-gather.3.cloned.1.call-start
  6.5 1.8 convert_element_type.30
  8.3 0.0 all-gather.3.cloned.1.call-update
  8.3 1.1 convert_element_type.31
  9.4 16.3 %collective-permute-start = (bf16[512,128]{1,0:T(8,128)(2,1)S(1)}, bf16[512,128]{1,0:T(8,128)(2,1)S(1)}, u32[]{:S(2)}, u32[]{:S(2)}) collective-permute-start(bf16[512,128]{1,0:T(8,128)(2,1)S(1)} %broadcast_select_fusion.2), channel_id=1, source_target_pairs={{0,2},{2,0},{1,3},{3,1},{4,6},{6,4},{5,7},{7,5},{8,10},{10,8},{9,1... | collective-permute-start | bytes 393224 | tf_op jit(solution)/shard_map/ppermute | solution.py:139
  25.7 2.6 %collective-permute-done = bf16[512,128]{1,0:T(8,128)(2,1)S(1)} collective-permute-done((bf16[512,128]{1,0:T(8,128)(2,1)S(1)}, bf16[512,128]{1,0:T(8,128)(2,1)S(1)}, u32[]{:S(2)}, u32[]{:S(2)}) %collective-permute-start) | collective-permute-done | bytes 131104 | tf_op jit(solution)/shard_map/ppermute | solution.py:139
  28.4 0.7 collective-permute-start.1
  29.1 0.0 collective-permute-done.1
  29.1 0.2 stack.28
  29.3 35.7 %all_to_all.25 = bf16[4,4,256,128]{3,2,1,0:T(8,128)(2,1)S(1)} all-to-all(bf16[4,4,256,128]{3,2,1,0:T(8,128)(2,1)S(1)} %stack.28), channel_id=1, replica_groups=mesh['x'=4,'zl'=8,'y'=4,'zh'=2,'c'=2] {'y'}, dimensions={0} | all-to-all | bytes 2097152 | tf_op jit(solution)/shard_map/all_to_all | solution.py:145
  65.0 4.4 %collective-permute-start.2 = (bf16[4,4,256,128]{3,2,1,0:T(8,128)(2,1)S(1)}, bf16[4,4,256,128]{3,2,1,0:T(8,128)(2,1)S(1)}, u32[]{:S(2)}, u32[]{:S(2)}) collective-permute-start(bf16[4,4,256,128]{3,2,1,0:T(8,128)(2,1)S(1)} %all_to_all.25), channel_id=1, source_target_pairs={{0,1},{1,0},{2,3},{3,2},{4,5},{5,4},{6,7},{7,6},{8,9},{9,8},{10,11... | collective-permute-start | bytes 3145736 | tf_op jit(solution)/shard_map/ppermute | solution.py:105
  69.5 0.1 fusion
  69.7 2.1 %collective-permute-done.2 = bf16[4,4,256,128]{3,2,1,0:T(8,128)(2,1)S(1)} collective-permute-done((bf16[4,4,256,128]{3,2,1,0:T(8,128)(2,1)S(1)}, bf16[4,4,256,128]{3,2,1,0:T(8,128)(2,1)S(1)}, u32[]{:S(2)}, u32[]{:S(2)}) %collective-permute-start.2) | collective-permute-done | bytes 1048608 | tf_op jit(solution)/shard_map/ppermute | solution.py:105
  71.7 0.1 broadcast_select_fusion.1
  71.9 0.8 copy.3
  72.7 0.8 copy.4
  73.5 2.8 %maximum_bitcast_fusion = bf16[2,2,2,256,4,128]{5,4,3,2,1,0:T(4,128)(2,1)} fusion(bf16[1,4,2,2,256,128]{5,1,4,3,0,2:T(4,128)(2,1)S(1)} %copy.4, bf16[1,4,2,2,256,128]{5,1,4,3,0,2:T(4,128)(2,1)S(1)} %copy.3), kind=kLoop, calls=%fused_computation.1 | loop fusion | flops 1048576 | bytes 4194304 | tf_op jit(solution)/shard_map/transpose | solution.py:68
  76.4 2.7 %reshape.32.right_ref = bf16[8,256,512]{2,1,0:T(8,128)(2,1)S(1)} reshape(bf16[2,2,2,256,4,128]{5,4,3,2,1,0:T(4,128)(2,1)} %maximum_bitcast_fusion) | data formatting | bytes 4194304 | tf_op jit(solution)/shard_map/reshape | solution.py:69
  79.1 8.2 %all-gather.3.cloned.1.call-done = bf16[8192,256]{1,0:T(8,128)(2,1)} async-done(((bf16[512,256]{1,0:T(8,128)(2,1)}), bf16[8192,256]{1,0:T(8,128)(2,1)}) %all-gather.3.cloned.1.call-update) | async-done | bytes 4194320 | tf_op jit(solution)/shard_map/all_gather | solution.py:132
  87.3 4.3 %shard_map.28 = bf16[4,4,256,128]{3,2,1,0:T(8,128)(2,1)S(1)} custom-call(bf16[16,512,256]{2,1,0:T(8,128)(2,1)} %bitcast.17, bf16[8,256,512]{2,1,0:T(8,128)(2,1)S(1)} %reshape.32.right_ref), custom_call_target="tpu_custom_call" | custom-call | flops 2147483648 | bytes 7340032 | tf_op jit(solution)/shard_map/pallas_call | solution.py:70
  91.6 18.1 %all_to_all.26 = bf16[16,256,128]{2,1,0:T(8,128)(2,1)S(1)} all-to-all(bf16[16,256,128]{2,1,0:T(8,128)(2,1)S(1)} %bitcast.23), channel_id=1, replica_groups=mesh['x'=4,'zl'=8,'y'=4,'zh'=2,'c'=2] {'x','y'}, dimensions={0} | all-to-all | bytes 2097152 | tf_op jit(solution)/shard_map/all_to_all | solution.py:150
  109.7 0.2 convert_reduce_fusion.1
  109.9 0.0 copy-start
  109.9 0.1 subtract_convert_fusion
  110.0 0.2 broadcast_in_dim.16
  110.2 15.0 %all_to_all.27 = bf16[16,256,128]{2,1,0:T(8,128)(2,1)S(1)} all-to-all(bf16[16,256,128]{2,1,0:T(8,128)(2,1)S(1)} %bitcast.26), channel_id=1, replica_groups=mesh['x'=4,'zl'=8,'y'=4,'zh'=2,'c'=2] {'x','y'}, dimensions={0} | all-to-all | bytes 2097152 | tf_op jit(solution)/shard_map/all_to_all | solution.py:155
  125.2 13.3 %collective-permute-start.3 = (bf16[4,4,256,128]{3,2,1,0:T(8,128)(2,1)S(1)}, bf16[4,4,256,128]{3,2,1,0:T(8,128)(2,1)S(1)}, u32[]{:S(2)}, u32[]{:S(2)}) collective-permute-start(bf16[4,4,256,128]{3,2,1,0:T(8,128)(2,1)S(1)} %bitcast.20), channel_id=1, source_target_pairs={{0,1},{1,0},{2,3},{3,2},{4,5},{5,4},{6,7},{7,6},{8,9},{9,8},{10,11... | collective-permute-start | bytes 3145736 | tf_op jit(solution)/shard_map/ppermute | solution.py:105
  138.4 2.3 %collective-permute-done.3.other_ref = bf16[4,4,256,128]{3,2,1,0:T(8,128)(2,1)S(1)} collective-permute-done((bf16[4,4,256,128]{3,2,1,0:T(8,128)(2,1)S(1)}, bf16[4,4,256,128]{3,2,1,0:T(8,128)(2,1)S(1)}, u32[]{:S(2)}, u32[]{:S(2)}) %collective-permute-start.3) | collective-permute-done | bytes 1048608 | tf_op jit(solution)/shard_map/ppermute | solution.py:105
  140.7 0.0 copy-done
  140.7 1.2 shard_map.30
  142.0 1.2 shard_map.29
  143.2 11.6 %all_to_all.28 = bf16[4,2,256,128]{3,2,1,0:T(8,128)(2,1)S(1)} all-to-all(bf16[4,2,256,128]{3,2,1,0:T(8,128)(2,1)S(1)} %shard_map.29), channel_id=1, replica_groups=mesh['x'=4,'zl'=8,'y'=4,'zh'=2,'c'=2] {'x'}, dimensions={0} | all-to-all | bytes 1048576 | tf_op jit(solution)/shard_map/all_to_all | solution.py:159
  154.8 0.0 copy-start.1
  154.8 0.1 reduce_sum.31
  154.9 7.1 %collective-permute-start.4 = (bf16[512,128]{1,0:T(8,128)(2,1)S(1)}, bf16[512,128]{1,0:T(8,128)(2,1)S(1)}, u32[]{:S(2)}, u32[]{:S(2)}) collective-permute-start(bf16[512,128]{1,0:T(8,128)(2,1)S(1)} %bitcast.30), channel_id=1, source_target_pairs={{0,2},{2,0},{1,3},{3,1},{4,6},{6,4},{5,7},{7,5},{8,10},{10,8},{9,1... | collective-permute-start | bytes 393224 | tf_op jit(solution)/shard_map/ppermute | solution.py:166
  162.0 10.3 %conditional.1 = (f32[512,128]{1,0:T(8,128)S(1)}) conditional(s32[]{:T(128)} %convert_element_type.29, () %tuple.13, bf16[4,2,256,128]{3,2,1,0:T(8,128)(2,1)S(1)} %shard_map.30), branch_computations={%region_1.2_spmd, %region_2.4_spmd} | conditional | flops 458752 | bytes 1835016 | solution.py:167
  162.0 10.2 %all_to_all.24 = bf16[4,2,256,128]{3,2,1,0:T(8,128)(2,1)S(1)} all-to-all(bf16[4,2,256,128]{3,2,1,0:T(8,128)(2,1)S(1)} %param.1), channel_id=1, replica_groups=mesh['x'=4,'zl'=8,'y'=4,'zh'=2,'c'=2] {'x'}, dimensions={0} | all-to-all | bytes 1048576 | tf_op jit(solution)/shard_map/cond/branch_1_fun/all_to_all | solution.py:159
  172.3 0.1 convert_reduce_fusion
  172.3 1.8 collective-permute-done.4
  174.2 0.0 copy-done.1
  174.2 0.9 maximum_add_fusion
  (6 shorter events, 0.1 us)
Async XLA Ops:
  6.5 80.8 %all-gather.3.cloned.1.call-start = ((), (), s32[]{:S(2)}) async-start(), calls=%async_computation.5 | async-start | bytes 4456448 | tf_op jit(solution)/shard_map/all_gather | solution.py:132
  9.4 18.9 %collective-permute-start = (bf16[512,128]{1,0:T(8,128)(2,1)S(1)}, bf16[512,128]{1,0:T(8,128)(2,1)S(1)}, u32[]{:S(2)}, u32[]{:S(2)}) collective-permute-start(bf16[512,128]{1,0:T(8,128)(2,1)S(1)} %broadcast_select_fusion.2), channel_id=1, source_target_pairs={{0,2},{2,0},{1,3},{3,1},{4,6},{6,4},{5,7},{7,5},{8,10},{10,8},{9,1... | collective-permute-start | bytes 393224 | tf_op jit(solution)/shard_map/ppermute | solution.py:139
  28.4 0.7 collective-permute-start.1
  65.0 6.7 %collective-permute-start.2 = (bf16[4,4,256,128]{3,2,1,0:T(8,128)(2,1)S(1)}, bf16[4,4,256,128]{3,2,1,0:T(8,128)(2,1)S(1)}, u32[]{:S(2)}, u32[]{:S(2)}) collective-permute-start(bf16[4,4,256,128]{3,2,1,0:T(8,128)(2,1)S(1)} %all_to_all.25), channel_id=1, source_target_pairs={{0,1},{1,0},{2,3},{3,2},{4,5},{5,4},{6,7},{7,6},{8,9},{9,8},{10,11... | collective-permute-start | bytes 3145736 | tf_op jit(solution)/shard_map/ppermute | solution.py:105
  109.9 30.8 %copy-start = (bf16[8192,256]{1,0:T(8,128)(2,1)S(1)}, bf16[8192,256]{1,0:T(8,128)(2,1)}, u32[]{:S(2)}) copy-start(bf16[8192,256]{1,0:T(8,128)(2,1)} %all-gather.3.cloned.1.call-done) | copy-start | bytes 12582916
  125.2 15.5 %collective-permute-start.3 = (bf16[4,4,256,128]{3,2,1,0:T(8,128)(2,1)S(1)}, bf16[4,4,256,128]{3,2,1,0:T(8,128)(2,1)S(1)}, u32[]{:S(2)}, u32[]{:S(2)}) collective-permute-start(bf16[4,4,256,128]{3,2,1,0:T(8,128)(2,1)S(1)} %bitcast.20), channel_id=1, source_target_pairs={{0,1},{1,0},{2,3},{3,2},{4,5},{5,4},{6,7},{7,6},{8,9},{9,8},{10,11... | collective-permute-start | bytes 3145736 | tf_op jit(solution)/shard_map/ppermute | solution.py:105
  154.8 19.3 %copy-start.1 = (f32[512,256]{1,0:T(8,128)S(1)}, f32[512,256]{1,0:T(8,128)}, u32[]{:S(2)}) copy-start(f32[512,256]{1,0:T(8,128)} %param.4) | copy-start | bytes 1572868
  154.9 19.2 %collective-permute-start.4 = (bf16[512,128]{1,0:T(8,128)(2,1)S(1)}, bf16[512,128]{1,0:T(8,128)(2,1)S(1)}, u32[]{:S(2)}, u32[]{:S(2)}) collective-permute-start(bf16[512,128]{1,0:T(8,128)(2,1)S(1)} %bitcast.30), channel_id=1, source_target_pairs={{0,2},{2,0},{1,3},{3,1},{4,6},{6,4},{5,7},{7,5},{8,10},{10,8},{9,1... | collective-permute-start | bytes 393224 | tf_op jit(solution)/shard_map/ppermute | solution.py:166
Sparse Core Ops, SparseCore 0:
  9.4 77.8 all-gather.2

commit v12 on v10

--- a/solution.py
+++ b/solution.py
@@ -135,14 +135,13 @@
     low = zh == 0
     first_col = at("x") * 2048 + at("zl") * 256 + zh * 128
     left, right = y_half[:, :128], y_half[:, 128:]
-    mine = jnp.where(low, left, right)
-    yours = lax.ppermute(jnp.where(low, right, left), "zh", SWAP)
+    turn = [(i * 4 + j, j * 4 + i) for i in range(4) for j in range(4)]
+    turn_swap = [(a * 2 + h, b * 2 + 1 - h) for a, b in turn for h in range(2)]
+    yours = lax.ppermute(jnp.where(low, right, left), PLANE + ("zh",), turn_swap)
+    mine = lax.ppermute(jnp.where(low, left, right), PLANE, turn)
     y_both = jnp.stack([jnp.where(low, mine, yours), jnp.where(low, yours, mine)])
     y_both = y_both.reshape(4, 256, 128)
-
-    turn = [(i * 4 + j, j * 4 + i) for i in range(4) for j in range(4)]
-    turned = lax.ppermute(y_both, PLANE, turn)
-    y_own = lax.all_to_all(jnp.stack([turned] * 4), "y", 0, 0, tiled=True)
+    y_own = lax.all_to_all(jnp.stack([y_both] * 4), "y", 0, 0, tiled=True)
     y_other = other_core(y_own)
     y_other, ident = lax.optimization_barrier((y_other, make_ident((4, 256, 128), first_col)))
     part = dot_right_all(z_rows, y_own, y_other)

time: 184 us -> 187 us (1.016)
  blocking collectives: 91 us -> 95.3 us
    all_to_all x1, blocking collectives: 18.1 us -> 22.1 us  [shards(): part = lax.all_to_all(part.reshape(16, 256, 128), PLANE, 0, 0, tiled=True)]
where the time goes in v12:
time: 187 us; the launch traced here: 186 us
  blocking collectives  95.3 us (51%)
  starting transfers between devices  40.7 us (22%)
  waiting for transfers between devices  15.3 us (8%)
  between operations  13.7 us (7%)
  other arithmetic  7.34 us (4%)
  local copies, waits for them, and re-layouts  6.96 us (4%)
  Pallas kernels  6.75 us (4%)
    all_to_all x1, blocking collectives, shards(): y_own = lax.all_to_all(jnp.stack([y_both] * 4), 'y', 0, 0, tiled=True)  36.3 us
    all_to_all x1, blocking collectives, shards(): part = lax.all_to_all(part.reshape(16, 256, 128), PLANE, 0, 0, tiled=True)  22.1 us
    all_to_all x2, blocking collectives, sum_x(): part = lax.all_to_all(part, 'x', 0, 0, tiled=True)  22 us
    ppermute x2, starting transfers between devices, other_core(): return lax.ppermute(block, 'c', SWAP)  16.8 us
    ppermute x1, starting transfers between devices, shards(): lax.ppermute(jnp.where(low, right, left), PLANE + ('zh',), turn_swap)  16.3 us
    all_to_all x1, blocking collectives, shards(): lax.all_to_all(spread, PLANE, 0, 0, tiled=True).reshape(4, 4, 256, 128)  15 us
    all_gather x1, waiting for transfers between devices, shards(): z_rows = lax.all_gather(z_half, AXES, axis_index_groups=Z_RINGS)  8.32 us
    ppermute x1, starting transfers between devices, shards(): yours = lax.ppermute(yours, 'zh', SWAP).astype(jnp.float32)  6.96 us
  transfers between devices with their start and end apart: 6, of which 4 were waited for; matrix products, arithmetic and copies ran while one was open for 5% of the time, Pallas kernels for 1%

profile of v12, /device:TPU:1, one launch (start us, length us, event | category | flops | bytes accessed | tf_op | source)
XLA Modules:
  0.0 186.1 jit_solution(17404247986963461332)
XLA Ops:
  6.5 0.0 all-gather.3.cloned.1.call-start
  6.5 1.8 convert_element_type.30
  8.3 0.0 all-gather.3.cloned.1.call-update
  8.3 1.1 convert_element_type.31
  9.4 0.7 collective-permute-start
  10.1 16.3 %collective-permute-start.1 = (bf16[512,128]{1,0:T(8,128)(2,1)S(1)}, bf16[512,128]{1,0:T(8,128)(2,1)S(1)}, u32[]{:S(2)}, u32[]{:S(2)}) collective-permute-start(bf16[512,128]{1,0:T(8,128)(2,1)S(1)} %get-tuple-element.20), channel_id=1, source_target_pairs={{0,2},{2,0},{4,130},{6,128},{8,258},{10,256},{12,386},{14,384},{12... | collective-permute-start | bytes 393224 | tf_op jit(solution)/shard_map/ppermute | solution.py:140
  26.4 0.0 collective-permute-done
  26.4 2.6 %collective-permute-done.1 = bf16[512,128]{1,0:T(8,128)(2,1)S(1)} collective-permute-done((bf16[512,128]{1,0:T(8,128)(2,1)S(1)}, bf16[512,128]{1,0:T(8,128)(2,1)S(1)}, u32[]{:S(2)}, u32[]{:S(2)}) %collective-permute-start.1) | collective-permute-done | bytes 131104 | tf_op jit(solution)/shard_map/ppermute | solution.py:140
  29.1 0.2 stack.24
  29.3 36.3 %all_to_all.25 = bf16[4,4,256,128]{3,2,1,0:T(8,128)(2,1)S(1)} all-to-all(bf16[4,4,256,128]{3,2,1,0:T(8,128)(2,1)S(1)} %stack.24), channel_id=1, replica_groups=mesh['x'=4,'zl'=8,'y'=4,'zh'=2,'c'=2] {'y'}, dimensions={0} | all-to-all | bytes 2097152 | tf_op jit(solution)/shard_map/all_to_all | solution.py:144
  65.6 3.8 %collective-permute-start.2 = (bf16[4,4,256,128]{3,2,1,0:T(8,128)(2,1)S(1)}, bf16[4,4,256,128]{3,2,1,0:T(8,128)(2,1)S(1)}, u32[]{:S(2)}, u32[]{:S(2)}) collective-permute-start(bf16[4,4,256,128]{3,2,1,0:T(8,128)(2,1)S(1)} %all_to_all.25), channel_id=1, source_target_pairs={{0,1},{1,0},{2,3},{3,2},{4,5},{5,4},{6,7},{7,6},{8,9},{9,8},{10,11... | collective-permute-start | bytes 3145736 | tf_op jit(solution)/shard_map/ppermute | solution.py:105
  69.5 0.1 fusion
  69.6 2.1 %collective-permute-done.2 = bf16[4,4,256,128]{3,2,1,0:T(8,128)(2,1)S(1)} collective-permute-done((bf16[4,4,256,128]{3,2,1,0:T(8,128)(2,1)S(1)}, bf16[4,4,256,128]{3,2,1,0:T(8,128)(2,1)S(1)}, u32[]{:S(2)}, u32[]{:S(2)}) %collective-permute-start.2) | collective-permute-done | bytes 1048608 | tf_op jit(solution)/shard_map/ppermute | solution.py:105
  71.7 0.1 broadcast_select_fusion.1
  71.8 0.8 copy.3
  72.6 0.8 copy.4
  73.5 2.8 %maximum_bitcast_fusion = bf16[2,2,2,256,4,128]{5,4,3,2,1,0:T(4,128)(2,1)} fusion(bf16[1,4,2,2,256,128]{5,1,4,3,0,2:T(4,128)(2,1)S(1)} %copy.4, bf16[1,4,2,2,256,128]{5,1,4,3,0,2:T(4,128)(2,1)S(1)} %copy.3), kind=kLoop, calls=%fused_computation.1 | loop fusion | flops 1048576 | bytes 4194304 | tf_op jit(solution)/shard_map/transpose | solution.py:68
  76.3 2.7 %reshape.28.right_ref = bf16[8,256,512]{2,1,0:T(8,128)(2,1)S(1)} reshape(bf16[2,2,2,256,4,128]{5,4,3,2,1,0:T(4,128)(2,1)} %maximum_bitcast_fusion) | data formatting | bytes 4194304 | tf_op jit(solution)/shard_map/reshape | solution.py:69
  79.1 8.3 %all-gather.3.cloned.1.call-done = bf16[8192,256]{1,0:T(8,128)(2,1)} async-done(((bf16[512,256]{1,0:T(8,128)(2,1)}), bf16[8192,256]{1,0:T(8,128)(2,1)}) %all-gather.3.cloned.1.call-update) | async-done | bytes 4194320 | tf_op jit(solution)/shard_map/all_gather | solution.py:132
  87.4 4.3 %shard_map.28 = bf16[4,4,256,128]{3,2,1,0:T(8,128)(2,1)S(1)} custom-call(bf16[16,512,256]{2,1,0:T(8,128)(2,1)} %bitcast.17, bf16[8,256,512]{2,1,0:T(8,128)(2,1)S(1)} %reshape.28.right_ref), custom_call_target="tpu_custom_call" | custom-call | flops 2147483648 | bytes 7340032 | tf_op jit(solution)/shard_map/pallas_call | solution.py:70
  91.6 22.1 %all_to_all.26 = bf16[16,256,128]{2,1,0:T(8,128)(2,1)S(1)} all-to-all(bf16[16,256,128]{2,1,0:T(8,128)(2,1)S(1)} %bitcast.23), channel_id=1, replica_groups=mesh['x'=4,'zl'=8,'y'=4,'zh'=2,'c'=2] {'x','y'}, dimensions={0} | all-to-all | bytes 2097152 | tf_op jit(solution)/shard_map/all_to_all | solution.py:149
  113.7 0.2 convert_reduce_fusion.1
  113.9 0.0 copy-start
  113.9 0.1 subtract_convert_fusion
  114.0 0.2 broadcast_in_dim.16
  114.2 15.0 %all_to_all.27 = bf16[16,256,128]{2,1,0:T(8,128)(2,1)S(1)} all-to-all(bf16[16,256,128]{2,1,0:T(8,128)(2,1)S(1)} %bitcast.26), channel_id=1, replica_groups=mesh['x'=4,'zl'=8,'y'=4,'zh'=2,'c'=2] {'x','y'}, dimensions={0} | all-to-all | bytes 2097152 | tf_op jit(solution)/shard_map/all_to_all | solution.py:154
  129.2 13.0 %collective-permute-start.3 = (bf16[4,4,256,128]{3,2,1,0:T(8,128)(2,1)S(1)}, bf16[4,4,256,128]{3,2,1,0:T(8,128)(2,1)S(1)}, u32[]{:S(2)}, u32[]{:S(2)}) collective-permute-start(bf16[4,4,256,128]{3,2,1,0:T(8,128)(2,1)S(1)} %bitcast.20), channel_id=1, source_target_pairs={{0,1},{1,0},{2,3},{3,2},{4,5},{5,4},{6,7},{7,6},{8,9},{9,8},{10,11... | collective-permute-start | bytes 3145736 | tf_op jit(solution)/shard_map/ppermute | solution.py:105
  142.2 2.3 %collective-permute-done.3.other_ref = bf16[4,4,256,128]{3,2,1,0:T(8,128)(2,1)S(1)} collective-permute-done((bf16[4,4,256,128]{3,2,1,0:T(8,128)(2,1)S(1)}, bf16[4,4,256,128]{3,2,1,0:T(8,128)(2,1)S(1)}, u32[]{:S(2)}, u32[]{:S(2)}) %collective-permute-start.3) | collective-permute-done | bytes 1048608 | tf_op jit(solution)/shard_map/ppermute | solution.py:105
  144.4 0.0 copy-done
  144.4 1.2 shard_map.30
  145.7 11.6 %all_to_all.28 = bf16[4,2,256,128]{3,2,1,0:T(8,128)(2,1)S(1)} all-to-all(bf16[4,2,256,128]{3,2,1,0:T(8,128)(2,1)S(1)} %shard_map.30), channel_id=1, replica_groups=mesh['x'=4,'zl'=8,'y'=4,'zh'=2,'c'=2] {'x'}, dimensions={0} | all-to-all | bytes 1048576 | tf_op jit(solution)/shard_map/all_to_all | solution.py:158
  157.3 0.1 reduce_sum.31
  157.4 7.0 %collective-permute-start.4 = (bf16[512,128]{1,0:T(8,128)(2,1)S(1)}, bf16[512,128]{1,0:T(8,128)(2,1)S(1)}, u32[]{:S(2)}, u32[]{:S(2)}) collective-permute-start(bf16[512,128]{1,0:T(8,128)(2,1)S(1)} %bitcast.30), channel_id=1, source_target_pairs={{0,2},{2,0},{1,3},{3,1},{4,6},{6,4},{5,7},{7,5},{8,10},{10,8},{9,1... | collective-permute-start | bytes 393224 | tf_op jit(solution)/shard_map/ppermute | solution.py:163
  164.4 0.0 copy-start.1
  164.4 2.2 %copy-done.1 = bf16[8192,256]{1,0:T(8,128)(2,1)S(1)} copy-done((bf16[8192,256]{1,0:T(8,128)(2,1)S(1)}, bf16[8192,256]{1,0:T(8,128)(2,1)}, u32[]{:S(2)}) %copy-start.1) | copy-done | bytes 4194328
  166.6 1.2 shard_map.29
  167.8 0.0 copy-start.2
  167.8 10.4 %conditional.1 = (f32[512,128]{1,0:T(8,128)S(1)}) conditional(s32[]{:T(128)} %convert_element_type.29, () %tuple.12, bf16[4,2,256,128]{3,2,1,0:T(8,128)(2,1)S(1)} %shard_map.29), branch_computations={%region_1.2_spmd, %region_2.4_spmd} | conditional | flops 458752 | bytes 1835016 | solution.py:164
  167.8 10.4 %all_to_all.24 = bf16[4,2,256,128]{3,2,1,0:T(8,128)(2,1)S(1)} all-to-all(bf16[4,2,256,128]{3,2,1,0:T(8,128)(2,1)S(1)} %param.1), channel_id=1, replica_groups=mesh['x'=4,'zl'=8,'y'=4,'zh'=2,'c'=2] {'x'}, dimensions={0} | all-to-all | bytes 1048576 | tf_op jit(solution)/shard_map/cond/branch_1_fun/all_to_all | solution.py:158
  178.2 0.1 convert_reduce_fusion
  178.3 0.0 collective-permute-done.4
  178.3 0.0 copy-done.2
  178.3 0.9 maximum_add_fusion
  (6 shorter events, 0.1 us)
Async XLA Ops:
  6.5 80.8 %all-gather.3.cloned.1.call-start = ((), (), s32[]{:S(2)}) async-start(), calls=%async_computation.5 | async-start | bytes 4456448 | tf_op jit(solution)/shard_map/all_gather | solution.py:132
  9.4 17.0 %collective-permute-start = (bf16[512,128]{1,0:T(8,128)(2,1)S(1)}, bf16[512,128]{1,0:T(8,128)(2,1)S(1)}, u32[]{:S(2)}, u32[]{:S(2)}) collective-permute-start(bf16[512,128]{1,0:T(8,128)(2,1)S(1)} %get-tuple-element.19), channel_id=1, source_target_pairs={{0,0},{4,128},{8,256},{12,384},{128,4},{132,132},{136,260},{140,38... | collective-permute-start | bytes 393224 | tf_op jit(solution)/shard_map/ppermute | solution.py:141
  10.1 18.9 %collective-permute-start.1 = (bf16[512,128]{1,0:T(8,128)(2,1)S(1)}, bf16[512,128]{1,0:T(8,128)(2,1)S(1)}, u32[]{:S(2)}, u32[]{:S(2)}) collective-permute-start(bf16[512,128]{1,0:T(8,128)(2,1)S(1)} %get-tuple-element.20), channel_id=1, source_target_pairs={{0,2},{2,0},{4,130},{6,128},{8,258},{10,256},{12,386},{14,384},{12... | collective-permute-start | bytes 393224 | tf_op jit(solution)/shard_map/ppermute | solution.py:140
  65.6 6.1 %collective-permute-start.2 = (bf16[4,4,256,128]{3,2,1,0:T(8,128)(2,1)S(1)}, bf16[4,4,256,128]{3,2,1,0:T(8,128)(2,1)S(1)}, u32[]{:S(2)}, u32[]{:S(2)}) collective-permute-start(bf16[4,4,256,128]{3,2,1,0:T(8,128)(2,1)S(1)} %all_to_all.25), channel_id=1, source_target_pairs={{0,1},{1,0},{2,3},{3,2},{4,5},{5,4},{6,7},{7,6},{8,9},{9,8},{10,11... | collective-permute-start | bytes 3145736 | tf_op jit(solution)/shard_map/ppermute | solution.py:105
  113.9 30.6 %copy-start = (bf16[8192,256]{1,0:T(8,128)(2,1)S(1)}, bf16[8192,256]{1,0:T(8,128)(2,1)}, u32[]{:S(2)}) copy-start(bf16[8192,256]{1,0:T(8,128)(2,1)} %all-gather.3.cloned.1.call-done) | copy-start | bytes 12582916
  129.2 15.3 %collective-permute-start.3 = (bf16[4,4,256,128]{3,2,1,0:T(8,128)(2,1)S(1)}, bf16[4,4,256,128]{3,2,1,0:T(8,128)(2,1)S(1)}, u32[]{:S(2)}, u32[]{:S(2)}) collective-permute-start(bf16[4,4,256,128]{3,2,1,0:T(8,128)(2,1)S(1)} %bitcast.20), channel_id=1, source_target_pairs={{0,1},{1,0},{2,3},{3,2},{4,5},{5,4},{6,7},{7,6},{8,9},{9,8},{10,11... | collective-permute-start | bytes 3145736 | tf_op jit(solution)/shard_map/ppermute | solution.py:105
  157.4 20.9 %collective-permute-start.4 = (bf16[512,128]{1,0:T(8,128)(2,1)S(1)}, bf16[512,128]{1,0:T(8,128)(2,1)S(1)}, u32[]{:S(2)}, u32[]{:S(2)}) collective-permute-start(bf16[512,128]{1,0:T(8,128)(2,1)S(1)} %bitcast.30), channel_id=1, source_target_pairs={{0,2},{2,0},{1,3},{3,1},{4,6},{6,4},{5,7},{7,5},{8,10},{10,8},{9,1... | collective-permute-start | bytes 393224 | tf_op jit(solution)/shard_map/ppermute | solution.py:163
  164.4 2.2 %copy-start.1 = (bf16[8192,256]{1,0:T(8,128)(2,1)S(1)}, bf16[8192,256]{1,0:T(8,128)(2,1)}, u32[]{:S(2)}) copy-start(bf16[8192,256]{1,0:T(8,128)(2,1)} %all-gather.3.cloned.1.call-done) | copy-start | bytes 12582916
  167.8 10.5 %copy-start.2 = (f32[512,256]{1,0:T(8,128)S(1)}, f32[512,256]{1,0:T(8,128)}, u32[]{:S(2)}) copy-start(f32[512,256]{1,0:T(8,128)} %param.4) | copy-start | bytes 1572868
Sparse Core Ops, SparseCore 0:
  9.4 77.8 all-gather.2

commit v13 on v10

--- a/solution.py
+++ b/solution.py
@@ -147,24 +147,29 @@
     y_other, ident = lax.optimization_barrier((y_other, make_ident((4, 256, 128), first_col)))
     part = dot_right_all(z_rows, y_own, y_other)
 
-    part = lax.all_to_all(part.reshape(16, 256, 128), PLANE, 0, 0, tiled=True)
+    def branch(step, block):
+        shape = jax.eval_shape(step, block)
+        return lax.cond(at("c") < 2, step, lambda b: jnp.zeros(shape.shape, shape.dtype), block)
+
+    def exchange(block):
+        return lax.all_to_all(block, PLANE, 0, 0, tiled=True)
+
+    part = branch(exchange, part.reshape(16, 256, 128))
     product = part.reshape(4, 4, 256, 128).astype(jnp.float32).sum(0)
     shift = make_shift(product, order, ident)
 
     spread = jnp.broadcast_to(shift[:, None], (4, 4, 256, 128)).reshape(16, 256, 128)
-    own = lax.all_to_all(spread, PLANE, 0, 0, tiled=True).reshape(4, 4, 256, 128)
+    own = branch(exchange, spread).reshape(4, 4, 256, 128)
     other = other_core(own)
 
     def sum_x(part):
         part = lax.all_to_all(part, "x", 0, 0, tiled=True)
         return part.astype(jnp.float32).sum(0).reshape(512, 128)
 
-    yours = sum_x(dot_right(1, z_rows, own, other)).astype(jnp.bfloat16)
+    yours = branch(sum_x, dot_right(1, z_rows, own, other)).astype(jnp.bfloat16)
     mine = dot_right(0, z_rows, own, other)
     yours = lax.ppermute(yours, "zh", SWAP).astype(jnp.float32)
-    mine = lax.cond(
-        at("c") < 2, sum_x, lambda part: jnp.zeros((512, 128), jnp.float32), mine
-    )
+    mine = branch(sum_x, mine)
     part = jnp.concatenate([jnp.where(low, mine, yours), jnp.where(low, yours, mine)], axis=1)
     return 1.5 * lax.reduce_precision(z_iter, 8, 7) + part
 

time: 184 us -> 187 us (1.016)
  local copies, waits for them, and re-layouts: 6.96 us -> 9.15 us
    unnamed x6, local copies, waits for them, and re-layouts: 2.19 us -> 4.37 us
where the time goes in v13:
time: 187 us; the launch traced here: 186 us
  blocking collectives  91 us (49%)
  starting transfers between devices  41.6 us (22%)
  waiting for transfers between devices  15.2 us (8%)
  between operations  13.6 us (7%)
  local copies, waits for them, and re-layouts  9.15 us (5%)
  Pallas kernels  7.72 us (4%)
  other arithmetic  7.32 us (4%)
    all_to_all x1, blocking collectives, shards(): y_own = lax.all_to_all(jnp.stack([turned] * 4), 'y', 0, 0, tiled=True)  35.7 us
    all_to_all x2, blocking collectives, exchange(): return lax.all_to_all(block, PLANE, 0, 0, tiled=True)  33.1 us
    all_to_all x2, blocking collectives, sum_x(): part = lax.all_to_all(part, 'x', 0, 0, tiled=True)  22.2 us
    ppermute x2, starting transfers between devices, other_core(): return lax.ppermute(block, 'c', SWAP)  17.6 us
    ppermute x1, starting transfers between devices, shards(): yours = lax.ppermute(jnp.where(low, right, left), 'zh', SWAP)  16.3 us
    all_gather x1, waiting for transfers between devices, shards(): z_rows = lax.all_gather(z_half, AXES, axis_index_groups=Z_RINGS)  8.19 us
    ppermute x1, starting transfers between devices, shards(): yours = lax.ppermute(yours, 'zh', SWAP).astype(jnp.float32)  7 us
    pallas_call x1, Pallas kernels, dot_right_all(): pl.pallas_call(dot_all_kernel, in_specs=[pl.BlockSpec(memory_space=pl.ANY...  5.23 us
  transfers between devices with their start and end apart: 6, of which 4 were waited for; matrix products, arithmetic and copies ran while one was open for 5% of the time, Pallas kernels for 1%

profile of v13, /device:TPU:1, one launch (start us, length us, event | category | flops | bytes accessed | tf_op | source)
XLA Modules:
  0.0 185.6 jit_solution(10208116363868204314)
XLA Ops:
  6.5 0.0 all-gather.3.cloned.1.call-start
  6.5 1.8 convert_element_type.38
  8.3 0.0 all-gather.3.cloned.1.call-update
  8.3 1.1 convert_element_type.39
  9.4 16.3 %collective-permute-start = (bf16[512,128]{1,0:T(8,128)(2,1)S(1)}, bf16[512,128]{1,0:T(8,128)(2,1)S(1)}, u32[]{:S(2)}, u32[]{:S(2)}) collective-permute-start(bf16[512,128]{1,0:T(8,128)(2,1)S(1)} %broadcast_select_fusion.2), channel_id=1, source_target_pairs={{0,2},{2,0},{1,3},{3,1},{4,6},{6,4},{5,7},{7,5},{8,10},{10,8},{9,1... | collective-permute-start | bytes 393224 | tf_op jit(solution)/shard_map/ppermute | solution.py:139
  25.7 2.6 %collective-permute-done = bf16[512,128]{1,0:T(8,128)(2,1)S(1)} collective-permute-done((bf16[512,128]{1,0:T(8,128)(2,1)S(1)}, bf16[512,128]{1,0:T(8,128)(2,1)S(1)}, u32[]{:S(2)}, u32[]{:S(2)}) %collective-permute-start) | collective-permute-done | bytes 131104 | tf_op jit(solution)/shard_map/ppermute | solution.py:139
  28.4 0.7 collective-permute-start.1
  29.1 0.0 collective-permute-done.1
  29.1 0.2 stack.28
  29.3 35.7 %all_to_all.25 = bf16[4,4,256,128]{3,2,1,0:T(8,128)(2,1)S(1)} all-to-all(bf16[4,4,256,128]{3,2,1,0:T(8,128)(2,1)S(1)} %stack.28), channel_id=1, replica_groups=mesh['x'=4,'zl'=8,'y'=4,'zh'=2,'c'=2] {'y'}, dimensions={0} | all-to-all | bytes 2097152 | tf_op jit(solution)/shard_map/all_to_all | solution.py:145
  65.0 4.4 %collective-permute-start.2 = (bf16[4,4,256,128]{3,2,1,0:T(8,128)(2,1)S(1)}, bf16[4,4,256,128]{3,2,1,0:T(8,128)(2,1)S(1)}, u32[]{:S(2)}, u32[]{:S(2)}) collective-permute-start(bf16[4,4,256,128]{3,2,1,0:T(8,128)(2,1)S(1)} %all_to_all.25), channel_id=1, source_target_pairs={{0,1},{1,0},{2,3},{3,2},{4,5},{5,4},{6,7},{7,6},{8,9},{9,8},{10,11... | collective-permute-start | bytes 3145736 | tf_op jit(solution)/shard_map/ppermute | solution.py:105
  69.5 0.1 fusion
  69.7 2.1 %collective-permute-done.2 = bf16[4,4,256,128]{3,2,1,0:T(8,128)(2,1)S(1)} collective-permute-done((bf16[4,4,256,128]{3,2,1,0:T(8,128)(2,1)S(1)}, bf16[4,4,256,128]{3,2,1,0:T(8,128)(2,1)S(1)}, u32[]{:S(2)}, u32[]{:S(2)}) %collective-permute-start.2) | collective-permute-done | bytes 1048608 | tf_op jit(solution)/shard_map/ppermute | solution.py:105
  71.7 0.1 broadcast_select_fusion.1
  71.9 0.8 copy.3
  72.7 0.8 copy.4
  73.5 2.8 %maximum_bitcast_fusion = bf16[2,2,2,256,4,128]{5,4,3,2,1,0:T(4,128)(2,1)} fusion(bf16[1,4,2,2,256,128]{5,1,4,3,0,2:T(4,128)(2,1)S(1)} %copy.4, bf16[1,4,2,2,256,128]{5,1,4,3,0,2:T(4,128)(2,1)S(1)} %copy.3), kind=kLoop, calls=%fused_computation.3 | loop fusion | flops 1048576 | bytes 4194304 | tf_op jit(solution)/shard_map/transpose | solution.py:68
  76.4 2.8 %reshape.43.right_ref = bf16[8,256,512]{2,1,0:T(8,128)(2,1)S(1)} reshape(bf16[2,2,2,256,4,128]{5,4,3,2,1,0:T(4,128)(2,1)} %maximum_bitcast_fusion) | data formatting | bytes 4194304 | tf_op jit(solution)/shard_map/reshape | solution.py:69
  79.1 8.2 %all-gather.3.cloned.1.call-done = bf16[8192,256]{1,0:T(8,128)(2,1)} async-done(((bf16[512,256]{1,0:T(8,128)(2,1)}), bf16[8192,256]{1,0:T(8,128)(2,1)}) %all-gather.3.cloned.1.call-update) | async-done | bytes 4194320 | tf_op jit(solution)/shard_map/all_gather | solution.py:132
  87.3 5.2 %shard_map.28 = bf16[4,4,256,128]{3,2,1,0:T(8,128)(2,1)} custom-call(bf16[16,512,256]{2,1,0:T(8,128)(2,1)} %bitcast.17, bf16[8,256,512]{2,1,0:T(8,128)(2,1)S(1)} %reshape.43.right_ref), custom_call_target="tpu_custom_call" | custom-call | flops 2147483648 | bytes 7340032 | tf_op jit(solution)/shard_map/pallas_call | solution.py:70
  92.5 18.5 %conditional.4 = (f32[4,256,128]{2,1,0:T(8,128)S(1)}) conditional(s32[]{:T(128)} %convert_element_type.37, () %tuple.37, bf16[4,4,256,128]{3,2,1,0:T(8,128)(2,1)} %shard_map.28), branch_computations={%region_0.1_spmd, %region_1.3_spmd} | conditional | flops 917504 | bytes 3670024 | solution.py:152
  92.6 18.4 %all_to_all.21 = bf16[16,256,128]{2,1,0:T(8,128)(2,1)S(1)} all-to-all(bf16[16,256,128]{2,1,0:T(8,128)(2,1)} %bitcast.26), channel_id=1, replica_groups=mesh['x'=4,'zl'=8,'y'=4,'zh'=2,'c'=2] {'x','y'}, dimensions={0} | all-to-all | bytes 2097152 | tf_op jit(solution)/shard_map/cond/branch_1_fun/all_to_all | solution.py:155
  110.9 0.2 convert_reduce_fusion
  111.1 0.1 subtract_convert_fusion
  111.2 14.9 %conditional.5 = (bf16[4,4,256,128]{3,2,1,0:T(8,128)(2,1)S(1)}) conditional(s32[]{:T(128)} %convert_element_type.37, () %tuple.35, bf16[4,256,128]{2,1,0:T(8,128)(2,1)S(1)} %subtract_convert_fusion), branch_computations={%region_3.4_spmd, %region_4.5_spmd} | conditional | bytes 3407880 | solution.py:152
  111.2 0.2 broadcast_in_dim.12
  111.4 14.7 %all_to_all.22 = bf16[16,256,128]{2,1,0:T(8,128)(2,1)S(1)} all-to-all(bf16[16,256,128]{2,1,0:T(8,128)(2,1)S(1)} %bitcast.23), channel_id=1, replica_groups=mesh['x'=4,'zl'=8,'y'=4,'zh'=2,'c'=2] {'x','y'}, dimensions={0} | all-to-all | bytes 2097152 | tf_op jit(solution)/shard_map/cond/branch_1_fun/all_to_all | solution.py:155
  126.1 13.2 %collective-permute-start.3 = (bf16[4,4,256,128]{3,2,1,0:T(8,128)(2,1)S(1)}, bf16[4,4,256,128]{3,2,1,0:T(8,128)(2,1)S(1)}, u32[]{:S(2)}, u32[]{:S(2)}) collective-permute-start(bf16[4,4,256,128]{3,2,1,0:T(8,128)(2,1)S(1)} %get-tuple-element.37.own_ref), channel_id=1, source_target_pairs={{0,1},{1,0},{2,3},{3,2},{4,5},{5,4},{6,7},{7,6},{8,9},{9,8},{10,11... | collective-permute-start | bytes 3145736 | tf_op jit(solution)/shard_map/ppermute | solution.py:105
  139.3 2.3 %collective-permute-done.3.other_ref = bf16[4,4,256,128]{3,2,1,0:T(8,128)(2,1)S(1)} collective-permute-done((bf16[4,4,256,128]{3,2,1,0:T(8,128)(2,1)S(1)}, bf16[4,4,256,128]{3,2,1,0:T(8,128)(2,1)S(1)}, u32[]{:S(2)}, u32[]{:S(2)}) %collective-permute-start.3) | collective-permute-done | bytes 1048608 | tf_op jit(solution)/shard_map/ppermute | solution.py:105
  141.6 0.0 copy-start
  141.6 2.2 %copy-done = bf16[8192,256]{1,0:T(8,128)(2,1)S(1)} copy-done((bf16[8192,256]{1,0:T(8,128)(2,1)S(1)}, bf16[8192,256]{1,0:T(8,128)(2,1)}, u32[]{:S(2)}) %copy-start) | copy-done | bytes 4194328
  143.8 1.2 shard_map.30
  145.0 11.7 %conditional.7 = (bf16[512,128]{1,0:T(8,128)(2,1)S(1)}) conditional(s32[]{:T(128)} %convert_element_type.37, () %tuple.38, bf16[4,2,256,128]{3,2,1,0:T(8,128)(2,1)S(1)} %shard_map.30), branch_computations={%region_8.9_spmd, %region_9.11_spmd} | conditional | flops 458752 | bytes 1703944 | solution.py:152
  145.0 11.6 %all_to_all.24 = bf16[4,2,256,128]{3,2,1,0:T(8,128)(2,1)S(1)} all-to-all(bf16[4,2,256,128]{3,2,1,0:T(8,128)(2,1)S(1)} %param.7), channel_id=1, replica_groups=mesh['x'=4,'zl'=8,'y'=4,'zh'=2,'c'=2] {'x'}, dimensions={0} | all-to-all | bytes 1048576 | tf_op jit(solution)/shard_map/cond/branch_1_fun/all_to_all | solution.py:166
  156.7 0.1 convert_reduce_fusion.2
  156.7 7.0 %collective-permute-start.4 = (bf16[512,128]{1,0:T(8,128)(2,1)S(1)}, bf16[512,128]{1,0:T(8,128)(2,1)S(1)}, u32[]{:S(2)}, u32[]{:S(2)}) collective-permute-start(bf16[512,128]{1,0:T(8,128)(2,1)S(1)} %get-tuple-element.39), channel_id=1, source_target_pairs={{0,2},{2,0},{1,3},{3,1},{4,6},{6,4},{5,7},{7,5},{8,10},{10,8},{9,1... | collective-permute-start | bytes 393224 | tf_op jit(solution)/shard_map/ppermute | solution.py:171
  163.8 0.0 copy-start.1
  163.8 2.2 %copy-done.1 = bf16[8192,256]{1,0:T(8,128)(2,1)S(1)} copy-done((bf16[8192,256]{1,0:T(8,128)(2,1)S(1)}, bf16[8192,256]{1,0:T(8,128)(2,1)}, u32[]{:S(2)}) %copy-start.1) | copy-done | bytes 4194328
  165.9 1.2 shard_map.29
  167.2 0.0 copy-start.2
  167.2 10.6 %conditional.6 = (f32[512,128]{1,0:T(8,128)S(1)}) conditional(s32[]{:T(128)} %convert_element_type.37, () %tuple.34, bf16[4,2,256,128]{3,2,1,0:T(8,128)(2,1)S(1)} %shard_map.29), branch_computations={%region_5.6_spmd, %region_6.8_spmd} | conditional | flops 458752 | bytes 1835016 | solution.py:152
  167.2 10.6 %all_to_all.23 = bf16[4,2,256,128]{3,2,1,0:T(8,128)(2,1)S(1)} all-to-all(bf16[4,2,256,128]{3,2,1,0:T(8,128)(2,1)S(1)} %param.5), channel_id=1, replica_groups=mesh['x'=4,'zl'=8,'y'=4,'zh'=2,'c'=2] {'x'}, dimensions={0} | all-to-all | bytes 1048576 | tf_op jit(solution)/shard_map/cond/branch_1_fun/all_to_all | solution.py:166
  177.8 0.1 convert_reduce_fusion.1
  177.8 0.0 collective-permute-done.4
  177.9 0.0 copy-done.2
  177.9 0.9 maximum_add_fusion
  (6 shorter events, 0.1 us)
Async XLA Ops:
  6.5 80.8 %all-gather.3.cloned.1.call-start = ((), (), s32[]{:S(2)}) async-start(), calls=%async_computation.5 | async-start | bytes 4456448 | tf_op jit(solution)/shard_map/all_gather | solution.py:132
  9.4 18.9 %collective-permute-start = (bf16[512,128]{1,0:T(8,128)(2,1)S(1)}, bf16[512,128]{1,0:T(8,128)(2,1)S(1)}, u32[]{:S(2)}, u32[]{:S(2)}) collective-permute-start(bf16[512,128]{1,0:T(8,128)(2,1)S(1)} %broadcast_select_fusion.2), channel_id=1, source_target_pairs={{0,2},{2,0},{1,3},{3,1},{4,6},{6,4},{5,7},{7,5},{8,10},{10,8},{9,1... | collective-permute-start | bytes 393224 | tf_op jit(solution)/shard_map/ppermute | solution.py:139
  28.4 0.7 collective-permute-start.1
  65.0 6.7 %collective-permute-start.2 = (bf16[4,4,256,128]{3,2,1,0:T(8,128)(2,1)S(1)}, bf16[4,4,256,128]{3,2,1,0:T(8,128)(2,1)S(1)}, u32[]{:S(2)}, u32[]{:S(2)}) collective-permute-start(bf16[4,4,256,128]{3,2,1,0:T(8,128)(2,1)S(1)} %all_to_all.25), channel_id=1, source_target_pairs={{0,1},{1,0},{2,3},{3,2},{4,5},{5,4},{6,7},{7,6},{8,9},{9,8},{10,11... | collective-permute-start | bytes 3145736 | tf_op jit(solution)/shard_map/ppermute | solution.py:105
  126.1 15.5 %collective-permute-start.3 = (bf16[4,4,256,128]{3,2,1,0:T(8,128)(2,1)S(1)}, bf16[4,4,256,128]{3,2,1,0:T(8,128)(2,1)S(1)}, u32[]{:S(2)}, u32[]{:S(2)}) collective-permute-start(bf16[4,4,256,128]{3,2,1,0:T(8,128)(2,1)S(1)} %get-tuple-element.37.own_ref), channel_id=1, source_target_pairs={{0,1},{1,0},{2,3},{3,2},{4,5},{5,4},{6,7},{7,6},{8,9},{9,8},{10,11... | collective-permute-start | bytes 3145736 | tf_op jit(solution)/shard_map/ppermute | solution.py:105
  141.6 2.2 %copy-start = (bf16[8192,256]{1,0:T(8,128)(2,1)S(1)}, bf16[8192,256]{1,0:T(8,128)(2,1)}, u32[]{:S(2)}) copy-start(bf16[8192,256]{1,0:T(8,128)(2,1)} %all-gather.3.cloned.1.call-done) | copy-start | bytes 12582916
  156.7 21.1 %collective-permute-start.4 = (bf16[512,128]{1,0:T(8,128)(2,1)S(1)}, bf16[512,128]{1,0:T(8,128)(2,1)S(1)}, u32[]{:S(2)}, u32[]{:S(2)}) collective-permute-start(bf16[512,128]{1,0:T(8,128)(2,1)S(1)} %get-tuple-element.39), channel_id=1, source_target_pairs={{0,2},{2,0},{1,3},{3,1},{4,6},{6,4},{5,7},{7,5},{8,10},{10,8},{9,1... | collective-permute-start | bytes 393224 | tf_op jit(solution)/shard_map/ppermute | solution.py:171
  163.8 2.2 %copy-start.1 = (bf16[8192,256]{1,0:T(8,128)(2,1)S(1)}, bf16[8192,256]{1,0:T(8,128)(2,1)}, u32[]{:S(2)}) copy-start(bf16[8192,256]{1,0:T(8,128)(2,1)} %all-gather.3.cloned.1.call-done) | copy-start | bytes 12582916
  167.2 10.7 %copy-start.2 = (f32[512,256]{1,0:T(8,128)S(1)}, f32[512,256]{1,0:T(8,128)}, u32[]{:S(2)}) copy-start(f32[512,256]{1,0:T(8,128)} %param.10) | copy-start | bytes 1572868
Sparse Core Ops, SparseCore 0:
  9.4 77.8 all-gather.2

commit v14 on v10

--- a/solution.py
+++ b/solution.py
@@ -101,6 +101,44 @@
     )(z_rows, own, other)
 
 
+def dot_part_kernel(core, z_ref, part_ref, *refs):
+    out_ref = refs[-1]
+    groups, _, depth, width = part_ref.shape
+    first = (1 - lax.axis_index("zh")) * 8 + (lax.axis_index("c") ^ core) * 2
+    for s in range(2):
+        total = None if core == 0 else refs[0][s]
+        for n in range(4):
+            right = jnp.concatenate([part_ref[j, n] for j in range(groups)], axis=1)
+            rows = z_ref[first + n // 2 * 4 + n % 2, s * depth : (s + 1) * depth, :]
+            term = jnp.dot(rows, right, preferred_element_type=jnp.float32)
+            total = term if total is None else total + term
+        if core == 0:
+            out_ref[s] = total
+        else:
+            for j in range(groups):
+                out_ref[j, s] = total[:, j * width : (j + 1) * width].astype(out_ref.dtype)
+
+
+def dot_part(core, z_rows, part, *sums):
+    groups, _, depth, width = part.shape
+    if core == 0:
+        out = jax.ShapeDtypeStruct((2, depth, groups * width), jnp.float32)
+    else:
+        out = jax.ShapeDtypeStruct((groups, 2, depth, width), jnp.bfloat16)
+    return pl.pallas_call(
+        functools.partial(dot_part_kernel, core),
+        in_specs=[pl.BlockSpec(memory_space=pltpu.VMEM)] * (2 + len(sums)),
+        out_specs=pl.BlockSpec(memory_space=pltpu.VMEM),
+        out_shape=out,
+        compiler_params=pltpu.CompilerParams(vmem_limit_bytes=32 * 2**20),
+        cost_estimate=pl.CostEstimate(
+            flops=z_rows.size * groups * width // 2,
+            bytes_accessed=z_rows.size // 2 + 5 * part.size,
+            transcendentals=0,
+        ),
+    )(z_rows, part, *sums)
+
+
 def other_core(block):
     return lax.ppermute(block, "c", SWAP)
 
@@ -159,7 +197,8 @@
         part = lax.all_to_all(part, "x", 0, 0, tiled=True)
         return part.astype(jnp.float32).sum(0).reshape(512, 128)
 
-    yours = sum_x(dot_right(1, z_rows, own, other)).astype(jnp.bfloat16)
+    yours = dot_part(1, z_rows, other, dot_part(0, z_rows, own))
+    yours = sum_x(yours).astype(jnp.bfloat16)
     mine = dot_right(0, z_rows, own, other)
     yours = lax.ppermute(yours, "zh", SWAP).astype(jnp.float32)
     mine = lax.cond(

time: 184 us -> 183 us (level)
  no operation moved by 1% of the time
where the time goes in v14:
time: 183 us; the launch traced here: 182 us
  blocking collectives  91 us (50%)
  starting transfers between devices  41.6 us (23%)
  waiting for transfers between devices  14.5 us (8%)
  between operations  13.7 us (7%)
  other arithmetic  7.33 us (4%)
  local copies, waits for them, and re-layouts  6.96 us (4%)
  Pallas kernels  6.94 us (4%)
    all_to_all x1, blocking collectives, shards(): y_own = lax.all_to_all(jnp.stack([turned] * 4), 'y', 0, 0, tiled=True)  35.7 us
    all_to_all x2, blocking collectives, sum_x(): part = lax.all_to_all(part, 'x', 0, 0, tiled=True)  22.2 us
    all_to_all x1, blocking collectives, shards(): part = lax.all_to_all(part.reshape(16, 256, 128), PLANE, 0, 0, tiled=True)  18.1 us
    ppermute x2, starting transfers between devices, other_core(): return lax.ppermute(block, 'c', SWAP)  17.7 us
    ppermute x1, starting transfers between devices, shards(): yours = lax.ppermute(jnp.where(low, right, left), 'zh', SWAP)  16.3 us
    all_to_all x1, blocking collectives, shards(): lax.all_to_all(spread, PLANE, 0, 0, tiled=True).reshape(4, 4, 256, 128)  15 us
    all_gather x1, waiting for transfers between devices, shards(): z_rows = lax.all_gather(z_half, AXES, axis_index_groups=Z_RINGS)  8.19 us
    ppermute x1, starting transfers between devices, shards(): yours = lax.ppermute(yours, 'zh', SWAP).astype(jnp.float32)  6.97 us
  transfers between devices with their start and end apart: 6, of which 4 were waited for; matrix products, arithmetic and copies ran while one was open for 5% of the time, Pallas kernels for 1%

profile of v14, /device:TPU:1, one launch (start us, length us, event | category | flops | bytes accessed | tf_op | source)
XLA Modules:
  0.0 182.0 jit_solution(14447416273815444380)
XLA Ops:
  6.5 0.0 all-gather.3.cloned.1.call-start
  6.5 1.8 convert_element_type.30
  8.3 0.0 all-gather.3.cloned.1.call-update
  8.3 1.1 convert_element_type.31
  9.4 16.3 %collective-permute-start = (bf16[512,128]{1,0:T(8,128)(2,1)S(1)}, bf16[512,128]{1,0:T(8,128)(2,1)S(1)}, u32[]{:S(2)}, u32[]{:S(2)}) collective-permute-start(bf16[512,128]{1,0:T(8,128)(2,1)S(1)} %broadcast_select_fusion.2), channel_id=1, source_target_pairs={{0,2},{2,0},{1,3},{3,1},{4,6},{6,4},{5,7},{7,5},{8,10},{10,8},{9,1... | collective-permute-start | bytes 393224 | tf_op jit(solution)/shard_map/ppermute | solution.py:177
  25.7 2.6 %collective-permute-done = bf16[512,128]{1,0:T(8,128)(2,1)S(1)} collective-permute-done((bf16[512,128]{1,0:T(8,128)(2,1)S(1)}, bf16[512,128]{1,0:T(8,128)(2,1)S(1)}, u32[]{:S(2)}, u32[]{:S(2)}) %collective-permute-start) | collective-permute-done | bytes 131104 | tf_op jit(solution)/shard_map/ppermute | solution.py:177
  28.4 0.7 collective-permute-start.1
  29.1 0.0 collective-permute-done.1
  29.1 0.2 stack.28
  29.3 35.7 %all_to_all.25 = bf16[4,4,256,128]{3,2,1,0:T(8,128)(2,1)S(1)} all-to-all(bf16[4,4,256,128]{3,2,1,0:T(8,128)(2,1)S(1)} %stack.28), channel_id=1, replica_groups=mesh['x'=4,'zl'=8,'y'=4,'zh'=2,'c'=2] {'y'}, dimensions={0} | all-to-all | bytes 2097152 | tf_op jit(solution)/shard_map/all_to_all | solution.py:183
  65.0 4.4 %collective-permute-start.2 = (bf16[4,4,256,128]{3,2,1,0:T(8,128)(2,1)S(1)}, bf16[4,4,256,128]{3,2,1,0:T(8,128)(2,1)S(1)}, u32[]{:S(2)}, u32[]{:S(2)}) collective-permute-start(bf16[4,4,256,128]{3,2,1,0:T(8,128)(2,1)S(1)} %all_to_all.25), channel_id=1, source_target_pairs={{0,1},{1,0},{2,3},{3,2},{4,5},{5,4},{6,7},{7,6},{8,9},{9,8},{10,11... | collective-permute-start | bytes 3145736 | tf_op jit(solution)/shard_map/ppermute | solution.py:143
  69.5 0.1 fusion
  69.7 2.1 %collective-permute-done.2 = bf16[4,4,256,128]{3,2,1,0:T(8,128)(2,1)S(1)} collective-permute-done((bf16[4,4,256,128]{3,2,1,0:T(8,128)(2,1)S(1)}, bf16[4,4,256,128]{3,2,1,0:T(8,128)(2,1)S(1)}, u32[]{:S(2)}, u32[]{:S(2)}) %collective-permute-start.2) | collective-permute-done | bytes 1048608 | tf_op jit(solution)/shard_map/ppermute | solution.py:143
  71.7 0.1 broadcast_select_fusion.1
  71.9 0.8 copy.3
  72.7 0.8 copy.4
  73.5 2.8 %maximum_bitcast_fusion = bf16[2,2,2,256,4,128]{5,4,3,2,1,0:T(4,128)(2,1)} fusion(bf16[1,4,2,2,256,128]{5,1,4,3,0,2:T(4,128)(2,1)S(1)} %copy.4, bf16[1,4,2,2,256,128]{5,1,4,3,0,2:T(4,128)(2,1)S(1)} %copy.3), kind=kLoop, calls=%fused_computation.1 | loop fusion | flops 1048576 | bytes 4194304 | tf_op jit(solution)/shard_map/transpose | solution.py:68
  76.4 2.7 %reshape.32.right_ref = bf16[8,256,512]{2,1,0:T(8,128)(2,1)S(1)} reshape(bf16[2,2,2,256,4,128]{5,4,3,2,1,0:T(4,128)(2,1)} %maximum_bitcast_fusion) | data formatting | bytes 4194304 | tf_op jit(solution)/shard_map/reshape | solution.py:69
  79.1 8.2 %all-gather.3.cloned.1.call-done = bf16[8192,256]{1,0:T(8,128)(2,1)} async-done(((bf16[512,256]{1,0:T(8,128)(2,1)}), bf16[8192,256]{1,0:T(8,128)(2,1)}) %all-gather.3.cloned.1.call-update) | async-done | bytes 4194320 | tf_op jit(solution)/shard_map/all_gather | solution.py:170
  87.3 4.3 %shard_map.28 = bf16[4,4,256,128]{3,2,1,0:T(8,128)(2,1)S(1)} custom-call(bf16[16,512,256]{2,1,0:T(8,128)(2,1)} %bitcast.17, bf16[8,256,512]{2,1,0:T(8,128)(2,1)S(1)} %reshape.32.right_ref), custom_call_target="tpu_custom_call" | custom-call | flops 2147483648 | bytes 7340032 | tf_op jit(solution)/shard_map/pallas_call | solution.py:70
  91.6 18.1 %all_to_all.26 = bf16[16,256,128]{2,1,0:T(8,128)(2,1)S(1)} all-to-all(bf16[16,256,128]{2,1,0:T(8,128)(2,1)S(1)} %bitcast.24), channel_id=1, replica_groups=mesh['x'=4,'zl'=8,'y'=4,'zh'=2,'c'=2] {'x','y'}, dimensions={0} | all-to-all | bytes 2097152 | tf_op jit(solution)/shard_map/all_to_all | solution.py:188
  109.7 0.2 convert_reduce_fusion.1
  109.9 0.0 copy-start
  109.9 0.1 subtract_convert_fusion
  110.0 0.2 broadcast_in_dim.16
  110.2 15.0 %all_to_all.27 = bf16[16,256,128]{2,1,0:T(8,128)(2,1)S(1)} all-to-all(bf16[16,256,128]{2,1,0:T(8,128)(2,1)S(1)} %bitcast.27), channel_id=1, replica_groups=mesh['x'=4,'zl'=8,'y'=4,'zh'=2,'c'=2] {'x','y'}, dimensions={0} | all-to-all | bytes 2097152 | tf_op jit(solution)/shard_map/all_to_all | solution.py:193
  125.2 13.3 %collective-permute-start.3 = (bf16[4,4,256,128]{3,2,1,0:T(8,128)(2,1)S(1)}, bf16[4,4,256,128]{3,2,1,0:T(8,128)(2,1)S(1)}, u32[]{:S(2)}, u32[]{:S(2)}) collective-permute-start(bf16[4,4,256,128]{3,2,1,0:T(8,128)(2,1)S(1)} %bitcast.21), channel_id=1, source_target_pairs={{0,1},{1,0},{2,3},{3,2},{4,5},{5,4},{6,7},{7,6},{8,9},{9,8},{10,11... | collective-permute-start | bytes 3145736 | tf_op jit(solution)/shard_map/ppermute | solution.py:143
  138.4 0.0 copy-done
  138.5 0.7 shard_map.30.refs_0_
  139.2 1.5 collective-permute-done.3.other_ref.part_ref
  140.7 0.7 shard_map.31
  141.4 11.6 %all_to_all.28 = bf16[4,2,256,128]{3,2,1,0:T(8,128)(2,1)S(1)} all-to-all(bf16[4,2,256,128]{3,2,1,0:T(8,128)(2,1)S(1)} %shard_map.31), channel_id=1, replica_groups=mesh['x'=4,'zl'=8,'y'=4,'zh'=2,'c'=2] {'x'}, dimensions={0} | all-to-all | bytes 1048576 | tf_op jit(solution)/shard_map/all_to_all | solution.py:197
  153.1 0.1 reduce_sum.31
  153.1 7.0 %collective-permute-start.4 = (bf16[512,128]{1,0:T(8,128)(2,1)S(1)}, bf16[512,128]{1,0:T(8,128)(2,1)S(1)}, u32[]{:S(2)}, u32[]{:S(2)}) collective-permute-start(bf16[512,128]{1,0:T(8,128)(2,1)S(1)} %bitcast.31), channel_id=1, source_target_pairs={{0,2},{2,0},{1,3},{3,1},{4,6},{6,4},{5,7},{7,5},{8,10},{10,8},{9,1... | collective-permute-start | bytes 393224 | tf_op jit(solution)/shard_map/ppermute | solution.py:203
  160.1 0.0 copy-start.1
  160.1 2.2 %copy-done.1 = bf16[8192,256]{1,0:T(8,128)(2,1)S(1)} copy-done((bf16[8192,256]{1,0:T(8,128)(2,1)S(1)}, bf16[8192,256]{1,0:T(8,128)(2,1)}, u32[]{:S(2)}) %copy-start.1) | copy-done | bytes 4194328
  162.3 1.2 shard_map.29
  163.6 0.0 copy-start.2
  163.6 10.6 %conditional.1 = (f32[512,128]{1,0:T(8,128)S(1)}) conditional(s32[]{:T(128)} %convert_element_type.29, () %tuple.12, bf16[4,2,256,128]{3,2,1,0:T(8,128)(2,1)S(1)} %shard_map.29), branch_computations={%region_1.2_spmd, %region_2.4_spmd} | conditional | flops 458752 | bytes 1835016 | solution.py:204
  163.6 10.6 %all_to_all.24 = bf16[4,2,256,128]{3,2,1,0:T(8,128)(2,1)S(1)} all-to-all(bf16[4,2,256,128]{3,2,1,0:T(8,128)(2,1)S(1)} %param.1), channel_id=1, replica_groups=mesh['x'=4,'zl'=8,'y'=4,'zh'=2,'c'=2] {'x'}, dimensions={0} | all-to-all | bytes 1048576 | tf_op jit(solution)/shard_map/cond/branch_1_fun/all_to_all | solution.py:197
  174.1 0.1 convert_reduce_fusion
  174.2 0.0 collective-permute-done.4
  174.3 0.0 copy-done.2
  174.3 0.9 maximum_add_fusion
  (6 shorter events, 0.1 us)
Async XLA Ops:
  6.5 80.8 %all-gather.3.cloned.1.call-start = ((), (), s32[]{:S(2)}) async-start(), calls=%async_computation.5 | async-start | bytes 4456448 | tf_op jit(solution)/shard_map/all_gather | solution.py:170
  9.4 18.9 %collective-permute-start = (bf16[512,128]{1,0:T(8,128)(2,1)S(1)}, bf16[512,128]{1,0:T(8,128)(2,1)S(1)}, u32[]{:S(2)}, u32[]{:S(2)}) collective-permute-start(bf16[512,128]{1,0:T(8,128)(2,1)S(1)} %broadcast_select_fusion.2), channel_id=1, source_target_pairs={{0,2},{2,0},{1,3},{3,1},{4,6},{6,4},{5,7},{7,5},{8,10},{10,8},{9,1... | collective-permute-start | bytes 393224 | tf_op jit(solution)/shard_map/ppermute | solution.py:177
  28.4 0.7 collective-permute-start.1
  65.0 6.7 %collective-permute-start.2 = (bf16[4,4,256,128]{3,2,1,0:T(8,128)(2,1)S(1)}, bf16[4,4,256,128]{3,2,1,0:T(8,128)(2,1)S(1)}, u32[]{:S(2)}, u32[]{:S(2)}) collective-permute-start(bf16[4,4,256,128]{3,2,1,0:T(8,128)(2,1)S(1)} %all_to_all.25), channel_id=1, source_target_pairs={{0,1},{1,0},{2,3},{3,2},{4,5},{5,4},{6,7},{7,6},{8,9},{9,8},{10,11... | collective-permute-start | bytes 3145736 | tf_op jit(solution)/shard_map/ppermute | solution.py:143
  109.9 28.6 %copy-start = (bf16[8192,256]{1,0:T(8,128)(2,1)S(1)}, bf16[8192,256]{1,0:T(8,128)(2,1)}, u32[]{:S(2)}) copy-start(bf16[8192,256]{1,0:T(8,128)(2,1)} %all-gather.3.cloned.1.call-done) | copy-start | bytes 12582916
  125.2 15.5 %collective-permute-start.3 = (bf16[4,4,256,128]{3,2,1,0:T(8,128)(2,1)S(1)}, bf16[4,4,256,128]{3,2,1,0:T(8,128)(2,1)S(1)}, u32[]{:S(2)}, u32[]{:S(2)}) collective-permute-start(bf16[4,4,256,128]{3,2,1,0:T(8,128)(2,1)S(1)} %bitcast.21), channel_id=1, source_target_pairs={{0,1},{1,0},{2,3},{3,2},{4,5},{5,4},{6,7},{7,6},{8,9},{9,8},{10,11... | collective-permute-start | bytes 3145736 | tf_op jit(solution)/shard_map/ppermute | solution.py:143
  153.1 21.1 %collective-permute-start.4 = (bf16[512,128]{1,0:T(8,128)(2,1)S(1)}, bf16[512,128]{1,0:T(8,128)(2,1)S(1)}, u32[]{:S(2)}, u32[]{:S(2)}) collective-permute-start(bf16[512,128]{1,0:T(8,128)(2,1)S(1)} %bitcast.31), channel_id=1, source_target_pairs={{0,2},{2,0},{1,3},{3,1},{4,6},{6,4},{5,7},{7,5},{8,10},{10,8},{9,1... | collective-permute-start | bytes 393224 | tf_op jit(solution)/shard_map/ppermute | solution.py:203
  160.1 2.2 %copy-start.1 = (bf16[8192,256]{1,0:T(8,128)(2,1)S(1)}, bf16[8192,256]{1,0:T(8,128)(2,1)}, u32[]{:S(2)}) copy-start(bf16[8192,256]{1,0:T(8,128)(2,1)} %all-gather.3.cloned.1.call-done) | copy-start | bytes 12582916
  163.6 10.7 %copy-start.2 = (f32[512,256]{1,0:T(8,128)S(1)}, f32[512,256]{1,0:T(8,128)}, u32[]{:S(2)}) copy-start(f32[512,256]{1,0:T(8,128)} %param.4) | copy-start | bytes 1572868
Sparse Core Ops, SparseCore 0:
  9.4 77.8 all-gather.2

commit v15 on v14

--- a/solution.py
+++ b/solution.py
@@ -200,12 +200,15 @@
     yours = dot_part(1, z_rows, other, dot_part(0, z_rows, own))
     yours = sum_x(yours).astype(jnp.bfloat16)
     mine = dot_right(0, z_rows, own, other)
-    yours = lax.ppermute(yours, "zh", SWAP).astype(jnp.float32)
+    yours = lax.ppermute(yours, "zh", SWAP)
     mine = lax.cond(
         at("c") < 2, sum_x, lambda part: jnp.zeros((512, 128), jnp.float32), mine
     )
-    part = jnp.concatenate([jnp.where(low, mine, yours), jnp.where(low, yours, mine)], axis=1)
-    return 1.5 * lax.reduce_precision(z_iter, 8, 7) + part
+    z_part = 1.5 * lax.reduce_precision(z_iter, 8, 7)
+    mine += jnp.where(low, z_part[:, :128], z_part[:, 128:])
+    yours, mine = lax.optimization_barrier((yours, mine))
+    yours = yours.astype(jnp.float32) + jnp.where(low, z_part[:, 128:], z_part[:, :128])
+    return jnp.concatenate([jnp.where(low, mine, yours), jnp.where(low, yours, mine)], axis=1)
 
 
 def solution(mesh):

time: 183 us -> 203 us (1.11)
  waiting for transfers between devices: 14.5 us -> 35.7 us
  blocking collectives: 91 us -> 81.8 us
  starting transfers between devices: 41.6 us -> 45.9 us
  local copies, waits for them, and re-layouts: 6.96 us -> 9.94 us
    ppermute x1, waiting for transfers between devices: 0.01 us -> 15.3 us  [shards(): yours = lax.ppermute(yours, 'zh', SWAP)]
    all_to_all x2 -> x1, blocking collectives: 22.2 us -> 12.8 us  [sum_x(): part = lax.all_to_all(part, 'x', 0, 0, tiled=True)]
    all_to_all x0 -> x1, waiting for transfers between devices: none -> 8.08 us  [sum_x(): part = lax.all_to_all(part, 'x', 0, 0, tiled=True)]
    all_to_all x0 -> x1, starting transfers between devices: none -> 3.47 us  [sum_x(): part = lax.all_to_all(part, 'x', 0, 0, tiled=True)]
    unnamed x6 -> x8, local copies, waits for them, and re-layouts: 2.19 us -> 5.15 us
    mul x0 -> x1, other arithmetic: none -> 2.14 us  [shards(): z_part = 1.5 * lax.reduce_precision(z_iter, 8, 7)]
  transfers between devices with their start and end apart: 6 -> 7, of which waited for: 4 -> 5; matrix products, arithmetic and copies ran while one was open for 5% -> 4% of each run, Pallas kernels for 1% -> 0%
where the time goes in v15:
time: 203 us; the launch traced here: 202 us
  blocking collectives  81.8 us (40%)
  starting transfers between devices  45.9 us (23%)
  waiting for transfers between devices  35.7 us (18%)
  between operations  13.7 us (7%)
  local copies, waits for them, and re-layouts  9.94 us (5%)
  Pallas kernels  8.55 us (4%)
  other arithmetic  6.9 us (3%)
    all_to_all x1, blocking collectives, shards(): y_own = lax.all_to_all(jnp.stack([turned] * 4), 'y', 0, 0, tiled=True)  35.8 us
    ppermute x2, starting transfers between devices, other_core(): return lax.ppermute(block, 'c', SWAP)  18.4 us
    all_to_all x1, blocking collectives, shards(): part = lax.all_to_all(part.reshape(16, 256, 128), PLANE, 0, 0, tiled=True)  18.2 us
    ppermute x1, starting transfers between devices, shards(): yours = lax.ppermute(jnp.where(low, right, left), 'zh', SWAP)  16.3 us
    ppermute x1, waiting for transfers between devices, shards(): yours = lax.ppermute(yours, 'zh', SWAP)  15.3 us
    all_to_all x1, blocking collectives, shards(): lax.all_to_all(spread, PLANE, 0, 0, tiled=True).reshape(4, 4, 256, 128)  15.1 us
    all_to_all x1, blocking collectives, sum_x(): part = lax.all_to_all(part, 'x', 0, 0, tiled=True)  12.8 us
    all_to_all x1, waiting for transfers between devices, sum_x(): part = lax.all_to_all(part, 'x', 0, 0, tiled=True)  8.08 us
  transfers between devices with their start and end apart: 7, of which 5 were waited for; matrix products, arithmetic and copies ran while one was open for 4% of the time, Pallas kernels for 0%

profile of v15, /device:TPU:1, one launch (start us, length us, event | category | flops | bytes accessed | tf_op | source)
XLA Modules:
  0.0 202.5 jit_solution(4322036877174924521)
XLA Ops:
  6.5 0.0 all-gather.3.cloned.1.call-start
  6.5 2.1 %reduce-precision_multiply_fusion = (f32[512,256]{1,0:T(8,128)}, bf16[512,256]{1,0:T(8,128)(2,1)}) fusion(f32[512,256]{1,0:T(8,128)} %param.4), kind=kLoop, calls=%fused_computation.6 | loop fusion | flops 393216 | bytes 1310720 | tf_op jit(solution)/shard_map/mul | solution.py:207
  8.7 0.0 all-gather.3.cloned.1.call-update
  8.7 1.1 convert_element_type.30
  9.8 16.3 %collective-permute-start = (bf16[512,128]{1,0:T(8,128)(2,1)S(1)}, bf16[512,128]{1,0:T(8,128)(2,1)S(1)}, u32[]{:S(2)}, u32[]{:S(2)}) collective-permute-start(bf16[512,128]{1,0:T(8,128)(2,1)S(1)} %broadcast_select_fusion.4), channel_id=1, source_target_pairs={{0,2},{2,0},{1,3},{3,1},{4,6},{6,4},{5,7},{7,5},{8,10},{10,8},{9,1... | collective-permute-start | bytes 393224 | tf_op jit(solution)/shard_map/ppermute | solution.py:177
  26.1 2.6 %collective-permute-done = bf16[512,128]{1,0:T(8,128)(2,1)S(1)} collective-permute-done((bf16[512,128]{1,0:T(8,128)(2,1)S(1)}, bf16[512,128]{1,0:T(8,128)(2,1)S(1)}, u32[]{:S(2)}, u32[]{:S(2)}) %collective-permute-start) | collective-permute-done | bytes 131104 | tf_op jit(solution)/shard_map/ppermute | solution.py:177
  28.8 0.7 collective-permute-start.1
  29.5 0.0 collective-permute-done.1
  29.5 0.2 stack.28
  29.7 35.8 %all_to_all.25 = bf16[4,4,256,128]{3,2,1,0:T(8,128)(2,1)S(1)} all-to-all(bf16[4,4,256,128]{3,2,1,0:T(8,128)(2,1)S(1)} %stack.28), channel_id=1, replica_groups=mesh['x'=4,'zl'=8,'y'=4,'zh'=2,'c'=2] {'y'}, dimensions={0} | all-to-all | bytes 2097152 | tf_op jit(solution)/shard_map/all_to_all | solution.py:183
  65.5 4.4 %collective-permute-start.2 = (bf16[4,4,256,128]{3,2,1,0:T(8,128)(2,1)S(1)}, bf16[4,4,256,128]{3,2,1,0:T(8,128)(2,1)S(1)}, u32[]{:S(2)}, u32[]{:S(2)}) collective-permute-start(bf16[4,4,256,128]{3,2,1,0:T(8,128)(2,1)S(1)} %all_to_all.25), channel_id=1, source_target_pairs={{0,1},{1,0},{2,3},{3,2},{4,5},{5,4},{6,7},{7,6},{8,9},{9,8},{10,11... | collective-permute-start | bytes 3145736 | tf_op jit(solution)/shard_map/ppermute | solution.py:143
  69.9 0.1 fusion
  70.0 2.1 %collective-permute-done.2 = bf16[4,4,256,128]{3,2,1,0:T(8,128)(2,1)S(1)} collective-permute-done((bf16[4,4,256,128]{3,2,1,0:T(8,128)(2,1)S(1)}, bf16[4,4,256,128]{3,2,1,0:T(8,128)(2,1)S(1)}, u32[]{:S(2)}, u32[]{:S(2)}) %collective-permute-start.2) | collective-permute-done | bytes 1048608 | tf_op jit(solution)/shard_map/ppermute | solution.py:143
  72.1 0.1 broadcast_select_fusion.1
  72.3 0.8 copy.3
  73.1 0.8 copy.4
  73.9 2.8 %maximum_bitcast_fusion = bf16[2,2,2,256,4,128]{5,4,3,2,1,0:T(4,128)(2,1)} fusion(bf16[1,4,2,2,256,128]{5,1,4,3,0,2:T(4,128)(2,1)S(1)} %copy.4, bf16[1,4,2,2,256,128]{5,1,4,3,0,2:T(4,128)(2,1)S(1)} %copy.3), kind=kLoop, calls=%fused_computation.1 | loop fusion | flops 1048576 | bytes 4194304 | tf_op jit(solution)/shard_map/transpose | solution.py:68
  76.7 2.8 %reshape.32.right_ref = bf16[8,256,512]{2,1,0:T(8,128)(2,1)S(1)} reshape(bf16[2,2,2,256,4,128]{5,4,3,2,1,0:T(4,128)(2,1)} %maximum_bitcast_fusion) | data formatting | bytes 4194304 | tf_op jit(solution)/shard_map/reshape | solution.py:69
  79.5 7.5 %all-gather.3.cloned.1.call-done = bf16[8192,256]{1,0:T(8,128)(2,1)} async-done(((bf16[512,256]{1,0:T(8,128)(2,1)}), bf16[8192,256]{1,0:T(8,128)(2,1)}) %all-gather.3.cloned.1.call-update) | async-done | bytes 4194320 | tf_op jit(solution)/shard_map/all_gather | solution.py:170
  87.1 4.3 %shard_map.28 = bf16[4,4,256,128]{3,2,1,0:T(8,128)(2,1)S(1)} custom-call(bf16[16,512,256]{2,1,0:T(8,128)(2,1)} %bitcast.17, bf16[8,256,512]{2,1,0:T(8,128)(2,1)S(1)} %reshape.32.right_ref), custom_call_target="tpu_custom_call" | custom-call | flops 2147483648 | bytes 7340032 | tf_op jit(solution)/shard_map/pallas_call | solution.py:70
  91.4 18.2 %all_to_all.26 = bf16[16,256,128]{2,1,0:T(8,128)(2,1)S(1)} all-to-all(bf16[16,256,128]{2,1,0:T(8,128)(2,1)S(1)} %bitcast.24), channel_id=1, replica_groups=mesh['x'=4,'zl'=8,'y'=4,'zh'=2,'c'=2] {'x','y'}, dimensions={0} | all-to-all | bytes 2097152 | tf_op jit(solution)/shard_map/all_to_all | solution.py:188
  109.6 0.2 convert_reduce_fusion.1
  109.8 0.1 subtract_convert_fusion
  109.9 0.2 broadcast_in_dim.16
  110.1 15.1 %all_to_all.27 = bf16[16,256,128]{2,1,0:T(8,128)(2,1)S(1)} all-to-all(bf16[16,256,128]{2,1,0:T(8,128)(2,1)S(1)} %bitcast.27), channel_id=1, replica_groups=mesh['x'=4,'zl'=8,'y'=4,'zh'=2,'c'=2] {'x','y'}, dimensions={0} | all-to-all | bytes 2097152 | tf_op jit(solution)/shard_map/all_to_all | solution.py:193
  125.1 14.0 %collective-permute-start.3 = (bf16[4,4,256,128]{3,2,1,0:T(8,128)(2,1)S(1)}, bf16[4,4,256,128]{3,2,1,0:T(8,128)(2,1)S(1)}, u32[]{:S(2)}, u32[]{:S(2)}) collective-permute-start(bf16[4,4,256,128]{3,2,1,0:T(8,128)(2,1)S(1)} %bitcast.21), channel_id=1, source_target_pairs={{0,1},{1,0},{2,3},{3,2},{4,5},{5,4},{6,7},{7,6},{8,9},{9,8},{10,11... | collective-permute-start | bytes 3145736 | tf_op jit(solution)/shard_map/ppermute | solution.py:143
  139.1 0.0 copy-start
  139.1 2.2 %copy-done = bf16[8192,256]{1,0:T(8,128)(2,1)S(1)} copy-done((bf16[8192,256]{1,0:T(8,128)(2,1)S(1)}, bf16[8192,256]{1,0:T(8,128)(2,1)}, u32[]{:S(2)}) %copy-start) | copy-done | bytes 4194328
  141.3 0.7 shard_map.29.refs_0_
  142.0 0.0 collective-permute-done.3.part_ref.other_ref
  142.0 2.1 %shard_map.31 = bf16[4,2,256,128]{3,2,1,0:T(8,128)(2,1)} custom-call(bf16[16,512,256]{2,1,0:T(8,128)(2,1)S(1)} %bitcast.19, bf16[4,4,256,128]{3,2,1,0:T(8,128)(2,1)S(1)} %bitcast.23, bf16[4,4,256,128]{3,2,1,0:T(8,128)(2,1)S(1)} %collective-permute-done.3.part_ref.other_ref), custom_call_target="tpu_custom_call" | custom-call | flops 1073741824 | bytes 4718592 | tf_op jit(solution)/shard_map/pallas_call | solution.py:90
  144.1 12.9 %conditional.1 = (f32[512,128]{1,0:T(8,128)S(1)}) conditional(s32[]{:T(128)} %convert_element_type.35, () %tuple.14, bf16[4,2,256,128]{3,2,1,0:T(8,128)(2,1)} %shard_map.31), branch_computations={%region_2.3_spmd, %region_3.5_spmd} | conditional | flops 458752 | bytes 1835016 | solution.py:204
  144.1 12.8 %all_to_all.24 = bf16[4,2,256,128]{3,2,1,0:T(8,128)(2,1)S(1)} all-to-all(bf16[4,2,256,128]{3,2,1,0:T(8,128)(2,1)} %param.1), channel_id=1, replica_groups=mesh['x'=4,'zl'=8,'y'=4,'zh'=2,'c'=2] {'x'}, dimensions={0} | all-to-all | bytes 1048576 | tf_op jit(solution)/shard_map/cond/branch_1_fun/all_to_all | solution.py:197
  156.9 0.1 convert_reduce_fusion
  156.9 0.0 copy-start.1
  156.9 2.2 %copy-done.1 = bf16[8192,256]{1,0:T(8,128)(2,1)S(1)} copy-done((bf16[8192,256]{1,0:T(8,128)(2,1)S(1)}, bf16[8192,256]{1,0:T(8,128)(2,1)}, u32[]{:S(2)}) %copy-start.1) | copy-done | bytes 4194328
  159.1 0.0 copy-start.2
  159.1 1.5 shard_map.30
  160.6 3.5 %all-to-all-start.4 = ((bf16[4,2,256,128]{3,2,1,0:T(8,128)(2,1)}), bf16[4,2,256,128]{3,2,1,0:T(8,128)(2,1)S(1)}, u32[]{:S(2)}, u32[]{:S(2)}) async-start(bf16[4,2,256,128]{3,2,1,0:T(8,128)(2,1)} %shard_map.30), calls=%async_computation.4 | async-start | bytes 1048576 | tf_op jit(solution)/shard_map/all_to_all | solution.py:197
  164.1 8.1 %all-to-all-done.4 = bf16[4,2,256,128]{3,2,1,0:T(8,128)(2,1)S(1)} async-done(((bf16[4,2,256,128]{3,2,1,0:T(8,128)(2,1)}), bf16[4,2,256,128]{3,2,1,0:T(8,128)(2,1)S(1)}, u32[]{:S(2)}, u32[]{:S(2)}) %all-to-all-start.4) | async-done | bytes 524320 | tf_op jit(solution)/shard_map/all_to_all | solution.py:197
  172.2 0.1 reduce_sum.31
  172.3 7.1 %collective-permute-start.4 = (bf16[512,128]{1,0:T(8,128)(2,1)S(1)}, bf16[512,128]{1,0:T(8,128)(2,1)S(1)}, u32[]{:S(2)}, u32[]{:S(2)}) collective-permute-start(bf16[512,128]{1,0:T(8,128)(2,1)S(1)} %bitcast.31), channel_id=1, source_target_pairs={{0,2},{2,0},{1,3},{3,1},{4,6},{6,4},{5,7},{7,5},{8,10},{10,8},{9,1... | collective-permute-start | bytes 393224 | tf_op jit(solution)/shard_map/ppermute | solution.py:203
  179.4 0.0 copy-done.2
  179.5 15.3 %collective-permute-done.4 = bf16[512,128]{1,0:T(8,128)(2,1)S(1)} collective-permute-done((bf16[512,128]{1,0:T(8,128)(2,1)S(1)}, bf16[512,128]{1,0:T(8,128)(2,1)S(1)}, u32[]{:S(2)}, u32[]{:S(2)}) %collective-permute-start.4) | collective-permute-done | bytes 131104 | tf_op jit(solution)/shard_map/ppermute | solution.py:203
  194.8 0.1 broadcast_select_fusion.3
  194.8 0.0 copy-start.3
  194.9 0.8 copy-done.3
  (7 shorter events, 0.1 us)
Async XLA Ops:
  6.5 80.5 %all-gather.3.cloned.1.call-start = ((), (), s32[]{:S(2)}) async-start(), calls=%async_computation.5 | async-start | bytes 4456448 | tf_op jit(solution)/shard_map/all_gather | solution.py:170
  9.8 18.9 %collective-permute-start = (bf16[512,128]{1,0:T(8,128)(2,1)S(1)}, bf16[512,128]{1,0:T(8,128)(2,1)S(1)}, u32[]{:S(2)}, u32[]{:S(2)}) collective-permute-start(bf16[512,128]{1,0:T(8,128)(2,1)S(1)} %broadcast_select_fusion.4), channel_id=1, source_target_pairs={{0,2},{2,0},{1,3},{3,1},{4,6},{6,4},{5,7},{7,5},{8,10},{10,8},{9,1... | collective-permute-start | bytes 393224 | tf_op jit(solution)/shard_map/ppermute | solution.py:177
  28.8 0.7 collective-permute-start.1
  65.5 6.7 %collective-permute-start.2 = (bf16[4,4,256,128]{3,2,1,0:T(8,128)(2,1)S(1)}, bf16[4,4,256,128]{3,2,1,0:T(8,128)(2,1)S(1)}, u32[]{:S(2)}, u32[]{:S(2)}) collective-permute-start(bf16[4,4,256,128]{3,2,1,0:T(8,128)(2,1)S(1)} %all_to_all.25), channel_id=1, source_target_pairs={{0,1},{1,0},{2,3},{3,2},{4,5},{5,4},{6,7},{7,6},{8,9},{9,8},{10,11... | collective-permute-start | bytes 3145736 | tf_op jit(solution)/shard_map/ppermute | solution.py:143
  125.1 16.9 %collective-permute-start.3 = (bf16[4,4,256,128]{3,2,1,0:T(8,128)(2,1)S(1)}, bf16[4,4,256,128]{3,2,1,0:T(8,128)(2,1)S(1)}, u32[]{:S(2)}, u32[]{:S(2)}) collective-permute-start(bf16[4,4,256,128]{3,2,1,0:T(8,128)(2,1)S(1)} %bitcast.21), channel_id=1, source_target_pairs={{0,1},{1,0},{2,3},{3,2},{4,5},{5,4},{6,7},{7,6},{8,9},{9,8},{10,11... | collective-permute-start | bytes 3145736 | tf_op jit(solution)/shard_map/ppermute | solution.py:143
  139.1 2.2 %copy-start = (bf16[8192,256]{1,0:T(8,128)(2,1)S(1)}, bf16[8192,256]{1,0:T(8,128)(2,1)}, u32[]{:S(2)}) copy-start(bf16[8192,256]{1,0:T(8,128)(2,1)} %all-gather.3.cloned.1.call-done) | copy-start | bytes 12582916
  156.9 2.2 %copy-start.1 = (bf16[8192,256]{1,0:T(8,128)(2,1)S(1)}, bf16[8192,256]{1,0:T(8,128)(2,1)}, u32[]{:S(2)}) copy-start(bf16[8192,256]{1,0:T(8,128)(2,1)} %all-gather.3.cloned.1.call-done) | copy-start | bytes 12582916
  159.1 20.3 %copy-start.2 = (f32[512,256]{1,0:T(8,128)S(1)}, f32[512,256]{1,0:T(8,128)}, u32[]{:S(2)}) copy-start(f32[512,256]{1,0:T(8,128)} %get-tuple-element.21) | copy-start | bytes 1572868
  160.6 11.6 %all-to-all-start.4 = ((bf16[4,2,256,128]{3,2,1,0:T(8,128)(2,1)}), bf16[4,2,256,128]{3,2,1,0:T(8,128)(2,1)S(1)}, u32[]{:S(2)}, u32[]{:S(2)}) async-start(bf16[4,2,256,128]{3,2,1,0:T(8,128)(2,1)} %shard_map.30), calls=%async_computation.4 | async-start | bytes 1048576 | tf_op jit(solution)/shard_map/all_to_all | solution.py:197
  172.3 22.5 %collective-permute-start.4 = (bf16[512,128]{1,0:T(8,128)(2,1)S(1)}, bf16[512,128]{1,0:T(8,128)(2,1)S(1)}, u32[]{:S(2)}, u32[]{:S(2)}) collective-permute-start(bf16[512,128]{1,0:T(8,128)(2,1)S(1)} %bitcast.31), channel_id=1, source_target_pairs={{0,2},{2,0},{1,3},{3,1},{4,6},{6,4},{5,7},{7,5},{8,10},{10,8},{9,1... | collective-permute-start | bytes 393224 | tf_op jit(solution)/shard_map/ppermute | solution.py:203
  194.8 0.8 copy-start.3
Sparse Core Ops, SparseCore 0:
  9.4 77.5 all-gather.2
